TPU v7x, 512 devices: a whole 4x8x8 slice. The times are simulated.
512 devices in a mesh: win: 32 (over y_lo, z), head: 16 (over x, y_hi, core).
Axes of the slice: x: 4, y: 8 (y_hi: 2, y_lo: 4; y = y_hi * 4 + y_lo), z: 8, core: 2. Of those that a mesh axis runs over, the one named last changes fastest.
Arguments:
- latents: bfloat16 [32, 8, 128, 3072], P('win', None, 'head'), may hold values from -6 to 6
- prompt_ids: int32 [32], P('win'), may hold values from 0 to 7
- modulation: float32 [8, 3, 3072], replicated, may hold values from -2.5 to 5
- w_qkv: bfloat16 [3, 3072, 3072], P(None, 'head'), may hold values from -0.5 to 0.5
- intersection: int32 [32], replicated, may hold values from 0 to 3, as said below
Outputs:
- blended: bfloat16 [32, 8, 128, 3072], P('win', None, 'head')
Inputs may be any that keep to these rules, and one draw needn't show every extreme that they name: intersection[0] is 0; every other entry lies in 1 to 3, and some entry equals 3.
All inputs are finite; a program needn't handle non-finite values.
Results may differ from a plain program's by a relative error of at most 0.024.
The roundings to bfloat16 on the way count: a program that leaves them out, or rounds other values in their place, can miss the bound.
Values may be sent and summed in bfloat16 or wider, within the bound.
No kernel may reach another device: no remote copies, remote signals or barrier semaphores. Data moves between devices by JAX's collectives and lax.ppermute only.
A program may use at most 64 MiB of HBM per device.

v0:
```python
import jax
import jax.numpy as jnp
from jax import lax
from jax.sharding import PartitionSpec as P

HEAD_DIM = 64
OMAX = 3
PROMPTS = 8


def shifted(value, axis, by):
    count = lax.axis_size(axis)
    pairs = [(i, i + by) for i in range(count) if 0 <= i + by < count]
    return lax.ppermute(value, axis, pairs)


def selectors(ov_prev, ov_next, frames, most):
    fidx = jnp.arange(frames, dtype=jnp.int32)[:, None]
    jidx = jnp.arange(most, dtype=jnp.int32)[None, :]
    sel_prev = ((fidx < ov_prev) & (jidx == most - ov_prev + fidx)).astype(jnp.float32)
    sel_next = ((fidx >= frames - ov_next) & (jidx == fidx - frames + ov_next)).astype(jnp.float32)
    count = 1.0 + jnp.sum(sel_prev, axis=1) + jnp.sum(sel_next, axis=1)
    return (sel_prev, sel_next, count)


def shards(latents, prompt_ids, modulation, w_qkv, intersection):
    frames = latents.shape[1]
    patches = latents.shape[2]
    width = latents.shape[3]
    local_width = w_qkv.shape[1]
    local_heads = local_width // HEAD_DIM
    onehot = (jnp.arange(PROMPTS, dtype=jnp.int32) == prompt_ids[0]).astype(jnp.float32)
    mods = jnp.einsum("p,pcd->cd", onehot, modulation, precision=lax.Precision.HIGHEST)
    xf = latents.astype(jnp.float32)
    mean = jnp.mean(xf, axis=-1, keepdims=True)
    var = jnp.mean((xf - mean) ** 2, axis=-1, keepdims=True)
    normed = ((xf - mean) / jnp.sqrt(var + 1e-06) * (1.0 + mods[1]) + mods[0]).astype(jnp.bfloat16)
    flat_weight = w_qkv.reshape(3 * local_width, width)
    rows = lax.all_gather(normed, "head", axis=0, tiled=True).reshape(-1, width)
    out = lax.dot_general(
        rows, flat_weight, (((1,), (1,)), ((), ())), preferred_element_type=jnp.float32
    )
    qkv = out.astype(jnp.bfloat16).reshape(-1, 3, local_width)
    length = qkv.shape[0]
    queries = qkv[:, 0].reshape(length, local_heads, HEAD_DIM)
    keys = qkv[:, 1].reshape(length, local_heads, HEAD_DIM)
    values = qkv[:, 2].reshape(length, local_heads, HEAD_DIM)
    factor = HEAD_DIM ** (-0.5)
    block = min(512, length)

    def attend(qblock):
        scores = (
            jnp.einsum("bhe,khe->hbk", qblock, keys, preferred_element_type=jnp.float32) * factor
        )
        scores = scores - jnp.max(scores, axis=-1, keepdims=True)
        expo = jnp.exp(scores)
        probs = (expo / jnp.sum(expo, axis=-1, keepdims=True)).astype(jnp.bfloat16)
        return jnp.einsum("hbk,khe->bhe", probs, values, preferred_element_type=jnp.float32).astype(
            jnp.bfloat16
        )

    attended = lax.map(attend, queries.reshape(length // block, block, local_heads, HEAD_DIM))
    attended = attended.reshape(length, local_width)
    window = lax.axis_index("win")
    ov_prev = lax.dynamic_index_in_dim(intersection, window, keepdims=False)
    padded = jnp.concatenate([intersection, jnp.zeros((1,), jnp.int32)])
    ov_next = lax.dynamic_index_in_dim(padded, window + 1, keepdims=False)
    sel_prev, sel_next, count = selectors(ov_prev, ov_next, frames, OMAX)
    mine = lax.all_to_all(attended, "head", split_axis=0, concat_axis=1, tiled=True).reshape(
        frames, patches, width
    )
    from_prev = shifted(mine[frames - OMAX :], "win", 1)
    from_next = shifted(mine[:OMAX], "win", -1)
    total = mine.astype(jnp.float32)
    total = total + jnp.einsum(
        "fj,jpe->fpe", sel_prev, from_prev.astype(jnp.float32), precision=lax.Precision.HIGHEST
    )
    total = total + jnp.einsum(
        "fj,jpe->fpe", sel_next, from_next.astype(jnp.float32), precision=lax.Precision.HIGHEST
    )
    averaged = (total / count[:, None, None]).astype(jnp.bfloat16)
    result = xf[0] + mods[2] * averaged.astype(jnp.float32)
    return result.astype(jnp.bfloat16)[None]


def solution(mesh):
    in_specs = (P("win", None, "head", None), P("win"), P(), P(None, "head", None), P())
    out_specs = P("win", None, "head", None)
    return jax.shard_map(shards, mesh=mesh, in_specs=in_specs, out_specs=out_specs, check_vma=False)
```

profile of v0, /device:TPU:24, one launch (start us, length us, event | category | flops | bytes accessed | tf_op | source)
XLA Modules:
  0.0 212.1 jit_solution(16126676532323454981)
XLA Ops:
  6.5 0.0 copy-start
  6.5 0.0 all-gather.2.cloned.1.call-start
  7.3 1.4 fusion.46
  8.8 1.4 convert_reduce_fusion
  10.2 1.5 fusion.37
  11.7 1.3 fusion.40
  12.9 1.0 copy.20
  13.9 0.0 all-gather.2.cloned.1.call-update
  14.0 1.2 dynamic_slice.12
  15.2 0.7 pad_add_fusion
  15.9 0.7 dynamic_slice.13
  17.8 91.1 %all-gather.2.cloned.1.call-done = bf16[16,8,8,3072]{3,2,1,0:T(8,128)(2,1)} async-done(((bf16[1,8,8,3072]{3,2,1,0:T(8,128)(2,1)}), bf16[16,8,8,3072]{3,2,1,0:T(8,128)(2,1)}) %all-gather.2.cloned.1.call-update) | async-done | bytes 6291472 | tf_op jit(solution)/shard_map/all_gather | solution.py:39
  108.9 6.6 %convolution_convert_fusion = bf16[1024,576]{0,1:T(8,128)(2,1)S(1)} fusion(bf16[1024,3072]{1,0:T(8,128)(2,1)} %bitcast.77, bf16[576,3072]{1,0:T(8,128)(2,1)S(1)} %bitcast.69), kind=kOutput, calls=%fused_computation.28 | convolution fusion | flops 3624468480 | bytes 11010048 | tf_op jit(solution)/shard_map/dot_general | solution.py:40
  115.5 1.0 fusion.62
  116.6 2.0 reshape_reshape_squeeze.3
  118.6 1.8 copy.21
  120.4 21.8 %while.10 = (s32[]{:T(128)}, bf16[2,512,3,64]{1,3,2,0:T(8,128)(2,1)}, bf16[2,512,3,64]{1,3,2,0:T(8,128)(2,1)}, bf16[1024,3,64]{0,2,1:T(8,128)(2,1)}, bf16[1024,3,64]{0,2,1:T(8,128)(2,1)}, /*index=5*/s32[]{:T(128)}) while((s32[]{:T(128)}, bf16[2,512,3,64]{1,3,2,0:T(8,128)(2,1)}, bf16[2,512,3,64]{1,3,2,0:T(8,128)(2,1)}, ...), condition=%wide.region_5.6_spmd, body=%wide.region_2.5_spmd.sunk | while | flops 410616832 | bytes 13776981 | solution.py:62
  120.4 6.2 %fusion.81 = (f32[3,512]{1,0:T(4,128)}, f32[3,512,1024]{2,1,0:T(8,128)}) fusion(bf16[1024,3,64]{0,2,1:T(8,128)(2,1)} %get-tuple-element.115, bf16[2,512,3,64]{1,3,2,0:T(8,128)(2,1)} %get-tuple-element.114, s32[]{:T(128)S(6)} %copy.44), kind=kOutput, calls=%fused_computation.67.clone.1 | convolution fusion | flops 206046208 | bytes 6887428 | tf_op jit(solution)/shard_map/while/body/eval_jaxpr/sub | solution.py:55
  126.6 4.6 %fusion.82 = bf16[2,512,3,64]{1,3,2,0:T(8,128)(2,1)} fusion(bf16[2,512,3,64]{1,3,2,0:T(8,128)(2,1)} %get-tuple-element.107, s32[]{:T(128)S(6)} %copy.44, bf16[1024,3,64]{0,2,1:T(8,128)(2,1)} %get-tuple-element.116, f32[3,512,1024]{2,1,0:T(8,128)} %get-tuple-element.98, f32[3,512]{1,0:T(4,128)} %get-tuple-element.99), kind=kOutput, calls=%fused_computation.9.clone.1 | convolution fusion | flops 204570624 | bytes 6889476 | tf_op jit(solution)/shard_map/while/body/eval_jaxpr/hbk,khe->bhe/dot_general | solution.py:58
  131.3 6.2 %fusion.81 = (f32[3,512]{1,0:T(4,128)}, f32[3,512,1024]{2,1,0:T(8,128)}) fusion(bf16[1024,3,64]{0,2,1:T(8,128)(2,1)} %get-tuple-element.115, bf16[2,512,3,64]{1,3,2,0:T(8,128)(2,1)} %get-tuple-element.114, s32[]{:T(128)S(6)} %copy.44), kind=kOutput, calls=%fused_computation.67.clone.1 | convolution fusion | flops 206046208 | bytes 6887428 | tf_op jit(solution)/shard_map/while/body/eval_jaxpr/sub | solution.py:55
  137.5 4.6 %fusion.82 = bf16[2,512,3,64]{1,3,2,0:T(8,128)(2,1)} fusion(bf16[2,512,3,64]{1,3,2,0:T(8,128)(2,1)} %get-tuple-element.107, s32[]{:T(128)S(6)} %copy.44, bf16[1024,3,64]{0,2,1:T(8,128)(2,1)} %get-tuple-element.116, f32[3,512,1024]{2,1,0:T(8,128)} %get-tuple-element.98, f32[3,512]{1,0:T(4,128)} %get-tuple-element.99), kind=kOutput, calls=%fused_computation.9.clone.1 | convolution fusion | flops 204570624 | bytes 6889476 | tf_op jit(solution)/shard_map/while/body/eval_jaxpr/hbk,khe->bhe/dot_general | solution.py:58
  142.2 2.3 %copy.32 = bf16[2,512,3,64]{3,2,1,0:T(4,128)(2,1)} copy(bf16[2,512,3,64]{1,3,2,0:T(8,128)(2,1)} %get-tuple-element.32) | data formatting | bytes 786432 | tf_op jit(solution)/shard_map/all_to_all | solution.py:69
  144.5 3.2 %reshape.93 = bf16[16,64,192]{2,1,0:T(8,128)(2,1)} reshape(bf16[2,512,3,64]{3,2,1,0:T(4,128)(2,1)} %copy.32) | data formatting | bytes 786432 | tf_op jit(solution)/shard_map/all_to_all | solution.py:69
  147.7 4.2 %all-to-all-start = ((bf16[16,64,192]{2,1,0:T(8,128)(2,1)}), bf16[16,64,192]{2,1,0:T(8,128)(2,1)}, u32[]{:S(2)}, u32[]{:S(2)}) async-start(bf16[16,64,192]{2,1,0:T(8,128)(2,1)} %reshape.93), calls=%async_computation | async-start | bytes 1048576 | tf_op jit(solution)/shard_map/all_to_all | solution.py:69
  151.9 0.7 add_add_fusion.1
  152.6 0.6 iota_compare_fusion.3
  153.2 0.5 copy-done.1
  153.7 0.0 copy-done.2
  153.7 0.5 copy-done.3
  154.3 0.5 add_add_fusion
  154.8 12.0 %all-to-all-done = bf16[16,64,192]{2,1,0:T(8,128)(2,1)} async-done(((bf16[16,64,192]{2,1,0:T(8,128)(2,1)}), bf16[16,64,192]{2,1,0:T(8,128)(2,1)}, u32[]{:S(2)}, u32[]{:S(2)}) %all-to-all-start) | async-done | bytes 393248 | tf_op jit(solution)/shard_map/all_to_all | solution.py:69
  166.8 1.7 fusion.63
  168.5 0.7 copy.28
  169.2 1.8 slice.39
  171.0 1.7 copy.29
  172.7 13.2 %collective-permute-start.1 = (bf16[3,8,3072]{2,0,1:T(4,128)(2,1)}, bf16[3,8,3072]{2,0,1:T(4,128)(2,1)}, u32[]{:S(2)}, u32[]{:S(2)}) collective-permute-start(bf16[3,8,3072]{2,0,1:T(4,128)(2,1)} %copy.29), channel_id=1, source_target_pairs={{16,0},{32,16},{48,32},{64,48},{80,64},{96,80},{112,96},{128,112},... | collective-permute-start | bytes 442376 | tf_op jit(solution)/shard_map/ppermute | solution.py:14
  185.9 1.6 copy.25
  187.5 1.8 slice.37
  189.3 1.7 copy.26
  191.1 2.1 collective-permute-start
  193.2 1.1 bitcast_convert_fusion
  194.3 1.6 copy.24
  195.9 2.5 %reshape.88 = f32[8,8,3072]{2,1,0:T(8,128)} reshape(f32[64,16,192]{2,1,0:T(8,128)} %copy.24) | data formatting | bytes 1572864 | tf_op jit(solution)/shard_map/convert_element_type | solution.py:74
  198.5 0.0 collective-permute-done.1
  198.5 1.2 fusion.43
  199.7 2.3 %collective-permute-done = bf16[3,8,3072]{2,0,1:T(4,128)(2,1)} collective-permute-done((bf16[3,8,3072]{2,0,1:T(4,128)(2,1)}, bf16[3,8,3072]{2,0,1:T(4,128)(2,1)}, u32[]{:S(2)}, u32[]{:S(2)}) %collective-permute-start) | collective-permute-done | bytes 147488 | tf_op jit(solution)/shard_map/ppermute | solution.py:14
  202.0 2.4 %fusion.34 = bf16[1,8,8,3072]{3,1,2,0:T(8,128)(2,1)S(1)} fusion(f32[8,8,3072]{2,0,1:T(8,128)S(1)} %fusion.43, bf16[3,8,3072]{2,0,1:T(4,128)(2,1)} %collective-permute-done, f32[8,8,3072]{2,1,0:T(8,128)} %reshape.88, f32[8]{0:T(128)} %add_add_fusion, f32[3072]{0:T(1024)S(1)} %bitcast.76, bf16[1,8,8,3072]{3,2,1,0:T(8,128)(2,1)} %param.7, s32[8]{0:T(128)} %copy-done.3, ...), kind=kOutput, calls=%fused_computation.27 | convolution fusion | flops 2949168 | bytes 2519112 | tf_op jit(solution)/shard_map/fj,jpe->fpe/dot_general | solution.py:75
  204.3 1.0 copy.30
  (12 shorter events, 0.1 us)
Async XLA Ops:
  6.5 102.4 %copy-start = (bf16[3,192,3072]{2,1,0:T(8,128)(2,1)S(1)}, bf16[3,192,3072]{2,1,0:T(8,128)(2,1)}, u32[]{:S(2)}) copy-start(bf16[3,192,3072]{2,1,0:T(8,128)(2,1)} %param.10) | copy-start | bytes 10616836
  6.5 102.4 %all-gather.2.cloned.1.call-start = ((), (), s32[]{:S(2)}) async-start(), calls=%async_computation.1 | async-start | bytes 6684672 | tf_op jit(solution)/shard_map/all_gather | solution.py:39
  147.7 19.1 %all-to-all-start = ((bf16[16,64,192]{2,1,0:T(8,128)(2,1)}), bf16[16,64,192]{2,1,0:T(8,128)(2,1)}, u32[]{:S(2)}, u32[]{:S(2)}) async-start(bf16[16,64,192]{2,1,0:T(8,128)(2,1)} %reshape.93), calls=%async_computation | async-start | bytes 1048576 | tf_op jit(solution)/shard_map/all_to_all | solution.py:69
  153.2 0.6 copy-start.2
  153.2 0.5 copy-start.1
  153.7 0.6 copy-start.3
  172.7 25.7 %collective-permute-start.1 = (bf16[3,8,3072]{2,0,1:T(4,128)(2,1)}, bf16[3,8,3072]{2,0,1:T(4,128)(2,1)}, u32[]{:S(2)}, u32[]{:S(2)}) collective-permute-start(bf16[3,8,3072]{2,0,1:T(4,128)(2,1)} %copy.29), channel_id=1, source_target_pairs={{16,0},{32,16},{48,32},{64,48},{80,64},{96,80},{112,96},{128,112},... | collective-permute-start | bytes 442376 | tf_op jit(solution)/shard_map/ppermute | solution.py:14
  191.1 10.9 %collective-permute-start = (bf16[3,8,3072]{2,0,1:T(4,128)(2,1)}, bf16[3,8,3072]{2,0,1:T(4,128)(2,1)}, u32[]{:S(2)}, u32[]{:S(2)}) collective-permute-start(bf16[3,8,3072]{2,0,1:T(4,128)(2,1)} %copy.26), channel_id=1, source_target_pairs={{0,16},{16,32},{32,48},{48,64},{64,80},{80,96},{96,112},{112,128},... | collective-permute-start | bytes 442376 | tf_op jit(solution)/shard_map/ppermute | solution.py:14
Sparse Core Ops, SparseCore 0:
  14.1 94.7 all-gather.1
where the time goes:
time: 213 us; the launch traced here: 212 us
  waiting for transfers between devices  105 us (49%)
  matrix products  33.4 us (16%)
  local copies, waits for them, and re-layouts  30.5 us (14%)
  starting transfers between devices  19.5 us (9%)
  between operations  15.6 us (7%)
  other arithmetic  7.83 us (4%)
    all_gather x1, waiting for transfers between devices, shards(): rows = lax.all_gather(normed, 'head', axis=0, tiled=True).reshape(-1, width)  91.1 us
    ppermute x2, starting transfers between devices, shifted(): return lax.ppermute(value, axis, pairs)  15.3 us
    sub x2, matrix products, attend(): scores = scores - jnp.max(scores, axis=-1, keepdims=True)  12.5 us
    all_to_all x1, waiting for transfers between devices, shards(): lax.all_to_all(attended, 'head', split_axis=0, concat_axis=1, tiled=True)  12 us
    dot_general x2, matrix products, attend(): jnp.einsum('hbk,khe->bhe', probs, values, preferred_element_type=jnp.floa...  9.3 us
    slice x4, local copies, waits for them, and re-layouts, shards(): from_prev = shifted(mine[frames - OMAX:], 'win', 1)  6.88 us
    dot_general x1, matrix products, shards(): lax.dot_general(rows, flat_weight, (((1,), (1,)), ((), ())), preferred_el...  6.62 us
    all_to_all x2, local copies, waits for them, and re-layouts, shards(): lax.all_to_all(attended, 'head', split_axis=0, concat_axis=1, tiled=True)  5.48 us
  transfers between devices with their start and end apart: 4, of which 3 were waited for; matrix products, arithmetic and copies ran while one was open for 8% of the time, Pallas kernels for 0%

commit v1 on v0

v1 whole, which is shorter than its diff:
```python
import functools

import jax
import jax.numpy as jnp
from jax import lax
from jax.experimental import pallas as pl
from jax.experimental.pallas import tpu as pltpu
from jax.sharding import Mesh
from jax.sharding import PartitionSpec as P

HEAD_DIM = 64
OMAX = 3
NX, NY, NC = 4, 2, 2
MIB = 1 << 20
OFFSETS = (0, 3, 1, 2)


def project_kernel(pid, t0, t1, t2, t3, mod_ref, wa, wb, oa, ob, va, vb, sems):
    copies = [pltpu.make_async_copy(wa, va, sems.at[0]), pltpu.make_async_copy(wb, vb, sems.at[1])]
    for c in copies:
        c.start()
    shift = mod_ref[0, 0:1, :]
    scale = 1.0 + mod_ref[0, 1:2, :]
    parts = []
    for t in (t0, t1, t2, t3):
        xf = t[...].astype(jnp.float32)
        mean = jnp.mean(xf, axis=-1, keepdims=True)
        xc = xf - mean
        var = jnp.mean(xc * xc, axis=-1, keepdims=True)
        parts.append((xc * lax.rsqrt(var + 1e-06) * scale + shift).astype(jnp.bfloat16))
    normed = jnp.concatenate(parts, axis=0)
    for c, v, o in zip(copies, (va, vb), (oa, ob)):
        c.wait()
        o[...] = lax.dot_general(
            normed, v[...], (((1,), (1,)), ((), ())), preferred_element_type=jnp.float32
        ).astype(jnp.bfloat16)


def project(pid, blocks, modulation, wa, wb):
    rows, width = blocks[0].shape
    feats = wa.shape[0]
    tok = pl.BlockSpec((rows, width), lambda i, p: (0, 0))
    out = pl.BlockSpec((4 * rows, feats), lambda i, p: (0, 0))
    hbm = pl.BlockSpec(memory_space=pl.ANY)
    shape = jax.ShapeDtypeStruct((4 * rows, feats), jnp.bfloat16)
    return pl.pallas_call(
        project_kernel,
        grid_spec=pltpu.PrefetchScalarGridSpec(
            num_scalar_prefetch=1,
            grid=(1,),
            in_specs=[tok] * 4 + [pl.BlockSpec((1, 3, width), lambda i, p: (p[0], 0, 0)), hbm, hbm],
            out_specs=[out, out],
            scratch_shapes=[
                pltpu.VMEM((feats, width), jnp.bfloat16),
                pltpu.VMEM((feats, width), jnp.bfloat16),
                pltpu.SemaphoreType.DMA((2,)),
            ],
        ),
        out_shape=[shape, shape],
        compiler_params=pltpu.CompilerParams(vmem_limit_bytes=48 * MIB),
    )(pid, *blocks, modulation, wa, wb)


def attend_kernel(first, count, place, g0, g1, g2, g3, out):
    groups = (g0, g1, g2, g3)
    per = g0.shape[0]
    rows = g0.shape[1]
    width = g0.shape[2] // 3
    keys = per * rows
    lane = lax.broadcasted_iota(jnp.int32, (4 * keys, 128), 1)
    heads = width // HEAD_DIM
    kk, vv = [], []
    for h in range(heads):
        a = width + h * HEAD_DIM
        kk.append(jnp.concatenate([g[:, :, a : a + HEAD_DIM].reshape(keys, HEAD_DIM) for g in groups], axis=0))
        a = 2 * width + h * HEAD_DIM
        v = jnp.concatenate([g[:, :, a : a + HEAD_DIM].reshape(keys, HEAD_DIM) for g in groups], axis=0)
        v = jnp.concatenate([v, jnp.zeros_like(v)], axis=1)
        vv.append(jnp.where(lane == HEAD_DIM, jnp.ones_like(v), v))
    for pair in (0, 2):
        results = []
        for h in range(heads):
            a = h * HEAD_DIM
            q = jnp.concatenate(
                [
                    g[:, first : first + count, a : a + HEAD_DIM].reshape(per * count, HEAD_DIM)
                    for g in groups[pair : pair + 2]
                ],
                axis=0,
            )
            s = lax.dot_general(q, kk[h], (((1,), (1,)), ((), ())), preferred_element_type=jnp.float32)
            top = jnp.max(s, axis=-1, keepdims=True)
            p = jnp.exp((s - top) * (HEAD_DIM**-0.5)).astype(jnp.bfloat16)
            o = lax.dot_general(p, vv[h], (((1,), (0,)), ((), ())), preferred_element_type=jnp.float32)
            results.append(o[:, :HEAD_DIM] / o[:, HEAD_DIM : HEAD_DIM + 1])
        both = jnp.concatenate(results, axis=1).astype(jnp.bfloat16).reshape(2 * per, count, width)
        for j in range(2):
            group = pair + j
            for n in range(per):
                x = lax.rem(place[0] + OFFSETS[n], NX)
                y = lax.rem(place[1] + group // 2, NY)
                c = lax.rem(place[2] + group % 2, NC)
                out[(x * NY + y) * NC + c] = both[j * per + n]


def attend(first, count, place, groups):
    per, rows, feats = groups[0].shape
    full = pl.BlockSpec(memory_space=pltpu.VMEM)
    return pl.pallas_call(
        functools.partial(attend_kernel, first, count),
        in_specs=[pl.BlockSpec(memory_space=pltpu.SMEM)] + [full] * 4,
        out_specs=full,
        out_shape=jax.ShapeDtypeStruct((4 * per, count, feats // 3), jnp.bfloat16),
        compiler_params=pltpu.CompilerParams(vmem_limit_bytes=48 * MIB),
    )(place, *groups)


def average_kernel(overlap, low, high, before, after, out):
    half = low.shape[1]
    each = 8
    frames = 2 * half // each
    ov_prev, ov_next = overlap[0], overlap[1]
    prev = before[...].astype(jnp.float32)
    nxt = after[...].astype(jnp.float32)
    for ref, base in ((low, 0), (high, frames // 2)):
        mine = ref[...].astype(jnp.float32)
        done = []
        for i in range(frames // 2):
            f = base + i
            cur = mine[:, i * each : (i + 1) * each]
            if f < OMAX:
                shared = f < ov_prev
                part = jnp.zeros_like(cur)
                for j in range(OMAX):
                    at = (frames // 2 - OMAX + j) * each
                    take = shared & (j == OMAX - ov_prev + f)
                    part = jnp.where(take, prev[:, at : at + each], part)
                cur = (cur + part) * jnp.where(shared, 0.5, 1.0)
            if f >= frames - OMAX:
                shared = f >= frames - ov_next
                part = jnp.zeros_like(cur)
                for j in range(OMAX):
                    take = shared & (j == f - frames + ov_next)
                    part = jnp.where(take, nxt[:, j * each : (j + 1) * each], part)
                cur = (cur + part) * jnp.where(shared, 0.5, 1.0)
            done.append(cur)
        out[:, base * each : base * each + half, :] = jnp.concatenate(done, axis=1).astype(jnp.bfloat16)


def average(overlap, low, high, before, after):
    full = pl.BlockSpec(memory_space=pltpu.VMEM)
    blocks, half, width = low.shape
    return pl.pallas_call(
        average_kernel,
        in_specs=[pl.BlockSpec(memory_space=pltpu.SMEM)] + [full] * 4,
        out_specs=full,
        out_shape=jax.ShapeDtypeStruct((blocks, 2 * half, width), jnp.bfloat16),
        compiler_params=pltpu.CompilerParams(vmem_limit_bytes=32 * MIB),
    )(overlap, low, high, before, after)


def blend_kernel(pid, lat, mod_ref, avg, out):
    blocks, _, width = avg.shape
    for b in range(0, blocks, 2):
        cols = slice(b * width, (b + 2) * width)
        a = jnp.concatenate([avg[b].astype(jnp.float32), avg[b + 1].astype(jnp.float32)], axis=1)
        out[:, cols] = (lat[:, cols].astype(jnp.float32) + mod_ref[0, 2:3, cols] * a).astype(jnp.bfloat16)


def blend(pid, lat, modulation, avg):
    rows, width = lat.shape
    tok = pl.BlockSpec((rows, width), lambda i, p: (0, 0))
    return pl.pallas_call(
        blend_kernel,
        grid_spec=pltpu.PrefetchScalarGridSpec(
            num_scalar_prefetch=1,
            grid=(1,),
            in_specs=[
                tok,
                pl.BlockSpec((1, 3, width), lambda i, p: (p[0], 0, 0)),
                pl.BlockSpec(avg.shape, lambda i, p: (0, 0, 0)),
            ],
            out_specs=tok,
        ),
        out_shape=jax.ShapeDtypeStruct((rows, width), jnp.bfloat16),
        compiler_params=pltpu.CompilerParams(vmem_limit_bytes=32 * MIB),
    )(pid, lat, modulation, avg)


def around(value, axis, by):
    n = lax.axis_size(axis)
    return lax.ppermute(value, axis, [(i, (i + by) % n) for i in range(n)])


def along(value, by):
    n = lax.axis_size(("ylo", "z"))
    return lax.ppermute(value, ("ylo", "z"), [(i, i + by) for i in range(n) if 0 <= i + by < n])


def shards(latents, prompt_ids, modulation, w_qkv, intersection):
    _, frames, patches, width = latents.shape
    rows = frames * patches
    mine = latents.reshape(rows, width)
    wa = w_qkv.reshape(-1, width)
    place = jnp.stack([lax.axis_index("x"), lax.axis_index("yhi"), lax.axis_index("core")]).astype(jnp.int32)

    other = around(mine, "yhi", 1)
    near = [mine] + [around(mine, "x", by) for by in (1, 3, 2)]
    wb = around(wa, "core", 1)
    far = [other] + [around(other, "x", by) for by in (1, 3, 2)]

    own0, give0 = project(prompt_ids, near, modulation, wa, wb)
    got0 = around(give0, "core", 1)
    own1, give1 = project(prompt_ids, far, modulation, wa, wb)
    got1 = around(give1, "core", 1)
    groups = [g.reshape(4, rows, -1) for g in (own0, got0, own1, got1)]

    low = attend(0, rows // 2, place, groups)
    after = along(low, -1)
    high = attend(rows // 2, rows // 2, place, groups)
    before = along(high, 1)

    window = lax.axis_index(("ylo", "z"))
    padded = jnp.concatenate([intersection, jnp.zeros((1,), jnp.int32)])
    overlap = lax.dynamic_slice(padded, (window,), (2,))
    avg = average(overlap, low, high, before, after)
    avg = lax.all_to_all(avg, ("x", "yhi", "core"), 0, 0)
    return blend(prompt_ids, mine, modulation, avg).reshape(latents.shape)


def solution(mesh):
    fine = Mesh(mesh.devices.reshape(4, 8, NX, NY, NC), ("ylo", "z", "x", "yhi", "core"))
    win, head = ("ylo", "z"), ("x", "yhi", "core")
    in_specs = (P(win, None, head, None), P(win), P(), P(None, head, None), P())
    out_specs = P(win, None, head, None)
    return jax.shard_map(shards, mesh=fine, in_specs=in_specs, out_specs=out_specs, check_vma=False)
```

time: 213 us -> 133 us (0.62)
  the two profiles are of different devices: /device:TPU:24 before, /device:TPU:200 now
where the time goes in v1:
time: 133 us; the launch traced here: 132 us
  starting transfers between devices  43.4 us (33%)
  waiting for transfers between devices  34.6 us (26%)
  blocking collectives  30.1 us (23%)
  Pallas kernels  19.7 us (15%)
  local copies, waits for them, and re-layouts  3.25 us (2%)
    ppermute x10, starting transfers between devices, around(): return lax.ppermute(value, axis, [(i, (i + by) % n) for i in range(n)])  36 us
    all_to_all x1, blocking collectives, shards(): avg = lax.all_to_all(avg, ('x', 'yhi', 'core'), 0, 0)  30.1 us
    ppermute x10, waiting for transfers between devices, around(): return lax.ppermute(value, axis, [(i, (i + by) % n) for i in range(n)])  25.6 us
    pallas_call x2, Pallas kernels, project(): pl.pallas_call(project_kernel, grid_spec=pltpu.PrefetchScalarGridSpec(num...  10.6 us
    ppermute x2, waiting for transfers between devices, along(): lax.ppermute(value, ('ylo', 'z'), [(i, i + by) for i in range(n) if 0 <=...  9.08 us
    pallas_call x2, Pallas kernels, attend(): pl.pallas_call(functools.partial(attend_kernel, first, count), in_specs=[...  7.44 us
    ppermute x2, starting transfers between devices, along(): lax.ppermute(value, ('ylo', 'z'), [(i, i + by) for i in range(n) if 0 <=...  7.41 us
    unnamed x9, local copies, waits for them, and re-layouts  3.18 us
  transfers between devices with their start and end apart: 12, of which 7 were waited for; matrix products, arithmetic and copies ran while one was open for 1% of the time, Pallas kernels for 8%

profile of v1, /device:TPU:200, one launch (start us, length us, event | category | flops | bytes accessed | tf_op | source)
XLA Modules:
  0.0 132.1 jit_solution(14100473569310087147)
XLA Ops:
  0.0 1.9 %collective-permute-start.3 = (bf16[576,3072]{1,0:T(8,128)(2,1)}, bf16[576,3072]{1,0:T(8,128)(2,1)}, u32[]{:S(2)}, u32[]{:S(2)}) collective-permute-start(bf16[576,3072]{1,0:T(8,128)(2,1)} %bitcast.10), channel_id=1, source_target_pairs={{0,1},{1,0},{2,3},{3,2},{4,5},{5,4},{6,7},{7,6},{8,9},{9,8},{10,11... | collective-permute-start | bytes 10616840 | tf_op jit(solution)/shard_map/ppermute | solution.py:192
  1.9 6.8 %collective-permute-start.5 = (bf16[64,3072]{1,0:T(8,128)(2,1)}, bf16[64,3072]{1,0:T(8,128)(2,1)S(1)}, u32[]{:S(2)}, u32[]{:S(2)}) collective-permute-start(bf16[64,3072]{1,0:T(8,128)(2,1)} %bitcast.13), channel_id=1, source_target_pairs={{0,2},{2,0},{1,3},{3,1},{4,6},{6,4},{5,7},{7,5},{8,10},{10,8},{9,1... | collective-permute-start | bytes 1179656 | tf_op jit(solution)/shard_map/ppermute | solution.py:192
  8.8 18.5 %collective-permute-done.5.t0 = bf16[64,3072]{1,0:T(8,128)(2,1)S(1)} collective-permute-done((bf16[64,3072]{1,0:T(8,128)(2,1)}, bf16[64,3072]{1,0:T(8,128)(2,1)S(1)}, u32[]{:S(2)}, u32[]{:S(2)}) %collective-permute-start.5) | collective-permute-done | bytes 393248 | tf_op jit(solution)/shard_map/ppermute | solution.py:192
  27.3 3.4 %collective-permute-start.6 = (bf16[64,3072]{1,0:T(8,128)(2,1)S(1)}, bf16[64,3072]{1,0:T(8,128)(2,1)S(1)}, u32[]{:S(2)}, u32[]{:S(2)}) collective-permute-start(bf16[64,3072]{1,0:T(8,128)(2,1)S(1)} %collective-permute-done.5.t0), channel_id=1, source_target_pairs={{0,4},{4,8},{8,12},{12,0},{1,5},{5,9},{9,13},{13,1},{2,6},{6,10},{... | collective-permute-start | bytes 1179656 | tf_op jit(solution)/shard_map/ppermute | solution.py:192
  30.7 3.7 %collective-permute-start.7 = (bf16[64,3072]{1,0:T(8,128)(2,1)S(1)}, bf16[64,3072]{1,0:T(8,128)(2,1)S(1)}, u32[]{:S(2)}, u32[]{:S(2)}) collective-permute-start(bf16[64,3072]{1,0:T(8,128)(2,1)S(1)} %collective-permute-done.5.t0), channel_id=1, source_target_pairs={{0,12},{4,0},{8,4},{12,8},{1,13},{5,1},{9,5},{13,9},{2,14},{6,2},{... | collective-permute-start | bytes 1179656 | tf_op jit(solution)/shard_map/ppermute | solution.py:192
  34.3 3.7 %collective-permute-start.8 = (bf16[64,3072]{1,0:T(8,128)(2,1)S(1)}, bf16[64,3072]{1,0:T(8,128)(2,1)S(1)}, u32[]{:S(2)}, u32[]{:S(2)}) collective-permute-start(bf16[64,3072]{1,0:T(8,128)(2,1)S(1)} %collective-permute-done.5.t0), channel_id=1, source_target_pairs={{0,8},{4,12},{8,0},{12,4},{1,9},{5,13},{9,1},{13,5},{2,10},{6,14},... | collective-permute-start | bytes 1179656 | tf_op jit(solution)/shard_map/ppermute | solution.py:192
  38.1 2.5 %collective-permute-start = (bf16[64,3072]{1,0:T(8,128)(2,1)}, bf16[64,3072]{1,0:T(8,128)(2,1)S(1)}, u32[]{:S(2)}, u32[]{:S(2)}) collective-permute-start(bf16[64,3072]{1,0:T(8,128)(2,1)} %bitcast.14), channel_id=1, source_target_pairs={{0,4},{4,8},{8,12},{12,0},{1,5},{5,9},{9,13},{13,1},{2,6},{6,10},{... | collective-permute-start | bytes 1179656 | tf_op jit(solution)/shard_map/ppermute | solution.py:192
  40.6 0.8 collective-permute-done.6.t1
  41.4 4.4 %collective-permute-start.1 = (bf16[64,3072]{1,0:T(8,128)(2,1)}, bf16[64,3072]{1,0:T(8,128)(2,1)S(1)}, u32[]{:S(2)}, u32[]{:S(2)}) collective-permute-start(bf16[64,3072]{1,0:T(8,128)(2,1)} %bitcast.15), channel_id=1, source_target_pairs={{0,12},{4,0},{8,4},{12,8},{1,13},{5,1},{9,5},{13,9},{2,14},{6,2},{... | collective-permute-start | bytes 1179656 | tf_op jit(solution)/shard_map/ppermute | solution.py:192
  45.9 3.2 %collective-permute-done.7.t2 = bf16[64,3072]{1,0:T(8,128)(2,1)S(1)} collective-permute-done((bf16[64,3072]{1,0:T(8,128)(2,1)S(1)}, bf16[64,3072]{1,0:T(8,128)(2,1)S(1)}, u32[]{:S(2)}, u32[]{:S(2)}) %collective-permute-start.7) | collective-permute-done | bytes 393248 | tf_op jit(solution)/shard_map/ppermute | solution.py:192
  49.1 5.5 %collective-permute-start.2 = (bf16[64,3072]{1,0:T(8,128)(2,1)}, bf16[64,3072]{1,0:T(8,128)(2,1)S(1)}, u32[]{:S(2)}, u32[]{:S(2)}) collective-permute-start(bf16[64,3072]{1,0:T(8,128)(2,1)} %bitcast.16), channel_id=1, source_target_pairs={{0,8},{4,12},{8,0},{12,4},{1,9},{5,13},{9,1},{13,5},{2,10},{6,14},... | collective-permute-start | bytes 1179656 | tf_op jit(solution)/shard_map/ppermute | solution.py:192
  54.6 1.2 copy.8.mod_ref
  56.4 0.0 collective-permute-done.8.t3
  56.4 0.0 collective-permute-done.3.wb
  56.4 0.0 copy-start
  56.4 2.0 %copy-done = bf16[3,192,3072]{2,1,0:T(8,128)(2,1)S(1)} copy-done((bf16[3,192,3072]{2,1,0:T(8,128)(2,1)S(1)}, bf16[3,192,3072]{2,1,0:T(8,128)(2,1)}, u32[]{:S(2)}) %copy-start) | copy-done | bytes 3538968
  58.4 0.0 copy-start.1
  58.4 0.0 copy-start.2
  58.4 5.3 %shard_map.56 = (bf16[256,576]{1,0:T(8,128)(2,1)S(1)}, bf16[256,576]{1,0:T(8,128)(2,1)S(1)}) custom-call(s32[1]{0:T(128)S(6)} %copy.9.pid, bf16[64,3072]{1,0:T(8,128)(2,1)S(1)} %collective-permute-done.5.t0, bf16[64,3072]{1,0:T(8,128)(2,1)S(1)} %collective-permute-done.6.t1, bf16[64,3072]{1,0:T(8,128)(2,1)S(1)} %collective-permute-done.7.t2, ...), custom_call_target="tpu_custom_call" | custom-call | tf_op jit(solution)/shard_map/pallas_call | solution.py:46
  63.7 0.0 copy-start.3
  63.8 1.9 %collective-permute-start.9 = (bf16[256,576]{1,0:T(8,128)(2,1)S(1)}, bf16[256,576]{1,0:T(8,128)(2,1)S(1)}, u32[]{:S(2)}, u32[]{:S(2)}) collective-permute-start(bf16[256,576]{1,0:T(8,128)(2,1)S(1)} %get-tuple-element.12), channel_id=1, source_target_pairs={{0,1},{1,0},{2,3},{3,2},{4,5},{5,4},{6,7},{7,6},{8,9},{9,8},{10,11... | collective-permute-start | bytes 884744 | tf_op jit(solution)/shard_map/ppermute | solution.py:192
  65.7 0.0 collective-permute-done.t1
  65.7 0.0 collective-permute-done.1.t2
  65.7 1.7 %collective-permute-done.2.t3 = bf16[64,3072]{1,0:T(8,128)(2,1)S(1)} collective-permute-done((bf16[64,3072]{1,0:T(8,128)(2,1)}, bf16[64,3072]{1,0:T(8,128)(2,1)S(1)}, u32[]{:S(2)}, u32[]{:S(2)}) %collective-permute-start.2) | collective-permute-done | bytes 393248 | tf_op jit(solution)/shard_map/ppermute | solution.py:192
  67.4 0.0 copy-done.1
  67.4 0.0 copy-done.2
  67.4 5.3 %shard_map.55 = (bf16[256,576]{1,0:T(8,128)(2,1)S(1)}, bf16[256,576]{1,0:T(8,128)(2,1)S(1)}) custom-call(s32[1]{0:T(128)S(6)} %copy.9.pid, bf16[64,3072]{1,0:T(8,128)(2,1)S(1)} %bitcast.17, bf16[64,3072]{1,0:T(8,128)(2,1)S(1)} %collective-permute-done.t1, bf16[64,3072]{1,0:T(8,128)(2,1)S(1)} %collective-permute-done.1.t2, ...), custom_call_target="tpu_custom_call" | custom-call | tf_op jit(solution)/shard_map/pallas_call | solution.py:46
  72.7 2.1 %collective-permute-start.4 = (bf16[256,576]{1,0:T(8,128)(2,1)S(1)}, bf16[256,576]{1,0:T(8,128)(2,1)S(1)}, u32[]{:S(2)}, u32[]{:S(2)}) collective-permute-start(bf16[256,576]{1,0:T(8,128)(2,1)S(1)} %get-tuple-element.10), channel_id=1, source_target_pairs={{0,1},{1,0},{2,3},{3,2},{4,5},{5,4},{6,7},{7,6},{8,9},{9,8},{10,11... | collective-permute-start | bytes 884744 | tf_op jit(solution)/shard_map/ppermute | solution.py:192
  74.8 0.1 pad_add_fusion.1.place
  74.9 0.0 collective-permute-done.9
  74.9 1.3 %collective-permute-done.4 = bf16[256,576]{1,0:T(8,128)(2,1)S(1)} collective-permute-done((bf16[256,576]{1,0:T(8,128)(2,1)S(1)}, bf16[256,576]{1,0:T(8,128)(2,1)S(1)}, u32[]{:S(2)}, u32[]{:S(2)}) %collective-permute-start.4) | collective-permute-done | bytes 294944 | tf_op jit(solution)/shard_map/ppermute | solution.py:192
  76.2 3.7 %shard_map.58.high = bf16[16,32,192]{2,1,0:T(8,128)(2,1)S(1)} custom-call(s32[3]{0:T(128)S(1)} %pad_add_fusion.1.place, bf16[4,64,576]{2,1,0:T(8,128)(2,1)S(1)} %bitcast.23, bf16[4,64,576]{2,1,0:T(8,128)(2,1)S(1)} %bitcast.25, bf16[4,64,576]{2,1,0:T(8,128)(2,1)S(1)} %bitcast.19, bf16[4,64,576]{2,1,0:T(8,128)(2,1)S(1)} %bitcast.21), custom_call_target="tpu_custom_call" | custom-call | tf_op jit(solution)/shard_map/pallas_call | solution.py:109
  79.9 3.7 %shard_map.57.low = bf16[16,32,192]{2,1,0:T(8,128)(2,1)S(1)} custom-call(s32[3]{0:T(128)S(1)} %pad_add_fusion.1.place, bf16[4,64,576]{2,1,0:T(8,128)(2,1)S(1)} %bitcast.24, bf16[4,64,576]{2,1,0:T(8,128)(2,1)S(1)} %bitcast.26, bf16[4,64,576]{2,1,0:T(8,128)(2,1)S(1)} %bitcast.20, bf16[4,64,576]{2,1,0:T(8,128)(2,1)S(1)} %bitcast.22), custom_call_target="tpu_custom_call" | custom-call | tf_op jit(solution)/shard_map/pallas_call | solution.py:109
  83.7 5.5 %collective-permute-start.10 = (bf16[16,32,192]{2,1,0:T(8,128)(2,1)S(1)}, bf16[16,32,192]{2,1,0:T(8,128)(2,1)S(1)}, u32[]{:S(2)}, u32[]{:S(2)}) collective-permute-start(bf16[16,32,192]{2,1,0:T(8,128)(2,1)S(1)} %shard_map.58.high), channel_id=1, source_target_pairs={{0,16},{16,32},{32,48},{48,64},{64,80},{80,96},{96,112},{112,128},... | collective-permute-start | bytes 589832 | tf_op jit(solution)/shard_map/ppermute | solution.py:197
  89.2 1.9 %collective-permute-start.11 = (bf16[16,32,192]{2,1,0:T(8,128)(2,1)S(1)}, bf16[16,32,192]{2,1,0:T(8,128)(2,1)S(1)}, u32[]{:S(2)}, u32[]{:S(2)}) collective-permute-start(bf16[16,32,192]{2,1,0:T(8,128)(2,1)S(1)} %shard_map.57.low), channel_id=1, source_target_pairs={{16,0},{32,16},{48,32},{64,48},{80,64},{96,80},{112,96},{128,112},... | collective-permute-start | bytes 589832 | tf_op jit(solution)/shard_map/ppermute | solution.py:197
  91.1 0.0 copy-done.3
  91.1 0.1 pad_add_fusion
  91.2 0.1 dynamic_slice.3.overlap
  91.3 3.7 %collective-permute-done.10.before = bf16[16,32,192]{2,1,0:T(8,128)(2,1)S(1)} collective-permute-done((bf16[16,32,192]{2,1,0:T(8,128)(2,1)S(1)}, bf16[16,32,192]{2,1,0:T(8,128)(2,1)S(1)}, u32[]{:S(2)}, u32[]{:S(2)}) %collective-permute-start.10) | collective-permute-done | bytes 196640 | tf_op jit(solution)/shard_map/ppermute | solution.py:197
  95.0 5.3 %collective-permute-done.11.after = bf16[16,32,192]{2,1,0:T(8,128)(2,1)S(1)} collective-permute-done((bf16[16,32,192]{2,1,0:T(8,128)(2,1)S(1)}, bf16[16,32,192]{2,1,0:T(8,128)(2,1)S(1)}, u32[]{:S(2)}, u32[]{:S(2)}) %collective-permute-start.11) | collective-permute-done | bytes 196640 | tf_op jit(solution)/shard_map/ppermute | solution.py:197
  100.3 0.7 shard_map.59
  101.1 30.1 %all_to_all.5.avg = bf16[16,64,192]{2,1,0:T(8,128)(2,1)S(1)} all-to-all(bf16[16,64,192]{2,1,0:T(8,128)(2,1)S(1)} %shard_map.59), channel_id=1, replica_groups=mesh['ylo'=4,'z'=8,'x'=4,'yhi'=2,'core'=2] {'x','yhi','core'}, dimensions={0} | all-to-all | bytes 786432 | tf_op jit(solution)/shard_map/all_to_all | solution.py:227
  131.2 0.9 shard_map.60
Async XLA Ops:
  0.0 56.4 %collective-permute-start.3 = (bf16[576,3072]{1,0:T(8,128)(2,1)}, bf16[576,3072]{1,0:T(8,128)(2,1)}, u32[]{:S(2)}, u32[]{:S(2)}) collective-permute-start(bf16[576,3072]{1,0:T(8,128)(2,1)} %bitcast.10), channel_id=1, source_target_pairs={{0,1},{1,0},{2,3},{3,2},{4,5},{5,4},{6,7},{7,6},{8,9},{9,8},{10,11... | collective-permute-start | bytes 10616840 | tf_op jit(solution)/shard_map/ppermute | solution.py:192
  1.9 25.4 %collective-permute-start.5 = (bf16[64,3072]{1,0:T(8,128)(2,1)}, bf16[64,3072]{1,0:T(8,128)(2,1)S(1)}, u32[]{:S(2)}, u32[]{:S(2)}) collective-permute-start(bf16[64,3072]{1,0:T(8,128)(2,1)} %bitcast.13), channel_id=1, source_target_pairs={{0,2},{2,0},{1,3},{3,1},{4,6},{6,4},{5,7},{7,5},{8,10},{10,8},{9,1... | collective-permute-start | bytes 1179656 | tf_op jit(solution)/shard_map/ppermute | solution.py:192
  27.3 14.1 %collective-permute-start.6 = (bf16[64,3072]{1,0:T(8,128)(2,1)S(1)}, bf16[64,3072]{1,0:T(8,128)(2,1)S(1)}, u32[]{:S(2)}, u32[]{:S(2)}) collective-permute-start(bf16[64,3072]{1,0:T(8,128)(2,1)S(1)} %collective-permute-done.5.t0), channel_id=1, source_target_pairs={{0,4},{4,8},{8,12},{12,0},{1,5},{5,9},{9,13},{13,1},{2,6},{6,10},{... | collective-permute-start | bytes 1179656 | tf_op jit(solution)/shard_map/ppermute | solution.py:192
  30.7 18.4 %collective-permute-start.7 = (bf16[64,3072]{1,0:T(8,128)(2,1)S(1)}, bf16[64,3072]{1,0:T(8,128)(2,1)S(1)}, u32[]{:S(2)}, u32[]{:S(2)}) collective-permute-start(bf16[64,3072]{1,0:T(8,128)(2,1)S(1)} %collective-permute-done.5.t0), channel_id=1, source_target_pairs={{0,12},{4,0},{8,4},{12,8},{1,13},{5,1},{9,5},{13,9},{2,14},{6,2},{... | collective-permute-start | bytes 1179656 | tf_op jit(solution)/shard_map/ppermute | solution.py:192
  34.3 22.1 %collective-permute-start.8 = (bf16[64,3072]{1,0:T(8,128)(2,1)S(1)}, bf16[64,3072]{1,0:T(8,128)(2,1)S(1)}, u32[]{:S(2)}, u32[]{:S(2)}) collective-permute-start(bf16[64,3072]{1,0:T(8,128)(2,1)S(1)} %collective-permute-done.5.t0), channel_id=1, source_target_pairs={{0,8},{4,12},{8,0},{12,4},{1,9},{5,13},{9,1},{13,5},{2,10},{6,14},... | collective-permute-start | bytes 1179656 | tf_op jit(solution)/shard_map/ppermute | solution.py:192
  38.1 27.6 %collective-permute-start = (bf16[64,3072]{1,0:T(8,128)(2,1)}, bf16[64,3072]{1,0:T(8,128)(2,1)S(1)}, u32[]{:S(2)}, u32[]{:S(2)}) collective-permute-start(bf16[64,3072]{1,0:T(8,128)(2,1)} %bitcast.14), channel_id=1, source_target_pairs={{0,4},{4,8},{8,12},{12,0},{1,5},{5,9},{9,13},{13,1},{2,6},{6,10},{... | collective-permute-start | bytes 1179656 | tf_op jit(solution)/shard_map/ppermute | solution.py:192
  41.4 24.3 %collective-permute-start.1 = (bf16[64,3072]{1,0:T(8,128)(2,1)}, bf16[64,3072]{1,0:T(8,128)(2,1)S(1)}, u32[]{:S(2)}, u32[]{:S(2)}) collective-permute-start(bf16[64,3072]{1,0:T(8,128)(2,1)} %bitcast.15), channel_id=1, source_target_pairs={{0,12},{4,0},{8,4},{12,8},{1,13},{5,1},{9,5},{13,9},{2,14},{6,2},{... | collective-permute-start | bytes 1179656 | tf_op jit(solution)/shard_map/ppermute | solution.py:192
  49.1 18.3 %collective-permute-start.2 = (bf16[64,3072]{1,0:T(8,128)(2,1)}, bf16[64,3072]{1,0:T(8,128)(2,1)S(1)}, u32[]{:S(2)}, u32[]{:S(2)}) collective-permute-start(bf16[64,3072]{1,0:T(8,128)(2,1)} %bitcast.16), channel_id=1, source_target_pairs={{0,8},{4,12},{8,0},{12,4},{1,9},{5,13},{9,1},{13,5},{2,10},{6,14},... | collective-permute-start | bytes 1179656 | tf_op jit(solution)/shard_map/ppermute | solution.py:192
  56.4 2.0 %copy-start = (bf16[3,192,3072]{2,1,0:T(8,128)(2,1)S(1)}, bf16[3,192,3072]{2,1,0:T(8,128)(2,1)}, u32[]{:S(2)}) copy-start(bf16[3,192,3072]{2,1,0:T(8,128)(2,1)} %param.8) | copy-start | bytes 10616836
  58.4 8.9 %copy-start.1 = (bf16[3,192,3072]{2,1,0:T(8,128)(2,1)S(1)}, bf16[3,192,3072]{2,1,0:T(8,128)(2,1)}, u32[]{:S(2)}) copy-start(bf16[3,192,3072]{2,1,0:T(8,128)(2,1)} %param.8) | copy-start | bytes 10616836
  58.4 8.9 %copy-start.2 = (bf16[1,8,8,3072]{3,2,1,0:T(8,128)(2,1)S(1)}, bf16[1,8,8,3072]{3,2,1,0:T(8,128)(2,1)}, u32[]{:S(2)}) copy-start(bf16[1,8,8,3072]{3,2,1,0:T(8,128)(2,1)} %param.5) | copy-start | bytes 1179652
  63.7 27.4 %copy-start.3 = (s32[32]{0:T(128)S(1)}, s32[32]{0:T(128)}, u32[]{:S(2)}) copy-start(s32[32]{0:T(128)} %param.9) | copy-start | bytes 388
  63.8 11.1 %collective-permute-start.9 = (bf16[256,576]{1,0:T(8,128)(2,1)S(1)}, bf16[256,576]{1,0:T(8,128)(2,1)S(1)}, u32[]{:S(2)}, u32[]{:S(2)}) collective-permute-start(bf16[256,576]{1,0:T(8,128)(2,1)S(1)} %get-tuple-element.12), channel_id=1, source_target_pairs={{0,1},{1,0},{2,3},{3,2},{4,5},{5,4},{6,7},{7,6},{8,9},{9,8},{10,11... | collective-permute-start | bytes 884744 | tf_op jit(solution)/shard_map/ppermute | solution.py:192
  72.7 3.5 %collective-permute-start.4 = (bf16[256,576]{1,0:T(8,128)(2,1)S(1)}, bf16[256,576]{1,0:T(8,128)(2,1)S(1)}, u32[]{:S(2)}, u32[]{:S(2)}) collective-permute-start(bf16[256,576]{1,0:T(8,128)(2,1)S(1)} %get-tuple-element.10), channel_id=1, source_target_pairs={{0,1},{1,0},{2,3},{3,2},{4,5},{5,4},{6,7},{7,6},{8,9},{9,8},{10,11... | collective-permute-start | bytes 884744 | tf_op jit(solution)/shard_map/ppermute | solution.py:192
  83.7 11.3 %collective-permute-start.10 = (bf16[16,32,192]{2,1,0:T(8,128)(2,1)S(1)}, bf16[16,32,192]{2,1,0:T(8,128)(2,1)S(1)}, u32[]{:S(2)}, u32[]{:S(2)}) collective-permute-start(bf16[16,32,192]{2,1,0:T(8,128)(2,1)S(1)} %shard_map.58.high), channel_id=1, source_target_pairs={{0,16},{16,32},{32,48},{48,64},{64,80},{80,96},{96,112},{112,128},... | collective-permute-start | bytes 589832 | tf_op jit(solution)/shard_map/ppermute | solution.py:197
  89.2 11.2 %collective-permute-start.11 = (bf16[16,32,192]{2,1,0:T(8,128)(2,1)S(1)}, bf16[16,32,192]{2,1,0:T(8,128)(2,1)S(1)}, u32[]{:S(2)}, u32[]{:S(2)}) collective-permute-start(bf16[16,32,192]{2,1,0:T(8,128)(2,1)S(1)} %shard_map.57.low), channel_id=1, source_target_pairs={{16,0},{32,16},{48,32},{64,48},{80,64},{96,80},{112,96},{128,112},... | collective-permute-start | bytes 589832 | tf_op jit(solution)/shard_map/ppermute | solution.py:197

commit v2 on v1

--- a/solution.py
+++ b/solution.py
@@ -15,12 +15,15 @@
 OFFSETS = (0, 3, 1, 2)
 
 
-def project_kernel(pid, t0, t1, t2, t3, mod_ref, wa, wb, oa, ob, va, vb, sems):
-    copies = [pltpu.make_async_copy(wa, va, sems.at[0]), pltpu.make_async_copy(wb, vb, sems.at[1])]
-    for c in copies:
-        c.start()
-    shift = mod_ref[0, 0:1, :]
-    scale = 1.0 + mod_ref[0, 1:2, :]
+def cost(flops, inputs, outputs, transcendentals=0):
+    size = sum(a.size * a.dtype.itemsize for a in (*inputs, *outputs))
+    return pl.CostEstimate(flops=flops, bytes_accessed=size, transcendentals=transcendentals)
+
+
+def project_kernel(pid, t0, t1, t2, t3, mod_ref, wa, wb, oa, ob):
+    row = pl.ds(pid[0], 1)
+    shift = mod_ref[0, row, :]
+    scale = 1.0 + mod_ref[1, row, :]
     parts = []
     for t in (t0, t1, t2, t3):
         xf = t[...].astype(jnp.float32)
@@ -29,35 +32,24 @@
         var = jnp.mean(xc * xc, axis=-1, keepdims=True)
         parts.append((xc * lax.rsqrt(var + 1e-06) * scale + shift).astype(jnp.bfloat16))
     normed = jnp.concatenate(parts, axis=0)
-    for c, v, o in zip(copies, (va, vb), (oa, ob)):
-        c.wait()
+    for w, o in ((wa, oa), (wb, ob)):
         o[...] = lax.dot_general(
-            normed, v[...], (((1,), (1,)), ((), ())), preferred_element_type=jnp.float32
+            normed, w[...], (((1,), (1,)), ((), ())), preferred_element_type=jnp.float32
         ).astype(jnp.bfloat16)
 
 
 def project(pid, blocks, modulation, wa, wb):
     rows, width = blocks[0].shape
     feats = wa.shape[0]
-    tok = pl.BlockSpec((rows, width), lambda i, p: (0, 0))
-    out = pl.BlockSpec((4 * rows, feats), lambda i, p: (0, 0))
-    hbm = pl.BlockSpec(memory_space=pl.ANY)
+    full = pl.BlockSpec(memory_space=pltpu.VMEM)
     shape = jax.ShapeDtypeStruct((4 * rows, feats), jnp.bfloat16)
     return pl.pallas_call(
         project_kernel,
-        grid_spec=pltpu.PrefetchScalarGridSpec(
-            num_scalar_prefetch=1,
-            grid=(1,),
-            in_specs=[tok] * 4 + [pl.BlockSpec((1, 3, width), lambda i, p: (p[0], 0, 0)), hbm, hbm],
-            out_specs=[out, out],
-            scratch_shapes=[
-                pltpu.VMEM((feats, width), jnp.bfloat16),
-                pltpu.VMEM((feats, width), jnp.bfloat16),
-                pltpu.SemaphoreType.DMA((2,)),
-            ],
-        ),
+        in_specs=[pl.BlockSpec(memory_space=pltpu.SMEM)] + [full] * 7,
+        out_specs=[full, full],
         out_shape=[shape, shape],
-        compiler_params=pltpu.CompilerParams(vmem_limit_bytes=48 * MIB),
+        cost_estimate=cost(16 * rows * feats * width, (*blocks, wa, wb), (shape, shape)),
+        compiler_params=pltpu.CompilerParams(vmem_limit_bytes=24 * MIB),
     )(pid, *blocks, modulation, wa, wb)
 
 
@@ -106,12 +98,15 @@
 def attend(first, count, place, groups):
     per, rows, feats = groups[0].shape
     full = pl.BlockSpec(memory_space=pltpu.VMEM)
+    shape = jax.ShapeDtypeStruct((4 * per, count, feats // 3), jnp.bfloat16)
+    scores = 16 * per * per * count * rows * (feats // 3 // HEAD_DIM)
     return pl.pallas_call(
         functools.partial(attend_kernel, first, count),
         in_specs=[pl.BlockSpec(memory_space=pltpu.SMEM)] + [full] * 4,
         out_specs=full,
-        out_shape=jax.ShapeDtypeStruct((4 * per, count, feats // 3), jnp.bfloat16),
-        compiler_params=pltpu.CompilerParams(vmem_limit_bytes=48 * MIB),
+        out_shape=shape,
+        cost_estimate=cost(16 * HEAD_DIM * scores, groups, (shape,), scores),
+        compiler_params=pltpu.CompilerParams(vmem_limit_bytes=24 * MIB),
     )(place, *groups)
 
 
@@ -155,35 +150,27 @@
         in_specs=[pl.BlockSpec(memory_space=pltpu.SMEM)] + [full] * 4,
         out_specs=full,
         out_shape=jax.ShapeDtypeStruct((blocks, 2 * half, width), jnp.bfloat16),
-        compiler_params=pltpu.CompilerParams(vmem_limit_bytes=32 * MIB),
+        compiler_params=pltpu.CompilerParams(vmem_limit_bytes=16 * MIB),
     )(overlap, low, high, before, after)
 
 
 def blend_kernel(pid, lat, mod_ref, avg, out):
     blocks, _, width = avg.shape
+    gate = mod_ref[2, pl.ds(pid[0], 1), :]
     for b in range(0, blocks, 2):
         cols = slice(b * width, (b + 2) * width)
         a = jnp.concatenate([avg[b].astype(jnp.float32), avg[b + 1].astype(jnp.float32)], axis=1)
-        out[:, cols] = (lat[:, cols].astype(jnp.float32) + mod_ref[0, 2:3, cols] * a).astype(jnp.bfloat16)
+        out[:, cols] = (lat[:, cols].astype(jnp.float32) + gate[:, cols] * a).astype(jnp.bfloat16)
 
 
 def blend(pid, lat, modulation, avg):
-    rows, width = lat.shape
-    tok = pl.BlockSpec((rows, width), lambda i, p: (0, 0))
+    full = pl.BlockSpec(memory_space=pltpu.VMEM)
     return pl.pallas_call(
         blend_kernel,
-        grid_spec=pltpu.PrefetchScalarGridSpec(
-            num_scalar_prefetch=1,
-            grid=(1,),
-            in_specs=[
-                tok,
-                pl.BlockSpec((1, 3, width), lambda i, p: (p[0], 0, 0)),
-                pl.BlockSpec(avg.shape, lambda i, p: (0, 0, 0)),
-            ],
-            out_specs=tok,
-        ),
-        out_shape=jax.ShapeDtypeStruct((rows, width), jnp.bfloat16),
-        compiler_params=pltpu.CompilerParams(vmem_limit_bytes=32 * MIB),
+        in_specs=[pl.BlockSpec(memory_space=pltpu.SMEM)] + [full] * 3,
+        out_specs=full,
+        out_shape=jax.ShapeDtypeStruct(lat.shape, jnp.bfloat16),
+        compiler_params=pltpu.CompilerParams(vmem_limit_bytes=16 * MIB),
     )(pid, lat, modulation, avg)
 
 
@@ -204,9 +191,11 @@
     wa = w_qkv.reshape(-1, width)
     place = jnp.stack([lax.axis_index("x"), lax.axis_index("yhi"), lax.axis_index("core")]).astype(jnp.int32)
 
+    modulation = jnp.transpose(modulation, (1, 0, 2))
     other = around(mine, "yhi", 1)
     near = [mine] + [around(mine, "x", by) for by in (1, 3, 2)]
     wb = around(wa, "core", 1)
+    other, *near = lax.optimization_barrier((other, *near))
     far = [other] + [around(other, "x", by) for by in (1, 3, 2)]
 
     own0, give0 = project(prompt_ids, near, modulation, wa, wb)

time: 133 us -> 118 us (0.89)
  the two profiles are of different devices: /device:TPU:200 before, /device:TPU:8 now
where the time goes in v2:
time: 118 us
  starting transfers between devices  48 us (41%)
  blocking collectives  25.9 us (22%)
  waiting for transfers between devices  23 us (19%)
  Pallas kernels  15.8 us (13%)
  local copies, waits for them, and re-layouts  4.05 us (3%)
    ppermute x10, starting transfers between devices, around(): return lax.ppermute(value, axis, [(i, (i + by) % n) for i in range(n)])  34.3 us
    all_to_all x1, blocking collectives, shards(): avg = lax.all_to_all(avg, ('x', 'yhi', 'core'), 0, 0)  25.9 us
    ppermute x10, waiting for transfers between devices, around(): return lax.ppermute(value, axis, [(i, (i + by) % n) for i in range(n)])  17.3 us
    ppermute x2, starting transfers between devices, along(): lax.ppermute(value, ('ylo', 'z'), [(i, i + by) for i in range(n) if 0 <=...  13.7 us
    pallas_call x2, Pallas kernels, attend(): pl.pallas_call(functools.partial(attend_kernel, first, count), in_specs=[...  7.44 us
    pallas_call x2, Pallas kernels, project(): pl.pallas_call(project_kernel, in_specs=[pl.BlockSpec(memory_space=pltpu....  6.67 us
    ppermute x2, waiting for transfers between devices, along(): lax.ppermute(value, ('ylo', 'z'), [(i, i + by) for i in range(n) if 0 <=...  5.67 us
    unnamed x14, local copies, waits for them, and re-layouts  3.97 us
  transfers between devices with their start and end apart: 12, of which 6 were waited for; matrix products, arithmetic and copies ran while one was open for 0% of the time, Pallas kernels for 6%

profile of v2, /device:TPU:8, one launch (start us, length us, event | category | flops | bytes accessed | tf_op | source)
XLA Modules:
  0.0 117.6 jit_solution(15303886612392902390)
XLA Ops:
  0.0 1.9 %collective-permute-start.4 = (bf16[576,3072]{1,0:T(8,128)(2,1)}, bf16[576,3072]{1,0:T(8,128)(2,1)S(1)}, u32[]{:S(2)}, u32[]{:S(2)}) collective-permute-start(bf16[576,3072]{1,0:T(8,128)(2,1)} %bitcast.11), channel_id=1, source_target_pairs={{0,1},{1,0},{2,3},{3,2},{4,5},{5,4},{6,7},{7,6},{8,9},{9,8},{10,11... | collective-permute-start | bytes 10616840 | tf_op jit(solution)/shard_map/ppermute | solution.py:179
  1.9 6.8 %collective-permute-start = (bf16[64,3072]{1,0:T(8,128)(2,1)}, bf16[64,3072]{1,0:T(8,128)(2,1)S(1)}, u32[]{:S(2)}, u32[]{:S(2)}) collective-permute-start(bf16[64,3072]{1,0:T(8,128)(2,1)} %bitcast.17), channel_id=1, source_target_pairs={{0,2},{2,0},{1,3},{3,1},{4,6},{6,4},{5,7},{7,5},{8,10},{10,8},{9,1... | collective-permute-start | bytes 1179656 | tf_op jit(solution)/shard_map/ppermute | solution.py:179
  8.8 3.4 %collective-permute-start.1 = (bf16[64,3072]{1,0:T(8,128)(2,1)}, bf16[64,3072]{1,0:T(8,128)(2,1)S(1)}, u32[]{:S(2)}, u32[]{:S(2)}) collective-permute-start(bf16[64,3072]{1,0:T(8,128)(2,1)} %bitcast.18), channel_id=1, source_target_pairs={{0,4},{4,8},{8,12},{12,0},{1,5},{5,9},{9,13},{13,1},{2,6},{6,10},{... | collective-permute-start | bytes 1179656 | tf_op jit(solution)/shard_map/ppermute | solution.py:179
  12.2 3.7 %collective-permute-start.2 = (bf16[64,3072]{1,0:T(8,128)(2,1)}, bf16[64,3072]{1,0:T(8,128)(2,1)S(1)}, u32[]{:S(2)}, u32[]{:S(2)}) collective-permute-start(bf16[64,3072]{1,0:T(8,128)(2,1)} %bitcast.19), channel_id=1, source_target_pairs={{0,12},{4,0},{8,4},{12,8},{1,13},{5,1},{9,5},{13,9},{2,14},{6,2},{... | collective-permute-start | bytes 1179656 | tf_op jit(solution)/shard_map/ppermute | solution.py:179
  15.8 3.7 %collective-permute-start.3 = (bf16[64,3072]{1,0:T(8,128)(2,1)}, bf16[64,3072]{1,0:T(8,128)(2,1)S(1)}, u32[]{:S(2)}, u32[]{:S(2)}) collective-permute-start(bf16[64,3072]{1,0:T(8,128)(2,1)} %bitcast.20), channel_id=1, source_target_pairs={{0,8},{4,12},{8,0},{12,4},{1,9},{5,13},{9,1},{13,5},{2,10},{6,14},... | collective-permute-start | bytes 1179656 | tf_op jit(solution)/shard_map/ppermute | solution.py:179
  19.6 7.7 %collective-permute-done.t0 = bf16[64,3072]{1,0:T(8,128)(2,1)S(1)} collective-permute-done((bf16[64,3072]{1,0:T(8,128)(2,1)}, bf16[64,3072]{1,0:T(8,128)(2,1)S(1)}, u32[]{:S(2)}, u32[]{:S(2)}) %collective-permute-start) | collective-permute-done | bytes 393248 | tf_op jit(solution)/shard_map/ppermute | solution.py:179
  27.3 0.0 collective-permute-done.1.t1
  27.3 5.8 %collective-permute-done.2.t2 = bf16[64,3072]{1,0:T(8,128)(2,1)S(1)} collective-permute-done((bf16[64,3072]{1,0:T(8,128)(2,1)}, bf16[64,3072]{1,0:T(8,128)(2,1)S(1)}, u32[]{:S(2)}, u32[]{:S(2)}) %collective-permute-start.2) | collective-permute-done | bytes 393248 | tf_op jit(solution)/shard_map/ppermute | solution.py:179
  33.1 0.0 collective-permute-done.3.t3
  33.1 4.6 %collective-permute-start.6 = (bf16[64,3072]{1,0:T(8,128)(2,1)S(1)}, bf16[64,3072]{1,0:T(8,128)(2,1)S(1)}, u32[]{:S(2)}, u32[]{:S(2)}) collective-permute-start(bf16[64,3072]{1,0:T(8,128)(2,1)S(1)} %collective-permute-done.t0), channel_id=1, source_target_pairs={{0,4},{4,8},{8,12},{12,0},{1,5},{5,9},{9,13},{13,1},{2,6},{6,10},{... | collective-permute-start | bytes 1179656 | tf_op jit(solution)/shard_map/ppermute | solution.py:179
  37.7 2.8 %collective-permute-start.7 = (bf16[64,3072]{1,0:T(8,128)(2,1)S(1)}, bf16[64,3072]{1,0:T(8,128)(2,1)S(1)}, u32[]{:S(2)}, u32[]{:S(2)}) collective-permute-start(bf16[64,3072]{1,0:T(8,128)(2,1)S(1)} %collective-permute-done.t0), channel_id=1, source_target_pairs={{0,12},{4,0},{8,4},{12,8},{1,13},{5,1},{9,5},{13,9},{2,14},{6,2},{... | collective-permute-start | bytes 1179656 | tf_op jit(solution)/shard_map/ppermute | solution.py:179
  40.5 3.4 %collective-permute-start.8 = (bf16[64,3072]{1,0:T(8,128)(2,1)S(1)}, bf16[64,3072]{1,0:T(8,128)(2,1)S(1)}, u32[]{:S(2)}, u32[]{:S(2)}) collective-permute-start(bf16[64,3072]{1,0:T(8,128)(2,1)S(1)} %collective-permute-done.t0), channel_id=1, source_target_pairs={{0,8},{4,12},{8,0},{12,4},{1,9},{5,13},{9,1},{13,5},{2,10},{6,14},... | collective-permute-start | bytes 1179656 | tf_op jit(solution)/shard_map/ppermute | solution.py:179
  44.5 0.0 collective-permute-done.4.wb
  44.5 0.0 copy-start
  44.5 2.0 %copy-done = bf16[3,192,3072]{2,1,0:T(8,128)(2,1)S(1)} copy-done((bf16[3,192,3072]{2,1,0:T(8,128)(2,1)S(1)}, bf16[3,192,3072]{2,1,0:T(8,128)(2,1)}, u32[]{:S(2)}) %copy-start) | copy-done | bytes 3538968
  46.5 0.0 copy-start.2
  46.5 1.0 copy-done.2
  47.5 0.0 copy-start.4
  47.5 1.0 copy-done.4
  48.5 0.0 copy-start.1
  48.5 3.3 %shard_map.55 = (bf16[256,576]{1,0:T(8,128)(2,1)S(1)}, bf16[256,576]{1,0:T(8,128)(2,1)S(1)}) custom-call(s32[1]{0:T(128)S(6)} %copy.6.pid, bf16[64,3072]{1,0:T(8,128)(2,1)S(1)} %bitcast.21, bf16[64,3072]{1,0:T(8,128)(2,1)S(1)} %collective-permute-done.1.t1, bf16[64,3072]{1,0:T(8,128)(2,1)S(1)} %collective-permute-done.2.t2, ...), custom_call_target="tpu_custom_call" | custom-call | flops 1811939328 | bytes 9240576 | tf_op jit(solution)/shard_map/pallas_call | solution.py:46
  51.8 1.9 %collective-permute-start.5 = (bf16[256,576]{1,0:T(8,128)(2,1)S(1)}, bf16[256,576]{1,0:T(8,128)(2,1)S(1)}, u32[]{:S(2)}, u32[]{:S(2)}) collective-permute-start(bf16[256,576]{1,0:T(8,128)(2,1)S(1)} %get-tuple-element.19), channel_id=1, source_target_pairs={{0,1},{1,0},{2,3},{3,2},{4,5},{5,4},{6,7},{7,6},{8,9},{9,8},{10,11... | collective-permute-start | bytes 884744 | tf_op jit(solution)/shard_map/ppermute | solution.py:179
  53.7 0.0 collective-permute-done.6.t1
  53.7 0.0 collective-permute-done.7.t2
  53.7 2.5 %collective-permute-done.8.t3 = bf16[64,3072]{1,0:T(8,128)(2,1)S(1)} collective-permute-done((bf16[64,3072]{1,0:T(8,128)(2,1)S(1)}, bf16[64,3072]{1,0:T(8,128)(2,1)S(1)}, u32[]{:S(2)}, u32[]{:S(2)}) %collective-permute-start.8) | collective-permute-done | bytes 393248 | tf_op jit(solution)/shard_map/ppermute | solution.py:179
  56.2 0.0 copy-done.1
  56.2 3.3 %shard_map.56 = (bf16[256,576]{1,0:T(8,128)(2,1)S(1)}, bf16[256,576]{1,0:T(8,128)(2,1)S(1)}) custom-call(s32[1]{0:T(128)S(6)} %copy.6.pid, bf16[64,3072]{1,0:T(8,128)(2,1)S(1)} %collective-permute-done.t0, bf16[64,3072]{1,0:T(8,128)(2,1)S(1)} %collective-permute-done.6.t1, bf16[64,3072]{1,0:T(8,128)(2,1)S(1)} %collective-permute-done.7.t2, ...), custom_call_target="tpu_custom_call" | custom-call | flops 1811939328 | bytes 9240576 | tf_op jit(solution)/shard_map/pallas_call | solution.py:46
  59.6 2.1 %collective-permute-start.9 = (bf16[256,576]{1,0:T(8,128)(2,1)S(1)}, bf16[256,576]{1,0:T(8,128)(2,1)S(1)}, u32[]{:S(2)}, u32[]{:S(2)}) collective-permute-start(bf16[256,576]{1,0:T(8,128)(2,1)S(1)} %get-tuple-element.22), channel_id=1, source_target_pairs={{0,1},{1,0},{2,3},{3,2},{4,5},{5,4},{6,7},{7,6},{8,9},{9,8},{10,11... | collective-permute-start | bytes 884744 | tf_op jit(solution)/shard_map/ppermute | solution.py:179
  61.7 0.1 pad_add_fusion.1.place
  61.8 0.0 collective-permute-done.5
  61.8 1.3 %collective-permute-done.9 = bf16[256,576]{1,0:T(8,128)(2,1)S(1)} collective-permute-done((bf16[256,576]{1,0:T(8,128)(2,1)S(1)}, bf16[256,576]{1,0:T(8,128)(2,1)S(1)}, u32[]{:S(2)}, u32[]{:S(2)}) %collective-permute-start.9) | collective-permute-done | bytes 294944 | tf_op jit(solution)/shard_map/ppermute | solution.py:179
  63.1 3.7 %shard_map.57.low = bf16[16,32,192]{2,1,0:T(8,128)(2,1)S(1)} custom-call(s32[3]{0:T(128)S(1)} %pad_add_fusion.1.place, bf16[4,64,576]{2,1,0:T(8,128)(2,1)S(1)} %bitcast.23, bf16[4,64,576]{2,1,0:T(8,128)(2,1)S(1)} %bitcast.25, bf16[4,64,576]{2,1,0:T(8,128)(2,1)S(1)} %bitcast.27, bf16[4,64,576]{2,1,0:T(8,128)(2,1)S(1)} %bitcast.29), custom_call_target="tpu_custom_call" | custom-call | flops 1610612736 | bytes 1376256 | tf_op jit(solution)/shard_map/pallas_call | solution.py:103
  66.8 0.0 copy-start.6
  66.8 0.0 copy-start.3
  66.8 0.0 copy-start.5
  66.9 3.7 %shard_map.58.high = bf16[16,32,192]{2,1,0:T(8,128)(2,1)S(1)} custom-call(s32[3]{0:T(128)S(1)} %pad_add_fusion.1.place, bf16[4,64,576]{2,1,0:T(8,128)(2,1)S(1)} %bitcast.24, bf16[4,64,576]{2,1,0:T(8,128)(2,1)S(1)} %bitcast.26, bf16[4,64,576]{2,1,0:T(8,128)(2,1)S(1)} %bitcast.28, bf16[4,64,576]{2,1,0:T(8,128)(2,1)S(1)} %bitcast.30), custom_call_target="tpu_custom_call" | custom-call | flops 1610612736 | bytes 1376256 | tf_op jit(solution)/shard_map/pallas_call | solution.py:103
  70.6 4.3 %collective-permute-start.10 = (bf16[16,32,192]{2,1,0:T(8,128)(2,1)S(1)}, bf16[16,32,192]{2,1,0:T(8,128)(2,1)S(1)}, u32[]{:S(2)}, u32[]{:S(2)}) collective-permute-start(bf16[16,32,192]{2,1,0:T(8,128)(2,1)S(1)} %shard_map.58.high), channel_id=1, source_target_pairs={{0,16},{16,32},{32,48},{48,64},{64,80},{80,96},{96,112},{112,128},... | collective-permute-start | bytes 589832 | tf_op jit(solution)/shard_map/ppermute | solution.py:184
  74.9 9.4 %collective-permute-start.11 = (bf16[16,32,192]{2,1,0:T(8,128)(2,1)S(1)}, bf16[16,32,192]{2,1,0:T(8,128)(2,1)S(1)}, u32[]{:S(2)}, u32[]{:S(2)}) collective-permute-start(bf16[16,32,192]{2,1,0:T(8,128)(2,1)S(1)} %shard_map.57.low), channel_id=1, source_target_pairs={{16,0},{32,16},{48,32},{64,48},{80,64},{96,80},{112,96},{128,112},... | collective-permute-start | bytes 589832 | tf_op jit(solution)/shard_map/ppermute | solution.py:184
  84.3 0.0 copy-done.6
  84.3 0.1 pad_add_fusion
  84.4 0.1 dynamic_slice.3.overlap
  84.4 4.5 %collective-permute-done.10.before = bf16[16,32,192]{2,1,0:T(8,128)(2,1)S(1)} collective-permute-done((bf16[16,32,192]{2,1,0:T(8,128)(2,1)S(1)}, bf16[16,32,192]{2,1,0:T(8,128)(2,1)S(1)}, u32[]{:S(2)}, u32[]{:S(2)}) %collective-permute-start.10) | collective-permute-done | bytes 196640 | tf_op jit(solution)/shard_map/ppermute | solution.py:184
  88.9 1.2 %collective-permute-done.11.after = bf16[16,32,192]{2,1,0:T(8,128)(2,1)S(1)} collective-permute-done((bf16[16,32,192]{2,1,0:T(8,128)(2,1)S(1)}, bf16[16,32,192]{2,1,0:T(8,128)(2,1)S(1)}, u32[]{:S(2)}, u32[]{:S(2)}) %collective-permute-start.11) | collective-permute-done | bytes 196640 | tf_op jit(solution)/shard_map/ppermute | solution.py:184
  90.1 0.7 shard_map.59
  90.9 25.9 %all_to_all.5.avg = bf16[16,64,192]{2,1,0:T(8,128)(2,1)S(1)} all-to-all(bf16[16,64,192]{2,1,0:T(8,128)(2,1)S(1)} %shard_map.59), channel_id=1, replica_groups=mesh['ylo'=4,'z'=8,'x'=4,'yhi'=2,'core'=2] {'x','yhi','core'}, dimensions={0} | all-to-all | bytes 786432 | tf_op jit(solution)/shard_map/all_to_all | solution.py:216
  116.7 0.0 copy-done.3
  116.7 0.0 copy-done.5
  116.7 0.9 shard_map.60
Async XLA Ops:
  0.0 44.5 %collective-permute-start.4 = (bf16[576,3072]{1,0:T(8,128)(2,1)}, bf16[576,3072]{1,0:T(8,128)(2,1)S(1)}, u32[]{:S(2)}, u32[]{:S(2)}) collective-permute-start(bf16[576,3072]{1,0:T(8,128)(2,1)} %bitcast.11), channel_id=1, source_target_pairs={{0,1},{1,0},{2,3},{3,2},{4,5},{5,4},{6,7},{7,6},{8,9},{9,8},{10,11... | collective-permute-start | bytes 10616840 | tf_op jit(solution)/shard_map/ppermute | solution.py:179
  1.9 25.4 %collective-permute-start = (bf16[64,3072]{1,0:T(8,128)(2,1)}, bf16[64,3072]{1,0:T(8,128)(2,1)S(1)}, u32[]{:S(2)}, u32[]{:S(2)}) collective-permute-start(bf16[64,3072]{1,0:T(8,128)(2,1)} %bitcast.17), channel_id=1, source_target_pairs={{0,2},{2,0},{1,3},{3,1},{4,6},{6,4},{5,7},{7,5},{8,10},{10,8},{9,1... | collective-permute-start | bytes 1179656 | tf_op jit(solution)/shard_map/ppermute | solution.py:179
  8.8 18.5 %collective-permute-start.1 = (bf16[64,3072]{1,0:T(8,128)(2,1)}, bf16[64,3072]{1,0:T(8,128)(2,1)S(1)}, u32[]{:S(2)}, u32[]{:S(2)}) collective-permute-start(bf16[64,3072]{1,0:T(8,128)(2,1)} %bitcast.18), channel_id=1, source_target_pairs={{0,4},{4,8},{8,12},{12,0},{1,5},{5,9},{9,13},{13,1},{2,6},{6,10},{... | collective-permute-start | bytes 1179656 | tf_op jit(solution)/shard_map/ppermute | solution.py:179
  12.2 20.9 %collective-permute-start.2 = (bf16[64,3072]{1,0:T(8,128)(2,1)}, bf16[64,3072]{1,0:T(8,128)(2,1)S(1)}, u32[]{:S(2)}, u32[]{:S(2)}) collective-permute-start(bf16[64,3072]{1,0:T(8,128)(2,1)} %bitcast.19), channel_id=1, source_target_pairs={{0,12},{4,0},{8,4},{12,8},{1,13},{5,1},{9,5},{13,9},{2,14},{6,2},{... | collective-permute-start | bytes 1179656 | tf_op jit(solution)/shard_map/ppermute | solution.py:179
  15.8 17.2 %collective-permute-start.3 = (bf16[64,3072]{1,0:T(8,128)(2,1)}, bf16[64,3072]{1,0:T(8,128)(2,1)S(1)}, u32[]{:S(2)}, u32[]{:S(2)}) collective-permute-start(bf16[64,3072]{1,0:T(8,128)(2,1)} %bitcast.20), channel_id=1, source_target_pairs={{0,8},{4,12},{8,0},{12,4},{1,9},{5,13},{9,1},{13,5},{2,10},{6,14},... | collective-permute-start | bytes 1179656 | tf_op jit(solution)/shard_map/ppermute | solution.py:179
  33.1 20.7 %collective-permute-start.6 = (bf16[64,3072]{1,0:T(8,128)(2,1)S(1)}, bf16[64,3072]{1,0:T(8,128)(2,1)S(1)}, u32[]{:S(2)}, u32[]{:S(2)}) collective-permute-start(bf16[64,3072]{1,0:T(8,128)(2,1)S(1)} %collective-permute-done.t0), channel_id=1, source_target_pairs={{0,4},{4,8},{8,12},{12,0},{1,5},{5,9},{9,13},{13,1},{2,6},{6,10},{... | collective-permute-start | bytes 1179656 | tf_op jit(solution)/shard_map/ppermute | solution.py:179
  37.7 16.0 %collective-permute-start.7 = (bf16[64,3072]{1,0:T(8,128)(2,1)S(1)}, bf16[64,3072]{1,0:T(8,128)(2,1)S(1)}, u32[]{:S(2)}, u32[]{:S(2)}) collective-permute-start(bf16[64,3072]{1,0:T(8,128)(2,1)S(1)} %collective-permute-done.t0), channel_id=1, source_target_pairs={{0,12},{4,0},{8,4},{12,8},{1,13},{5,1},{9,5},{13,9},{2,14},{6,2},{... | collective-permute-start | bytes 1179656 | tf_op jit(solution)/shard_map/ppermute | solution.py:179
  40.5 15.8 %collective-permute-start.8 = (bf16[64,3072]{1,0:T(8,128)(2,1)S(1)}, bf16[64,3072]{1,0:T(8,128)(2,1)S(1)}, u32[]{:S(2)}, u32[]{:S(2)}) collective-permute-start(bf16[64,3072]{1,0:T(8,128)(2,1)S(1)} %collective-permute-done.t0), channel_id=1, source_target_pairs={{0,8},{4,12},{8,0},{12,4},{1,9},{5,13},{9,1},{13,5},{2,10},{6,14},... | collective-permute-start | bytes 1179656 | tf_op jit(solution)/shard_map/ppermute | solution.py:179
  44.5 2.0 %copy-start = (bf16[3,192,3072]{2,1,0:T(8,128)(2,1)S(1)}, bf16[3,192,3072]{2,1,0:T(8,128)(2,1)}, u32[]{:S(2)}) copy-start(bf16[3,192,3072]{2,1,0:T(8,128)(2,1)} %param.8) | copy-start | bytes 10616836
  46.5 1.0 copy-start.2
  47.5 1.0 copy-start.4
  48.5 7.8 %copy-start.1 = (bf16[3,192,3072]{2,1,0:T(8,128)(2,1)S(1)}, bf16[3,192,3072]{2,1,0:T(8,128)(2,1)}, u32[]{:S(2)}) copy-start(bf16[3,192,3072]{2,1,0:T(8,128)(2,1)} %param.8) | copy-start | bytes 10616836
  51.8 10.0 %collective-permute-start.5 = (bf16[256,576]{1,0:T(8,128)(2,1)S(1)}, bf16[256,576]{1,0:T(8,128)(2,1)S(1)}, u32[]{:S(2)}, u32[]{:S(2)}) collective-permute-start(bf16[256,576]{1,0:T(8,128)(2,1)S(1)} %get-tuple-element.19), channel_id=1, source_target_pairs={{0,1},{1,0},{2,3},{3,2},{4,5},{5,4},{6,7},{7,6},{8,9},{9,8},{10,11... | collective-permute-start | bytes 884744 | tf_op jit(solution)/shard_map/ppermute | solution.py:179
  59.6 3.5 %collective-permute-start.9 = (bf16[256,576]{1,0:T(8,128)(2,1)S(1)}, bf16[256,576]{1,0:T(8,128)(2,1)S(1)}, u32[]{:S(2)}, u32[]{:S(2)}) collective-permute-start(bf16[256,576]{1,0:T(8,128)(2,1)S(1)} %get-tuple-element.22), channel_id=1, source_target_pairs={{0,1},{1,0},{2,3},{3,2},{4,5},{5,4},{6,7},{7,6},{8,9},{9,8},{10,11... | collective-permute-start | bytes 884744 | tf_op jit(solution)/shard_map/ppermute | solution.py:179
  66.8 17.5 %copy-start.6 = (s32[32]{0:T(128)S(1)}, s32[32]{0:T(128)}, u32[]{:S(2)}) copy-start(s32[32]{0:T(128)} %param.9) | copy-start | bytes 388
  66.8 49.9 %copy-start.3 = (f32[8,3,3072]{2,0,1:T(8,128)S(1)}, f32[8,3,3072]{2,0,1:T(8,128)}, u32[]{:S(2)}) copy-start(f32[8,3,3072]{2,0,1:T(8,128)} %param.7) | copy-start | bytes 884740
  66.8 49.9 %copy-start.5 = (bf16[1,8,8,3072]{3,2,1,0:T(8,128)(2,1)S(1)}, bf16[1,8,8,3072]{3,2,1,0:T(8,128)(2,1)}, u32[]{:S(2)}) copy-start(bf16[1,8,8,3072]{3,2,1,0:T(8,128)(2,1)} %param.5) | copy-start | bytes 1179652
  70.6 18.3 %collective-permute-start.10 = (bf16[16,32,192]{2,1,0:T(8,128)(2,1)S(1)}, bf16[16,32,192]{2,1,0:T(8,128)(2,1)S(1)}, u32[]{:S(2)}, u32[]{:S(2)}) collective-permute-start(bf16[16,32,192]{2,1,0:T(8,128)(2,1)S(1)} %shard_map.58.high), channel_id=1, source_target_pairs={{0,16},{16,32},{32,48},{48,64},{64,80},{80,96},{96,112},{112,128},... | collective-permute-start | bytes 589832 | tf_op jit(solution)/shard_map/ppermute | solution.py:184
  74.9 15.2 %collective-permute-start.11 = (bf16[16,32,192]{2,1,0:T(8,128)(2,1)S(1)}, bf16[16,32,192]{2,1,0:T(8,128)(2,1)S(1)}, u32[]{:S(2)}, u32[]{:S(2)}) collective-permute-start(bf16[16,32,192]{2,1,0:T(8,128)(2,1)S(1)} %shard_map.57.low), channel_id=1, source_target_pairs={{16,0},{32,16},{48,32},{64,48},{80,64},{96,80},{112,96},{128,112},... | collective-permute-start | bytes 589832 | tf_op jit(solution)/shard_map/ppermute | solution.py:184

commit v3 on v2

v3 whole, which is shorter than its diff:
```python
import functools

import jax
import jax.numpy as jnp
from jax import lax
from jax.experimental import pallas as pl
from jax.experimental.pallas import tpu as pltpu
from jax.sharding import Mesh
from jax.sharding import PartitionSpec as P

HEAD_DIM = 64
OMAX = 3
NX, NY, NC = 4, 2, 2
MIB = 1 << 20
OFFSETS = (0, 3, 1, 2)


def cost(flops, inputs, outputs, transcendentals=0):
    size = sum(a.size * a.dtype.itemsize for a in (*inputs, *outputs))
    return pl.CostEstimate(flops=flops, bytes_accessed=size, transcendentals=transcendentals)


def project_kernel(blocks, pid, *refs):
    tokens, mod_ref, rest = refs[:blocks], refs[blocks], refs[blocks + 1 :]
    row = pl.ds(pid[0], 1)
    shift = mod_ref[0, row, :]
    scale = 1.0 + mod_ref[1, row, :]
    parts = []
    for t in tokens:
        for i in range(0, t.shape[0], 64):
            xf = t[i : i + 64].astype(jnp.float32)
            mean = jnp.mean(xf, axis=-1, keepdims=True)
            xc = xf - mean
            var = jnp.mean(xc * xc, axis=-1, keepdims=True)
            parts.append((xc * lax.rsqrt(var + 1e-06) * scale + shift).astype(jnp.bfloat16))
    normed = jnp.concatenate(parts, axis=0)
    half = len(rest) // 2
    for w, o in zip(rest[:half], rest[half:]):
        o[...] = lax.dot_general(
            normed, w[...], (((1,), (1,)), ((), ())), preferred_element_type=jnp.float32
        ).astype(jnp.bfloat16)


def project(pid, blocks, modulation, weights):
    rows = sum(b.shape[0] for b in blocks)
    feats, width = weights[0].shape
    full = pl.BlockSpec(memory_space=pltpu.VMEM)
    shapes = [jax.ShapeDtypeStruct((rows, feats), jnp.bfloat16)] * len(weights)
    return pl.pallas_call(
        functools.partial(project_kernel, len(blocks)),
        in_specs=[pl.BlockSpec(memory_space=pltpu.SMEM)] + [full] * (len(blocks) + 1 + len(weights)),
        out_specs=[full] * len(weights),
        out_shape=shapes,
        cost_estimate=cost(2 * rows * feats * width * len(weights), (*blocks, *weights), shapes),
        compiler_params=pltpu.CompilerParams(vmem_limit_bytes=24 * MIB),
    )(pid, *blocks, modulation, *weights)


def attend_kernel(first, count, place, near, far, swapped, out):
    groups = (near, far, swapped)
    width = near.shape[2] // 3
    heads = width // HEAD_DIM

    def columns(refs, part, h, rows=slice(None)):
        a = part * width + h * HEAD_DIM
        taken = [g[:, rows, a : a + HEAD_DIM] for g in refs]
        return jnp.concatenate([t.reshape(-1, HEAD_DIM) for t in taken], axis=0)

    kk, vv = [], []
    for h in range(heads):
        kk.append(columns(groups, 1, h))
        v = columns(groups, 2, h)
        lane = lax.broadcasted_iota(jnp.int32, (v.shape[0], 2 * HEAD_DIM), 1)
        vv.append(jnp.where(lane == HEAD_DIM, jnp.ones_like(v[:1, :1]), jnp.concatenate([v, jnp.zeros_like(v)], axis=1)))
    for refs in ((near,), (far, swapped)):
        results = []
        for h in range(heads):
            q = columns(refs, 0, h, slice(first, first + count))
            s = lax.dot_general(q, kk[h], (((1,), (1,)), ((), ())), preferred_element_type=jnp.float32)
            top = jnp.max(s, axis=-1, keepdims=True)
            p = jnp.exp((s - top) * (HEAD_DIM**-0.5)).astype(jnp.bfloat16)
            o = lax.dot_general(p, vv[h], (((1,), (0,)), ((), ())), preferred_element_type=jnp.float32)
            results.append(o[:, :HEAD_DIM] / o[:, HEAD_DIM : HEAD_DIM + 1])
        both = jnp.concatenate(results, axis=1).astype(jnp.bfloat16).reshape(-1, count, width)
        for n in range(both.shape[0]):
            if refs[0] is near:
                x, y, c = n // NC, place[1], n % NC
            else:
                x = lax.rem(place[0] + OFFSETS[n % NX], NX)
                y = 1 - place[1]
                c = place[2] if n < NX else 1 - place[2]
            out[(x * NY + y) * NC + c] = both[n]


def attend(first, count, place, groups):
    blocks = sum(g.shape[0] for g in groups)
    _, rows, feats = groups[0].shape
    full = pl.BlockSpec(memory_space=pltpu.VMEM)
    shape = jax.ShapeDtypeStruct((blocks, count, feats // 3), jnp.bfloat16)
    scores = blocks * blocks * count * rows * (feats // 3 // HEAD_DIM)
    return pl.pallas_call(
        functools.partial(attend_kernel, first, count),
        in_specs=[pl.BlockSpec(memory_space=pltpu.SMEM)] + [full] * 3,
        out_specs=full,
        out_shape=shape,
        cost_estimate=cost(4 * HEAD_DIM * scores, groups, (shape,), scores),
        compiler_params=pltpu.CompilerParams(vmem_limit_bytes=24 * MIB),
    )(place, *groups)


def join(mine, shared, takes):
    part = jnp.zeros_like(mine)
    for take, other in takes:
        part = jnp.where(take, other, part)
    return (mine + part) * jnp.where(shared, 0.5, 1.0)


def average_high_kernel(overlap, high, after, out):
    half = high.shape[1]
    each = 8
    count = half // each
    ov_next = overlap[1]
    mine = high[...].astype(jnp.float32)
    nxt = after[...].astype(jnp.float32)
    done = []
    for i in range(count):
        cur = mine[:, i * each : (i + 1) * each]
        if i >= count - OMAX:
            takes = [(j == i - count + ov_next, nxt[:, j * each : (j + 1) * each]) for j in range(OMAX)]
            cur = join(cur, i >= count - ov_next, takes)
        done.append(cur)
    out[...] = jnp.concatenate(done, axis=1).astype(jnp.bfloat16)


def average_low_kernel(overlap, low, before, high, out):
    half = low.shape[1]
    each = 8
    count = half // each
    ov_prev = overlap[0]
    mine = low[...].astype(jnp.float32)
    prev = before[...].astype(jnp.float32)
    done = []
    for i in range(count):
        cur = mine[:, i * each : (i + 1) * each]
        if i < OMAX:
            takes = [
                (j == OMAX - ov_prev + i, prev[:, (count - OMAX + j) * each : (count - OMAX + j + 1) * each])
                for j in range(OMAX)
            ]
            cur = join(cur, i < ov_prev, [((i < ov_prev) & t, o) for t, o in takes])
        done.append(cur)
    out[:, :half, :] = jnp.concatenate(done, axis=1).astype(jnp.bfloat16)
    out[:, half:, :] = high[...]


def average(kernel, overlap, parts, rows):
    full = pl.BlockSpec(memory_space=pltpu.VMEM)
    blocks, _, width = parts[0].shape
    shape = jax.ShapeDtypeStruct((blocks, rows, width), jnp.bfloat16)
    return pl.pallas_call(
        kernel,
        in_specs=[pl.BlockSpec(memory_space=pltpu.SMEM)] + [full] * len(parts),
        out_specs=full,
        out_shape=shape,
        cost_estimate=cost(8 * blocks * rows * width, parts, (shape,)),
        compiler_params=pltpu.CompilerParams(vmem_limit_bytes=16 * MIB),
    )(overlap, *parts)


def blend_kernel(pid, lat, mod_ref, avg, out):
    blocks, _, width = avg.shape
    gate = mod_ref[2, pl.ds(pid[0], 1), :]
    for b in range(0, blocks, 2):
        cols = slice(b * width, (b + 2) * width)
        a = jnp.concatenate([avg[b].astype(jnp.float32), avg[b + 1].astype(jnp.float32)], axis=1)
        out[:, cols] = (lat[:, cols].astype(jnp.float32) + gate[:, cols] * a).astype(jnp.bfloat16)


def blend(pid, lat, modulation, avg):
    full = pl.BlockSpec(memory_space=pltpu.VMEM)
    return pl.pallas_call(
        blend_kernel,
        in_specs=[pl.BlockSpec(memory_space=pltpu.SMEM)] + [full] * 3,
        out_specs=full,
        out_shape=jax.ShapeDtypeStruct(lat.shape, jnp.bfloat16),
        compiler_params=pltpu.CompilerParams(vmem_limit_bytes=16 * MIB),
    )(pid, lat, modulation, avg)


def around(value, axis, by):
    n = lax.axis_size(axis)
    return lax.ppermute(value, axis, [(i, (i + by) % n) for i in range(n)])


def along(value, by):
    n = lax.axis_size(("ylo", "z"))
    return lax.ppermute(value, ("ylo", "z"), [(i, i + by) for i in range(n) if 0 <= i + by < n])


def shards(latents, prompt_ids, modulation, w_qkv, intersection):
    _, frames, patches, width = latents.shape
    rows = frames * patches
    mine = latents.reshape(rows, width)
    wa = w_qkv.reshape(-1, width)
    place = jnp.stack([lax.axis_index("x"), lax.axis_index("yhi"), lax.axis_index("core")]).astype(jnp.int32)

    modulation = jnp.transpose(modulation, (1, 0, 2))
    window = lax.axis_index(("ylo", "z"))
    padded = jnp.concatenate([intersection, jnp.zeros((1,), jnp.int32)])
    overlap = lax.dynamic_slice(padded, (window,), (2,))

    near = lax.all_gather(mine, ("x", "core"), axis=0, tiled=True)
    other = around(mine, "yhi", 1)
    wb = around(wa, "core", 1)
    far = [other] + [around(other, "x", by) for by in (1, 3, 2)]

    own, give = project(prompt_ids, far, modulation, [wa, wb])
    got = around(give, "core", 1)
    (home,) = project(prompt_ids, [near], modulation, [wa])
    groups = [g.reshape(-1, rows, g.shape[-1]) for g in (home, own, got)]

    half = rows // 2
    low = attend(0, half, place, groups)
    after = along(low, -1)
    high = attend(half, half, place, groups)
    before = along(high, 1)

    avg = average(average_high_kernel, overlap, (high, after), half)
    avg = average(average_low_kernel, overlap, (low, before, avg), rows)
    avg = lax.all_to_all(avg, ("x", "yhi", "core"), 0, 0)
    return blend(prompt_ids, mine, modulation, avg).reshape(latents.shape)


def solution(mesh):
    fine = Mesh(mesh.devices.reshape(4, 8, NX, NY, NC), ("ylo", "z", "x", "yhi", "core"))
    win, head = ("ylo", "z"), ("x", "yhi", "core")
    in_specs = (P(win, None, head, None), P(win), P(), P(None, head, None), P())
    out_specs = P(win, None, head, None)
    return jax.shard_map(shards, mesh=fine, in_specs=in_specs, out_specs=out_specs, check_vma=False)
```

time: 118 us -> 142 us (1.20)
  the two profiles are of different devices: /device:TPU:8 before, /device:TPU:57 now
where the time goes in v3:
time: 142 us; the launch traced here: 141 us
  waiting for transfers between devices  46.7 us (33%)
  starting transfers between devices  29.7 us (21%)
  blocking collectives  25 us (18%)
  Pallas kernels  18.8 us (13%)
  between operations  14.2 us (10%)
  local copies, waits for them, and re-layouts  6.64 us (5%)
    ppermute x6, waiting for transfers between devices, around(): return lax.ppermute(value, axis, [(i, (i + by) % n) for i in range(n)])  37.1 us
    all_to_all x1, blocking collectives, shards(): avg = lax.all_to_all(avg, ('x', 'yhi', 'core'), 0, 0)  25 us
    ppermute x6, starting transfers between devices, around(): return lax.ppermute(value, axis, [(i, (i + by) % n) for i in range(n)])  19.6 us
    ppermute x2, starting transfers between devices, along(): lax.ppermute(value, ('ylo', 'z'), [(i, i + by) for i in range(n) if 0 <=...  10 us
    ppermute x2, waiting for transfers between devices, along(): lax.ppermute(value, ('ylo', 'z'), [(i, i + by) for i in range(n) if 0 <=...  8.86 us
    pallas_call x2, Pallas kernels, attend(): pl.pallas_call(functools.partial(attend_kernel, first, count), in_specs=[...  8.35 us
    pallas_call x2, Pallas kernels, project(): pl.pallas_call(functools.partial(project_kernel, len(blocks)), in_specs=[...  8.25 us
    unnamed x20, local copies, waits for them, and re-layouts  6.56 us
  transfers between devices with their start and end apart: 9, of which 4 were waited for; matrix products, arithmetic and copies ran while one was open for 0% of the time, Pallas kernels for 9%

profile of v3, /device:TPU:57, one launch (start us, length us, event | category | flops | bytes accessed | tf_op | source)
XLA Modules:
  0.0 141.2 jit_solution(15679979679096807537)
XLA Ops:
  6.5 0.0 all-gather.2.cloned.1.call-start
  6.5 0.7 all-gather.2.cloned.1.call-update
  7.3 2.6 %collective-permute-start.4 = (bf16[576,3072]{1,0:T(8,128)(2,1)}, bf16[576,3072]{1,0:T(8,128)(2,1)S(1)}, u32[]{:S(2)}, u32[]{:S(2)}) collective-permute-start(bf16[576,3072]{1,0:T(8,128)(2,1)} %bitcast.10), channel_id=1, source_target_pairs={{0,1},{1,0},{2,3},{3,2},{4,5},{5,4},{6,7},{7,6},{8,9},{9,8},{10,11... | collective-permute-start | bytes 10616840 | tf_op jit(solution)/shard_map/ppermute | solution.py:192
  9.8 4.4 %collective-permute-start = (bf16[64,3072]{1,0:T(8,128)(2,1)}, bf16[64,3072]{1,0:T(8,128)(2,1)S(1)}, u32[]{:S(2)}, u32[]{:S(2)}) collective-permute-start(bf16[64,3072]{1,0:T(8,128)(2,1)} %bitcast.17), channel_id=1, source_target_pairs={{0,2},{2,0},{1,3},{3,1},{4,6},{6,4},{5,7},{7,5},{8,10},{10,8},{9,1... | collective-permute-start | bytes 1179656 | tf_op jit(solution)/shard_map/ppermute | solution.py:192
  14.3 20.8 %collective-permute-done.refs_0_ = bf16[64,3072]{1,0:T(8,128)(2,1)S(1)} collective-permute-done((bf16[64,3072]{1,0:T(8,128)(2,1)}, bf16[64,3072]{1,0:T(8,128)(2,1)S(1)}, u32[]{:S(2)}, u32[]{:S(2)}) %collective-permute-start) | collective-permute-done | bytes 393248 | tf_op jit(solution)/shard_map/ppermute | solution.py:192
  35.1 3.1 %collective-permute-start.1 = (bf16[64,3072]{1,0:T(8,128)(2,1)S(1)}, bf16[64,3072]{1,0:T(8,128)(2,1)S(1)}, u32[]{:S(2)}, u32[]{:S(2)}) collective-permute-start(bf16[64,3072]{1,0:T(8,128)(2,1)S(1)} %collective-permute-done.refs_0_), channel_id=1, source_target_pairs={{0,4},{4,8},{8,12},{12,0},{1,5},{5,9},{9,13},{13,1},{2,6},{6,10},{... | collective-permute-start | bytes 1179656 | tf_op jit(solution)/shard_map/ppermute | solution.py:192
  38.2 3.4 %collective-permute-start.2 = (bf16[64,3072]{1,0:T(8,128)(2,1)S(1)}, bf16[64,3072]{1,0:T(8,128)(2,1)S(1)}, u32[]{:S(2)}, u32[]{:S(2)}) collective-permute-start(bf16[64,3072]{1,0:T(8,128)(2,1)S(1)} %collective-permute-done.refs_0_), channel_id=1, source_target_pairs={{0,12},{4,0},{8,4},{12,8},{1,13},{5,1},{9,5},{13,9},{2,14},{6,2},{... | collective-permute-start | bytes 1179656 | tf_op jit(solution)/shard_map/ppermute | solution.py:192
  41.6 3.4 %collective-permute-start.3 = (bf16[64,3072]{1,0:T(8,128)(2,1)S(1)}, bf16[64,3072]{1,0:T(8,128)(2,1)S(1)}, u32[]{:S(2)}, u32[]{:S(2)}) collective-permute-start(bf16[64,3072]{1,0:T(8,128)(2,1)S(1)} %collective-permute-done.refs_0_), channel_id=1, source_target_pairs={{0,8},{4,12},{8,0},{12,4},{1,9},{5,13},{9,1},{13,5},{2,10},{6,14},... | collective-permute-start | bytes 1179656 | tf_op jit(solution)/shard_map/ppermute | solution.py:192
  45.7 7.6 %collective-permute-done.1.refs_1_ = bf16[64,3072]{1,0:T(8,128)(2,1)S(1)} collective-permute-done((bf16[64,3072]{1,0:T(8,128)(2,1)S(1)}, bf16[64,3072]{1,0:T(8,128)(2,1)S(1)}, u32[]{:S(2)}, u32[]{:S(2)}) %collective-permute-start.1) | collective-permute-done | bytes 393248 | tf_op jit(solution)/shard_map/ppermute | solution.py:192
  53.3 0.0 collective-permute-done.2.refs_2_
  53.3 8.7 %collective-permute-done.3.refs_3_ = bf16[64,3072]{1,0:T(8,128)(2,1)S(1)} collective-permute-done((bf16[64,3072]{1,0:T(8,128)(2,1)S(1)}, bf16[64,3072]{1,0:T(8,128)(2,1)S(1)}, u32[]{:S(2)}, u32[]{:S(2)}) %collective-permute-start.3) | collective-permute-done | bytes 393248 | tf_op jit(solution)/shard_map/ppermute | solution.py:192
  62.0 0.0 collective-permute-done.4.refs_6_
  62.0 0.0 copy-start
  62.0 2.0 %copy-done = bf16[3,192,3072]{2,1,0:T(8,128)(2,1)S(1)} copy-done((bf16[3,192,3072]{2,1,0:T(8,128)(2,1)S(1)}, bf16[3,192,3072]{2,1,0:T(8,128)(2,1)}, u32[]{:S(2)}) %copy-start) | copy-done | bytes 3538968
  64.0 0.0 copy-start.3
  64.0 1.0 copy-done.3
  65.0 0.0 copy-start.1
  65.0 4.1 %shard_map.56 = (bf16[256,576]{1,0:T(8,128)(2,1)S(1)}, bf16[256,576]{1,0:T(8,128)(2,1)}) custom-call(s32[1]{0:T(128)S(6)} %copy.6.pid, bf16[64,3072]{1,0:T(8,128)(2,1)S(1)} %collective-permute-done.refs_0_, bf16[64,3072]{1,0:T(8,128)(2,1)S(1)} %collective-permute-done.1.refs_1_, bf16[64,3072]{1,0:T(8,128)(2,1)S(1)} %collective-permute-done.2.refs_2_, ...), custom_call_target="tpu_custom_call" | custom-call | flops 1811939328 | bytes 9240576 | tf_op jit(solution)/shard_map/pallas_call | solution.py:49
  69.0 0.0 copy-start.7
  69.0 0.7 copy-done.7
  69.8 2.7 %collective-permute-start.5 = (bf16[256,576]{1,0:T(8,128)(2,1)}, bf16[256,576]{1,0:T(8,128)(2,1)}, u32[]{:S(2)}, u32[]{:S(2)}) collective-permute-start(bf16[256,576]{1,0:T(8,128)(2,1)} %get-tuple-element.8), channel_id=1, source_target_pairs={{0,1},{1,0},{2,3},{3,2},{4,5},{5,4},{6,7},{7,6},{8,9},{9,8},{10,11... | collective-permute-start | bytes 884744 | tf_op jit(solution)/shard_map/ppermute | solution.py:192
  72.5 0.1 pad_add_fusion.1.place
  72.6 0.0 all-gather.2.cloned.1.call-done.refs_0_
  72.6 0.0 copy-done.1
  72.6 0.0 copy-start.2
  72.6 1.9 %copy-done.2 = bf16[512,3072]{1,0:T(8,128)(2,1)S(1)} copy-done((bf16[512,3072]{1,0:T(8,128)(2,1)S(1)}, bf16[512,3072]{1,0:T(8,128)(2,1)}, u32[]{:S(2)}) %copy-start.2) | copy-done | bytes 3145752
  74.5 1.0 copy-done.4
  75.4 4.2 %shard_map.55 = bf16[512,576]{1,0:T(8,128)(2,1)S(1)} custom-call(s32[1]{0:T(128)S(6)} %copy.6.pid, bf16[512,3072]{1,0:T(8,128)(2,1)S(1)} %copy-done.2, f32[3,8,3072]{2,1,0:T(8,128)S(1)} %bitcast.14, bf16[576,3072]{1,0:T(8,128)(2,1)S(1)} %bitcast.12), custom_call_target="tpu_custom_call" | custom-call | flops 1811939328 | bytes 7274496 | tf_op jit(solution)/shard_map/pallas_call | solution.py:49
  79.6 0.0 copy-start.9
  79.6 0.0 collective-permute-done.5
  79.6 0.0 copy-done.8
  79.6 4.2 %shard_map.57.low = bf16[16,32,192]{2,1,0:T(8,128)(2,1)S(1)} custom-call(s32[3]{0:T(128)S(1)} %pad_add_fusion.1.place, bf16[8,64,576]{2,1,0:T(8,128)(2,1)S(1)} %bitcast.19, bf16[4,64,576]{2,1,0:T(8,128)(2,1)S(1)} %bitcast.21, bf16[4,64,576]{2,1,0:T(8,128)(2,1)} %bitcast.8.swapped), custom_call_target="tpu_custom_call" | custom-call | flops 402653184 | bytes 1376256 | tf_op jit(solution)/shard_map/pallas_call | solution.py:101
  83.8 0.0 copy-start.5
  83.8 0.0 copy-start.6
  83.8 8.1 %collective-permute-start.7 = (bf16[16,32,192]{2,1,0:T(8,128)(2,1)S(1)}, bf16[16,32,192]{2,1,0:T(8,128)(2,1)S(1)}, u32[]{:S(2)}, u32[]{:S(2)}) collective-permute-start(bf16[16,32,192]{2,1,0:T(8,128)(2,1)S(1)} %shard_map.57.low), channel_id=1, source_target_pairs={{16,0},{32,16},{48,32},{64,48},{80,64},{96,80},{112,96},{128,112},... | collective-permute-start | bytes 589832 | tf_op jit(solution)/shard_map/ppermute | solution.py:197
  91.9 4.2 %shard_map.58.high = bf16[16,32,192]{2,1,0:T(8,128)(2,1)S(1)} custom-call(s32[3]{0:T(128)S(1)} %pad_add_fusion.1.place, bf16[8,64,576]{2,1,0:T(8,128)(2,1)S(1)} %bitcast.20, bf16[4,64,576]{2,1,0:T(8,128)(2,1)S(1)} %bitcast.22, bf16[4,64,576]{2,1,0:T(8,128)(2,1)} %bitcast.8.swapped), custom_call_target="tpu_custom_call" | custom-call | flops 402653184 | bytes 1376256 | tf_op jit(solution)/shard_map/pallas_call | solution.py:101
  96.1 1.9 %collective-permute-start.6 = (bf16[16,32,192]{2,1,0:T(8,128)(2,1)S(1)}, bf16[16,32,192]{2,1,0:T(8,128)(2,1)S(1)}, u32[]{:S(2)}, u32[]{:S(2)}) collective-permute-start(bf16[16,32,192]{2,1,0:T(8,128)(2,1)S(1)} %shard_map.58.high), channel_id=1, source_target_pairs={{0,16},{16,32},{32,48},{48,64},{64,80},{80,96},{96,112},{112,128},... | collective-permute-start | bytes 589832 | tf_op jit(solution)/shard_map/ppermute | solution.py:197
  98.1 0.0 copy-done.9
  98.1 0.1 pad_add_fusion
  98.1 0.1 dynamic_slice.3.overlap
  98.2 0.0 collective-permute-done.7.after
  98.2 0.6 shard_map.59.high
  98.9 8.9 %collective-permute-done.6.before = bf16[16,32,192]{2,1,0:T(8,128)(2,1)S(1)} collective-permute-done((bf16[16,32,192]{2,1,0:T(8,128)(2,1)S(1)}, bf16[16,32,192]{2,1,0:T(8,128)(2,1)S(1)}, u32[]{:S(2)}, u32[]{:S(2)}) %collective-permute-start.6) | collective-permute-done | bytes 196640 | tf_op jit(solution)/shard_map/ppermute | solution.py:197
  107.7 0.6 shard_map.60
  108.4 25.0 %all_to_all.5.avg = bf16[16,64,192]{2,1,0:T(8,128)(2,1)S(1)} all-to-all(bf16[16,64,192]{2,1,0:T(8,128)(2,1)S(1)} %shard_map.60), channel_id=1, replica_groups=mesh['ylo'=4,'z'=8,'x'=4,'yhi'=2,'core'=2] {'x','yhi','core'}, dimensions={0} | all-to-all | bytes 786432 | tf_op jit(solution)/shard_map/all_to_all | solution.py:230
  133.4 0.0 copy-done.5
  133.4 0.0 copy-done.6
  133.4 0.9 shard_map.61
  (2 shorter events, 0.0 us)
Async XLA Ops:
  6.5 66.0 %all-gather.2.cloned.1.call-start = ((), (), s32[]{:S(2)}) async-start(), calls=%async_computation.1 | async-start | bytes 3538944 | tf_op jit(solution)/shard_map/all_gather | solution.py:212
  7.3 54.8 %collective-permute-start.4 = (bf16[576,3072]{1,0:T(8,128)(2,1)}, bf16[576,3072]{1,0:T(8,128)(2,1)S(1)}, u32[]{:S(2)}, u32[]{:S(2)}) collective-permute-start(bf16[576,3072]{1,0:T(8,128)(2,1)} %bitcast.10), channel_id=1, source_target_pairs={{0,1},{1,0},{2,3},{3,2},{4,5},{5,4},{6,7},{7,6},{8,9},{9,8},{10,11... | collective-permute-start | bytes 10616840 | tf_op jit(solution)/shard_map/ppermute | solution.py:192
  9.8 25.3 %collective-permute-start = (bf16[64,3072]{1,0:T(8,128)(2,1)}, bf16[64,3072]{1,0:T(8,128)(2,1)S(1)}, u32[]{:S(2)}, u32[]{:S(2)}) collective-permute-start(bf16[64,3072]{1,0:T(8,128)(2,1)} %bitcast.17), channel_id=1, source_target_pairs={{0,2},{2,0},{1,3},{3,1},{4,6},{6,4},{5,7},{7,5},{8,10},{10,8},{9,1... | collective-permute-start | bytes 1179656 | tf_op jit(solution)/shard_map/ppermute | solution.py:192
  35.1 18.2 %collective-permute-start.1 = (bf16[64,3072]{1,0:T(8,128)(2,1)S(1)}, bf16[64,3072]{1,0:T(8,128)(2,1)S(1)}, u32[]{:S(2)}, u32[]{:S(2)}) collective-permute-start(bf16[64,3072]{1,0:T(8,128)(2,1)S(1)} %collective-permute-done.refs_0_), channel_id=1, source_target_pairs={{0,4},{4,8},{8,12},{12,0},{1,5},{5,9},{9,13},{13,1},{2,6},{6,10},{... | collective-permute-start | bytes 1179656 | tf_op jit(solution)/shard_map/ppermute | solution.py:192
  38.2 15.1 %collective-permute-start.2 = (bf16[64,3072]{1,0:T(8,128)(2,1)S(1)}, bf16[64,3072]{1,0:T(8,128)(2,1)S(1)}, u32[]{:S(2)}, u32[]{:S(2)}) collective-permute-start(bf16[64,3072]{1,0:T(8,128)(2,1)S(1)} %collective-permute-done.refs_0_), channel_id=1, source_target_pairs={{0,12},{4,0},{8,4},{12,8},{1,13},{5,1},{9,5},{13,9},{2,14},{6,2},{... | collective-permute-start | bytes 1179656 | tf_op jit(solution)/shard_map/ppermute | solution.py:192
  41.6 20.4 %collective-permute-start.3 = (bf16[64,3072]{1,0:T(8,128)(2,1)S(1)}, bf16[64,3072]{1,0:T(8,128)(2,1)S(1)}, u32[]{:S(2)}, u32[]{:S(2)}) collective-permute-start(bf16[64,3072]{1,0:T(8,128)(2,1)S(1)} %collective-permute-done.refs_0_), channel_id=1, source_target_pairs={{0,8},{4,12},{8,0},{12,4},{1,9},{5,13},{9,1},{13,5},{2,10},{6,14},... | collective-permute-start | bytes 1179656 | tf_op jit(solution)/shard_map/ppermute | solution.py:192
  62.0 2.0 %copy-start = (bf16[3,192,3072]{2,1,0:T(8,128)(2,1)S(1)}, bf16[3,192,3072]{2,1,0:T(8,128)(2,1)}, u32[]{:S(2)}) copy-start(bf16[3,192,3072]{2,1,0:T(8,128)(2,1)} %param.8) | copy-start | bytes 10616836
  64.0 1.0 copy-start.3
  65.0 7.6 %copy-start.1 = (bf16[3,192,3072]{2,1,0:T(8,128)(2,1)S(1)}, bf16[3,192,3072]{2,1,0:T(8,128)(2,1)}, u32[]{:S(2)}) copy-start(bf16[3,192,3072]{2,1,0:T(8,128)(2,1)} %param.8) | copy-start | bytes 10616836
  69.0 0.7 copy-start.7
  69.8 9.9 %collective-permute-start.5 = (bf16[256,576]{1,0:T(8,128)(2,1)}, bf16[256,576]{1,0:T(8,128)(2,1)}, u32[]{:S(2)}, u32[]{:S(2)}) collective-permute-start(bf16[256,576]{1,0:T(8,128)(2,1)} %get-tuple-element.8), channel_id=1, source_target_pairs={{0,1},{1,0},{2,3},{3,2},{4,5},{5,4},{6,7},{7,6},{8,9},{9,8},{10,11... | collective-permute-start | bytes 884744 | tf_op jit(solution)/shard_map/ppermute | solution.py:192
  72.6 1.9 %copy-start.2 = (bf16[512,3072]{1,0:T(8,128)(2,1)S(1)}, bf16[512,3072]{1,0:T(8,128)(2,1)}, u32[]{:S(2)}) copy-start(bf16[512,3072]{1,0:T(8,128)(2,1)} %all-gather.2.cloned.1.call-done.refs_0_) | copy-start | bytes 9437188
  74.5 1.0 copy-start.4
  75.4 4.2 %copy-start.8 = (bf16[256,576]{1,0:T(8,128)(2,1)S(1)}, bf16[256,576]{1,0:T(8,128)(2,1)}, u32[]{:S(2)}) copy-start(bf16[256,576]{1,0:T(8,128)(2,1)} %copy-done.7) | copy-start | bytes 884740
  79.6 18.5 %copy-start.9 = (s32[32]{0:T(128)S(1)}, s32[32]{0:T(128)}, u32[]{:S(2)}) copy-start(s32[32]{0:T(128)} %param.9) | copy-start | bytes 388
  83.8 49.6 %copy-start.5 = (f32[8,3,3072]{2,0,1:T(8,128)S(1)}, f32[8,3,3072]{2,0,1:T(8,128)}, u32[]{:S(2)}) copy-start(f32[8,3,3072]{2,0,1:T(8,128)} %param.7) | copy-start | bytes 884740
  83.8 49.6 %copy-start.6 = (bf16[1,8,8,3072]{3,2,1,0:T(8,128)(2,1)S(1)}, bf16[1,8,8,3072]{3,2,1,0:T(8,128)(2,1)}, u32[]{:S(2)}) copy-start(bf16[1,8,8,3072]{3,2,1,0:T(8,128)(2,1)} %param.5) | copy-start | bytes 1179652
  83.8 14.4 %collective-permute-start.7 = (bf16[16,32,192]{2,1,0:T(8,128)(2,1)S(1)}, bf16[16,32,192]{2,1,0:T(8,128)(2,1)S(1)}, u32[]{:S(2)}, u32[]{:S(2)}) collective-permute-start(bf16[16,32,192]{2,1,0:T(8,128)(2,1)S(1)} %shard_map.57.low), channel_id=1, source_target_pairs={{16,0},{32,16},{48,32},{64,48},{80,64},{96,80},{112,96},{128,112},... | collective-permute-start | bytes 589832 | tf_op jit(solution)/shard_map/ppermute | solution.py:197
  96.1 11.6 %collective-permute-start.6 = (bf16[16,32,192]{2,1,0:T(8,128)(2,1)S(1)}, bf16[16,32,192]{2,1,0:T(8,128)(2,1)S(1)}, u32[]{:S(2)}, u32[]{:S(2)}) collective-permute-start(bf16[16,32,192]{2,1,0:T(8,128)(2,1)S(1)} %shard_map.58.high), channel_id=1, source_target_pairs={{0,16},{16,32},{32,48},{48,64},{64,80},{80,96},{96,112},{112,128},... | collective-permute-start | bytes 589832 | tf_op jit(solution)/shard_map/ppermute | solution.py:197
Sparse Core Ops, SparseCore 0:
  9.5 41.7 all-gather.1

commit v4 on v3

--- a/solution.py
+++ b/solution.py
@@ -56,9 +56,9 @@
     )(pid, *blocks, modulation, *weights)
 
 
-def attend_kernel(first, count, place, near, far, swapped, out):
-    groups = (near, far, swapped)
-    width = near.shape[2] // 3
+def attend_kernel(first, count, place, *refs):
+    groups, out = refs[:-1], refs[-1]
+    width = groups[0].shape[2] // 3
     heads = width // HEAD_DIM
 
     def columns(refs, part, h, rows=slice(None)):
@@ -72,10 +72,10 @@
         v = columns(groups, 2, h)
         lane = lax.broadcasted_iota(jnp.int32, (v.shape[0], 2 * HEAD_DIM), 1)
         vv.append(jnp.where(lane == HEAD_DIM, jnp.ones_like(v[:1, :1]), jnp.concatenate([v, jnp.zeros_like(v)], axis=1)))
-    for refs in ((near,), (far, swapped)):
+    for pair in range(0, len(groups), 2):
         results = []
         for h in range(heads):
-            q = columns(refs, 0, h, slice(first, first + count))
+            q = columns(groups[pair : pair + 2], 0, h, slice(first, first + count))
             s = lax.dot_general(q, kk[h], (((1,), (1,)), ((), ())), preferred_element_type=jnp.float32)
             top = jnp.max(s, axis=-1, keepdims=True)
             p = jnp.exp((s - top) * (HEAD_DIM**-0.5)).astype(jnp.bfloat16)
@@ -83,12 +83,9 @@
             results.append(o[:, :HEAD_DIM] / o[:, HEAD_DIM : HEAD_DIM + 1])
         both = jnp.concatenate(results, axis=1).astype(jnp.bfloat16).reshape(-1, count, width)
         for n in range(both.shape[0]):
-            if refs[0] is near:
-                x, y, c = n // NC, place[1], n % NC
-            else:
-                x = lax.rem(place[0] + OFFSETS[n % NX], NX)
-                y = 1 - place[1]
-                c = place[2] if n < NX else 1 - place[2]
+            x = lax.rem(place[0] + OFFSETS[n % NX], NX)
+            y = place[1] if pair == 0 else 1 - place[1]
+            c = place[2] if n < NX else 1 - place[2]
             out[(x * NY + y) * NC + c] = both[n]
 
 
@@ -100,7 +97,7 @@
     scores = blocks * blocks * count * rows * (feats // 3 // HEAD_DIM)
     return pl.pallas_call(
         functools.partial(attend_kernel, first, count),
-        in_specs=[pl.BlockSpec(memory_space=pltpu.SMEM)] + [full] * 3,
+        in_specs=[pl.BlockSpec(memory_space=pltpu.SMEM)] + [full] * len(groups),
         out_specs=full,
         out_shape=shape,
         cost_estimate=cost(4 * HEAD_DIM * scores, groups, (shape,), scores),
@@ -209,15 +206,17 @@
     padded = jnp.concatenate([intersection, jnp.zeros((1,), jnp.int32)])
     overlap = lax.dynamic_slice(padded, (window,), (2,))
 
-    near = lax.all_gather(mine, ("x", "core"), axis=0, tiled=True)
     other = around(mine, "yhi", 1)
+    near = [mine] + [around(mine, "x", by) for by in (1, 3, 2)]
     wb = around(wa, "core", 1)
+    other, *near = lax.optimization_barrier((other, *near))
     far = [other] + [around(other, "x", by) for by in (1, 3, 2)]
 
-    own, give = project(prompt_ids, far, modulation, [wa, wb])
-    got = around(give, "core", 1)
-    (home,) = project(prompt_ids, [near], modulation, [wa])
-    groups = [g.reshape(-1, rows, g.shape[-1]) for g in (home, own, got)]
+    groups = []
+    for blocks in (near, far):
+        own, give = project(prompt_ids, blocks, modulation, [wa, wb])
+        groups += [own, around(give, "core", 1)]
+    groups = [g.reshape(-1, rows, g.shape[-1]) for g in groups]
 
     half = rows // 2
     low = attend(0, half, place, groups)

time: 142 us -> 123 us (0.87)
  the two profiles are of different devices: /device:TPU:57 before, /device:TPU:8 now
where the time goes in v4:
time: 123 us; the launch traced here: 122 us
  starting transfers between devices  48.1 us (39%)
  waiting for transfers between devices  26.8 us (22%)
  blocking collectives  25.9 us (21%)
  Pallas kernels  16.4 us (13%)
  local copies, waits for them, and re-layouts  4.05 us (3%)
    ppermute x10, starting transfers between devices, around(): return lax.ppermute(value, axis, [(i, (i + by) % n) for i in range(n)])  34.1 us
    all_to_all x1, blocking collectives, shards(): avg = lax.all_to_all(avg, ('x', 'yhi', 'core'), 0, 0)  25.9 us
    ppermute x10, waiting for transfers between devices, around(): return lax.ppermute(value, axis, [(i, (i + by) % n) for i in range(n)])  17.5 us
    ppermute x2, starting transfers between devices, along(): lax.ppermute(value, ('ylo', 'z'), [(i, i + by) for i in range(n) if 0 <=...  14 us
    ppermute x2, waiting for transfers between devices, along(): lax.ppermute(value, ('ylo', 'z'), [(i, i + by) for i in range(n) if 0 <=...  9.32 us
    pallas_call x2, Pallas kernels, attend(): pl.pallas_call(functools.partial(attend_kernel, first, count), in_specs=[...  7.46 us
    pallas_call x2, Pallas kernels, project(): pl.pallas_call(functools.partial(project_kernel, len(blocks)), in_specs=[...  6.67 us
    unnamed x14, local copies, waits for them, and re-layouts  3.97 us
  transfers between devices with their start and end apart: 12, of which 5 were waited for; matrix products, arithmetic and copies ran while one was open for 0% of the time, Pallas kernels for 9%

profile of v4, /device:TPU:8, one launch (start us, length us, event | category | flops | bytes accessed | tf_op | source)
XLA Modules:
  0.0 122.2 jit_solution(5594932612432325215)
XLA Ops:
  0.0 1.9 %collective-permute-start.4 = (bf16[576,3072]{1,0:T(8,128)(2,1)}, bf16[576,3072]{1,0:T(8,128)(2,1)S(1)}, u32[]{:S(2)}, u32[]{:S(2)}) collective-permute-start(bf16[576,3072]{1,0:T(8,128)(2,1)} %bitcast.11), channel_id=1, source_target_pairs={{0,1},{1,0},{2,3},{3,2},{4,5},{5,4},{6,7},{7,6},{8,9},{9,8},{10,11... | collective-permute-start | bytes 10616840 | tf_op jit(solution)/shard_map/ppermute | solution.py:189
  1.9 6.8 %collective-permute-start = (bf16[64,3072]{1,0:T(8,128)(2,1)}, bf16[64,3072]{1,0:T(8,128)(2,1)S(1)}, u32[]{:S(2)}, u32[]{:S(2)}) collective-permute-start(bf16[64,3072]{1,0:T(8,128)(2,1)} %bitcast.17), channel_id=1, source_target_pairs={{0,2},{2,0},{1,3},{3,1},{4,6},{6,4},{5,7},{7,5},{8,10},{10,8},{9,1... | collective-permute-start | bytes 1179656 | tf_op jit(solution)/shard_map/ppermute | solution.py:189
  8.8 3.4 %collective-permute-start.1 = (bf16[64,3072]{1,0:T(8,128)(2,1)}, bf16[64,3072]{1,0:T(8,128)(2,1)S(1)}, u32[]{:S(2)}, u32[]{:S(2)}) collective-permute-start(bf16[64,3072]{1,0:T(8,128)(2,1)} %bitcast.18), channel_id=1, source_target_pairs={{0,4},{4,8},{8,12},{12,0},{1,5},{5,9},{9,13},{13,1},{2,6},{6,10},{... | collective-permute-start | bytes 1179656 | tf_op jit(solution)/shard_map/ppermute | solution.py:189
  12.2 3.7 %collective-permute-start.2 = (bf16[64,3072]{1,0:T(8,128)(2,1)}, bf16[64,3072]{1,0:T(8,128)(2,1)S(1)}, u32[]{:S(2)}, u32[]{:S(2)}) collective-permute-start(bf16[64,3072]{1,0:T(8,128)(2,1)} %bitcast.19), channel_id=1, source_target_pairs={{0,12},{4,0},{8,4},{12,8},{1,13},{5,1},{9,5},{13,9},{2,14},{6,2},{... | collective-permute-start | bytes 1179656 | tf_op jit(solution)/shard_map/ppermute | solution.py:189
  15.8 3.7 %collective-permute-start.3 = (bf16[64,3072]{1,0:T(8,128)(2,1)}, bf16[64,3072]{1,0:T(8,128)(2,1)S(1)}, u32[]{:S(2)}, u32[]{:S(2)}) collective-permute-start(bf16[64,3072]{1,0:T(8,128)(2,1)} %bitcast.20), channel_id=1, source_target_pairs={{0,8},{4,12},{8,0},{12,4},{1,9},{5,13},{9,1},{13,5},{2,10},{6,14},... | collective-permute-start | bytes 1179656 | tf_op jit(solution)/shard_map/ppermute | solution.py:189
  19.6 7.7 %collective-permute-done.refs_0_ = bf16[64,3072]{1,0:T(8,128)(2,1)S(1)} collective-permute-done((bf16[64,3072]{1,0:T(8,128)(2,1)}, bf16[64,3072]{1,0:T(8,128)(2,1)S(1)}, u32[]{:S(2)}, u32[]{:S(2)}) %collective-permute-start) | collective-permute-done | bytes 393248 | tf_op jit(solution)/shard_map/ppermute | solution.py:189
  27.3 0.0 collective-permute-done.1.refs_1_
  27.3 5.8 %collective-permute-done.2.refs_2_ = bf16[64,3072]{1,0:T(8,128)(2,1)S(1)} collective-permute-done((bf16[64,3072]{1,0:T(8,128)(2,1)}, bf16[64,3072]{1,0:T(8,128)(2,1)S(1)}, u32[]{:S(2)}, u32[]{:S(2)}) %collective-permute-start.2) | collective-permute-done | bytes 393248 | tf_op jit(solution)/shard_map/ppermute | solution.py:189
  33.1 0.0 collective-permute-done.3.refs_3_
  33.1 4.6 %collective-permute-start.6 = (bf16[64,3072]{1,0:T(8,128)(2,1)S(1)}, bf16[64,3072]{1,0:T(8,128)(2,1)S(1)}, u32[]{:S(2)}, u32[]{:S(2)}) collective-permute-start(bf16[64,3072]{1,0:T(8,128)(2,1)S(1)} %collective-permute-done.refs_0_), channel_id=1, source_target_pairs={{0,4},{4,8},{8,12},{12,0},{1,5},{5,9},{9,13},{13,1},{2,6},{6,10},{... | collective-permute-start | bytes 1179656 | tf_op jit(solution)/shard_map/ppermute | solution.py:189
  37.7 2.8 %collective-permute-start.7 = (bf16[64,3072]{1,0:T(8,128)(2,1)S(1)}, bf16[64,3072]{1,0:T(8,128)(2,1)S(1)}, u32[]{:S(2)}, u32[]{:S(2)}) collective-permute-start(bf16[64,3072]{1,0:T(8,128)(2,1)S(1)} %collective-permute-done.refs_0_), channel_id=1, source_target_pairs={{0,12},{4,0},{8,4},{12,8},{1,13},{5,1},{9,5},{13,9},{2,14},{6,2},{... | collective-permute-start | bytes 1179656 | tf_op jit(solution)/shard_map/ppermute | solution.py:189
  40.5 3.4 %collective-permute-start.8 = (bf16[64,3072]{1,0:T(8,128)(2,1)S(1)}, bf16[64,3072]{1,0:T(8,128)(2,1)S(1)}, u32[]{:S(2)}, u32[]{:S(2)}) collective-permute-start(bf16[64,3072]{1,0:T(8,128)(2,1)S(1)} %collective-permute-done.refs_0_), channel_id=1, source_target_pairs={{0,8},{4,12},{8,0},{12,4},{1,9},{5,13},{9,1},{13,5},{2,10},{6,14},... | collective-permute-start | bytes 1179656 | tf_op jit(solution)/shard_map/ppermute | solution.py:189
  44.5 0.0 collective-permute-done.4.refs_6_
  44.5 0.0 copy-start
  44.5 2.0 %copy-done = bf16[3,192,3072]{2,1,0:T(8,128)(2,1)S(1)} copy-done((bf16[3,192,3072]{2,1,0:T(8,128)(2,1)S(1)}, bf16[3,192,3072]{2,1,0:T(8,128)(2,1)}, u32[]{:S(2)}) %copy-start) | copy-done | bytes 3538968
  46.5 0.0 copy-start.2
  46.5 1.0 copy-done.2
  47.5 0.0 copy-start.4
  47.5 1.0 copy-done.4
  48.5 3.3 %shard_map.55 = (bf16[256,576]{1,0:T(8,128)(2,1)S(1)}, bf16[256,576]{1,0:T(8,128)(2,1)S(1)}) custom-call(s32[1]{0:T(128)S(6)} %copy.6.pid, bf16[64,3072]{1,0:T(8,128)(2,1)S(1)} %bitcast.21, bf16[64,3072]{1,0:T(8,128)(2,1)S(1)} %collective-permute-done.1.refs_1_, bf16[64,3072]{1,0:T(8,128)(2,1)S(1)} %collective-permute-done.2.refs_2_, ...), custom_call_target="tpu_custom_call" | custom-call | flops 1811939328 | bytes 9240576 | tf_op jit(solution)/shard_map/pallas_call | solution.py:49
  51.8 1.9 %collective-permute-start.5 = (bf16[256,576]{1,0:T(8,128)(2,1)S(1)}, bf16[256,576]{1,0:T(8,128)(2,1)S(1)}, u32[]{:S(2)}, u32[]{:S(2)}) collective-permute-start(bf16[256,576]{1,0:T(8,128)(2,1)S(1)} %get-tuple-element.19), channel_id=1, source_target_pairs={{0,1},{1,0},{2,3},{3,2},{4,5},{5,4},{6,7},{7,6},{8,9},{9,8},{10,11... | collective-permute-start | bytes 884744 | tf_op jit(solution)/shard_map/ppermute | solution.py:189
  53.7 0.0 collective-permute-done.6.refs_1_
  53.7 0.0 collective-permute-done.7.refs_2_
  53.7 2.5 %collective-permute-done.8.refs_3_ = bf16[64,3072]{1,0:T(8,128)(2,1)S(1)} collective-permute-done((bf16[64,3072]{1,0:T(8,128)(2,1)S(1)}, bf16[64,3072]{1,0:T(8,128)(2,1)S(1)}, u32[]{:S(2)}, u32[]{:S(2)}) %collective-permute-start.8) | collective-permute-done | bytes 393248 | tf_op jit(solution)/shard_map/ppermute | solution.py:189
  56.2 0.0 copy-done.1
  56.2 3.3 %shard_map.56 = (bf16[256,576]{1,0:T(8,128)(2,1)S(1)}, bf16[256,576]{1,0:T(8,128)(2,1)S(1)}) custom-call(s32[1]{0:T(128)S(6)} %copy.6.pid, bf16[64,3072]{1,0:T(8,128)(2,1)S(1)} %collective-permute-done.refs_0_, bf16[64,3072]{1,0:T(8,128)(2,1)S(1)} %collective-permute-done.6.refs_1_, bf16[64,3072]{1,0:T(8,128)(2,1)S(1)} %collective-permute-done.7.refs_2_, ...), custom_call_target="tpu_custom_call" | custom-call | flops 1811939328 | bytes 9240576 | tf_op jit(solution)/shard_map/pallas_call | solution.py:49
  59.6 0.0 copy-start.6
  59.6 1.9 %collective-permute-start.9 = (bf16[256,576]{1,0:T(8,128)(2,1)S(1)}, bf16[256,576]{1,0:T(8,128)(2,1)S(1)}, u32[]{:S(2)}, u32[]{:S(2)}) collective-permute-start(bf16[256,576]{1,0:T(8,128)(2,1)S(1)} %get-tuple-element.22), channel_id=1, source_target_pairs={{0,1},{1,0},{2,3},{3,2},{4,5},{5,4},{6,7},{7,6},{8,9},{9,8},{10,11... | collective-permute-start | bytes 884744 | tf_op jit(solution)/shard_map/ppermute | solution.py:189
  61.5 0.1 pad_add_fusion.1.place
  61.6 0.0 collective-permute-done.5
  61.6 1.5 %collective-permute-done.9 = bf16[256,576]{1,0:T(8,128)(2,1)S(1)} collective-permute-done((bf16[256,576]{1,0:T(8,128)(2,1)S(1)}, bf16[256,576]{1,0:T(8,128)(2,1)S(1)}, u32[]{:S(2)}, u32[]{:S(2)}) %collective-permute-start.9) | collective-permute-done | bytes 294944 | tf_op jit(solution)/shard_map/ppermute | solution.py:189
  63.1 3.7 %shard_map.57.low = bf16[16,32,192]{2,1,0:T(8,128)(2,1)S(1)} custom-call(s32[3]{0:T(128)S(1)} %pad_add_fusion.1.place, bf16[4,64,576]{2,1,0:T(8,128)(2,1)S(1)} %bitcast.23, bf16[4,64,576]{2,1,0:T(8,128)(2,1)S(1)} %bitcast.25, bf16[4,64,576]{2,1,0:T(8,128)(2,1)S(1)} %bitcast.27, bf16[4,64,576]{2,1,0:T(8,128)(2,1)S(1)} %bitcast.29), custom_call_target="tpu_custom_call" | custom-call | flops 402653184 | bytes 1376256 | tf_op jit(solution)/shard_map/pallas_call | solution.py:98
  66.8 0.0 copy-start.3
  66.9 0.0 copy-start.5
  66.9 12.1 %collective-permute-start.11 = (bf16[16,32,192]{2,1,0:T(8,128)(2,1)S(1)}, bf16[16,32,192]{2,1,0:T(8,128)(2,1)S(1)}, u32[]{:S(2)}, u32[]{:S(2)}) collective-permute-start(bf16[16,32,192]{2,1,0:T(8,128)(2,1)S(1)} %shard_map.57.low), channel_id=1, source_target_pairs={{16,0},{32,16},{48,32},{64,48},{80,64},{96,80},{112,96},{128,112},... | collective-permute-start | bytes 589832 | tf_op jit(solution)/shard_map/ppermute | solution.py:194
  78.9 3.7 %shard_map.58.high = bf16[16,32,192]{2,1,0:T(8,128)(2,1)S(1)} custom-call(s32[3]{0:T(128)S(1)} %pad_add_fusion.1.place, bf16[4,64,576]{2,1,0:T(8,128)(2,1)S(1)} %bitcast.24, bf16[4,64,576]{2,1,0:T(8,128)(2,1)S(1)} %bitcast.26, bf16[4,64,576]{2,1,0:T(8,128)(2,1)S(1)} %bitcast.28, bf16[4,64,576]{2,1,0:T(8,128)(2,1)S(1)} %bitcast.30), custom_call_target="tpu_custom_call" | custom-call | flops 402653184 | bytes 1376256 | tf_op jit(solution)/shard_map/pallas_call | solution.py:98
  82.7 1.9 %collective-permute-start.10 = (bf16[16,32,192]{2,1,0:T(8,128)(2,1)S(1)}, bf16[16,32,192]{2,1,0:T(8,128)(2,1)S(1)}, u32[]{:S(2)}, u32[]{:S(2)}) collective-permute-start(bf16[16,32,192]{2,1,0:T(8,128)(2,1)S(1)} %shard_map.58.high), channel_id=1, source_target_pairs={{0,16},{16,32},{32,48},{48,64},{64,80},{80,96},{96,112},{112,128},... | collective-permute-start | bytes 589832 | tf_op jit(solution)/shard_map/ppermute | solution.py:194
  84.6 0.0 copy-done.6
  84.6 0.1 pad_add_fusion
  84.7 0.1 dynamic_slice.3.overlap
  84.8 0.0 collective-permute-done.11.after
  84.8 0.6 shard_map.59.high
  85.4 9.3 %collective-permute-done.10.before = bf16[16,32,192]{2,1,0:T(8,128)(2,1)S(1)} collective-permute-done((bf16[16,32,192]{2,1,0:T(8,128)(2,1)S(1)}, bf16[16,32,192]{2,1,0:T(8,128)(2,1)S(1)}, u32[]{:S(2)}, u32[]{:S(2)}) %collective-permute-start.10) | collective-permute-done | bytes 196640 | tf_op jit(solution)/shard_map/ppermute | solution.py:194
  94.7 0.6 shard_map.60
  95.4 25.9 %all_to_all.5.avg = bf16[16,64,192]{2,1,0:T(8,128)(2,1)S(1)} all-to-all(bf16[16,64,192]{2,1,0:T(8,128)(2,1)S(1)} %shard_map.60), channel_id=1, replica_groups=mesh['ylo'=4,'z'=8,'x'=4,'yhi'=2,'core'=2] {'x','yhi','core'}, dimensions={0} | all-to-all | bytes 786432 | tf_op jit(solution)/shard_map/all_to_all | solution.py:229
  121.2 0.0 copy-done.3
  121.2 0.0 copy-done.5
  121.2 0.9 shard_map.61
  (1 shorter events, 0.0 us)
Async XLA Ops:
  0.0 44.5 %collective-permute-start.4 = (bf16[576,3072]{1,0:T(8,128)(2,1)}, bf16[576,3072]{1,0:T(8,128)(2,1)S(1)}, u32[]{:S(2)}, u32[]{:S(2)}) collective-permute-start(bf16[576,3072]{1,0:T(8,128)(2,1)} %bitcast.11), channel_id=1, source_target_pairs={{0,1},{1,0},{2,3},{3,2},{4,5},{5,4},{6,7},{7,6},{8,9},{9,8},{10,11... | collective-permute-start | bytes 10616840 | tf_op jit(solution)/shard_map/ppermute | solution.py:189
  1.9 25.4 %collective-permute-start = (bf16[64,3072]{1,0:T(8,128)(2,1)}, bf16[64,3072]{1,0:T(8,128)(2,1)S(1)}, u32[]{:S(2)}, u32[]{:S(2)}) collective-permute-start(bf16[64,3072]{1,0:T(8,128)(2,1)} %bitcast.17), channel_id=1, source_target_pairs={{0,2},{2,0},{1,3},{3,1},{4,6},{6,4},{5,7},{7,5},{8,10},{10,8},{9,1... | collective-permute-start | bytes 1179656 | tf_op jit(solution)/shard_map/ppermute | solution.py:189
  8.8 18.5 %collective-permute-start.1 = (bf16[64,3072]{1,0:T(8,128)(2,1)}, bf16[64,3072]{1,0:T(8,128)(2,1)S(1)}, u32[]{:S(2)}, u32[]{:S(2)}) collective-permute-start(bf16[64,3072]{1,0:T(8,128)(2,1)} %bitcast.18), channel_id=1, source_target_pairs={{0,4},{4,8},{8,12},{12,0},{1,5},{5,9},{9,13},{13,1},{2,6},{6,10},{... | collective-permute-start | bytes 1179656 | tf_op jit(solution)/shard_map/ppermute | solution.py:189
  12.2 20.9 %collective-permute-start.2 = (bf16[64,3072]{1,0:T(8,128)(2,1)}, bf16[64,3072]{1,0:T(8,128)(2,1)S(1)}, u32[]{:S(2)}, u32[]{:S(2)}) collective-permute-start(bf16[64,3072]{1,0:T(8,128)(2,1)} %bitcast.19), channel_id=1, source_target_pairs={{0,12},{4,0},{8,4},{12,8},{1,13},{5,1},{9,5},{13,9},{2,14},{6,2},{... | collective-permute-start | bytes 1179656 | tf_op jit(solution)/shard_map/ppermute | solution.py:189
  15.8 17.2 %collective-permute-start.3 = (bf16[64,3072]{1,0:T(8,128)(2,1)}, bf16[64,3072]{1,0:T(8,128)(2,1)S(1)}, u32[]{:S(2)}, u32[]{:S(2)}) collective-permute-start(bf16[64,3072]{1,0:T(8,128)(2,1)} %bitcast.20), channel_id=1, source_target_pairs={{0,8},{4,12},{8,0},{12,4},{1,9},{5,13},{9,1},{13,5},{2,10},{6,14},... | collective-permute-start | bytes 1179656 | tf_op jit(solution)/shard_map/ppermute | solution.py:189
  33.1 20.7 %collective-permute-start.6 = (bf16[64,3072]{1,0:T(8,128)(2,1)S(1)}, bf16[64,3072]{1,0:T(8,128)(2,1)S(1)}, u32[]{:S(2)}, u32[]{:S(2)}) collective-permute-start(bf16[64,3072]{1,0:T(8,128)(2,1)S(1)} %collective-permute-done.refs_0_), channel_id=1, source_target_pairs={{0,4},{4,8},{8,12},{12,0},{1,5},{5,9},{9,13},{13,1},{2,6},{6,10},{... | collective-permute-start | bytes 1179656 | tf_op jit(solution)/shard_map/ppermute | solution.py:189
  37.7 16.0 %collective-permute-start.7 = (bf16[64,3072]{1,0:T(8,128)(2,1)S(1)}, bf16[64,3072]{1,0:T(8,128)(2,1)S(1)}, u32[]{:S(2)}, u32[]{:S(2)}) collective-permute-start(bf16[64,3072]{1,0:T(8,128)(2,1)S(1)} %collective-permute-done.refs_0_), channel_id=1, source_target_pairs={{0,12},{4,0},{8,4},{12,8},{1,13},{5,1},{9,5},{13,9},{2,14},{6,2},{... | collective-permute-start | bytes 1179656 | tf_op jit(solution)/shard_map/ppermute | solution.py:189
  40.5 15.8 %collective-permute-start.8 = (bf16[64,3072]{1,0:T(8,128)(2,1)S(1)}, bf16[64,3072]{1,0:T(8,128)(2,1)S(1)}, u32[]{:S(2)}, u32[]{:S(2)}) collective-permute-start(bf16[64,3072]{1,0:T(8,128)(2,1)S(1)} %collective-permute-done.refs_0_), channel_id=1, source_target_pairs={{0,8},{4,12},{8,0},{12,4},{1,9},{5,13},{9,1},{13,5},{2,10},{6,14},... | collective-permute-start | bytes 1179656 | tf_op jit(solution)/shard_map/ppermute | solution.py:189
  44.5 2.0 %copy-start = (bf16[3,192,3072]{2,1,0:T(8,128)(2,1)S(1)}, bf16[3,192,3072]{2,1,0:T(8,128)(2,1)}, u32[]{:S(2)}) copy-start(bf16[3,192,3072]{2,1,0:T(8,128)(2,1)} %param.8) | copy-start | bytes 10616836
  46.5 1.0 copy-start.2
  47.5 1.0 copy-start.4
  48.5 7.8 %copy-start.1 = (bf16[3,192,3072]{2,1,0:T(8,128)(2,1)S(1)}, bf16[3,192,3072]{2,1,0:T(8,128)(2,1)}, u32[]{:S(2)}) copy-start(bf16[3,192,3072]{2,1,0:T(8,128)(2,1)} %param.8) | copy-start | bytes 10616836
  51.8 9.8 %collective-permute-start.5 = (bf16[256,576]{1,0:T(8,128)(2,1)S(1)}, bf16[256,576]{1,0:T(8,128)(2,1)S(1)}, u32[]{:S(2)}, u32[]{:S(2)}) collective-permute-start(bf16[256,576]{1,0:T(8,128)(2,1)S(1)} %get-tuple-element.19), channel_id=1, source_target_pairs={{0,1},{1,0},{2,3},{3,2},{4,5},{5,4},{6,7},{7,6},{8,9},{9,8},{10,11... | collective-permute-start | bytes 884744 | tf_op jit(solution)/shard_map/ppermute | solution.py:189
  59.6 25.0 %copy-start.6 = (s32[32]{0:T(128)S(1)}, s32[32]{0:T(128)}, u32[]{:S(2)}) copy-start(s32[32]{0:T(128)} %param.9) | copy-start | bytes 388
  59.6 3.5 %collective-permute-start.9 = (bf16[256,576]{1,0:T(8,128)(2,1)S(1)}, bf16[256,576]{1,0:T(8,128)(2,1)S(1)}, u32[]{:S(2)}, u32[]{:S(2)}) collective-permute-start(bf16[256,576]{1,0:T(8,128)(2,1)S(1)} %get-tuple-element.22), channel_id=1, source_target_pairs={{0,1},{1,0},{2,3},{3,2},{4,5},{5,4},{6,7},{7,6},{8,9},{9,8},{10,11... | collective-permute-start | bytes 884744 | tf_op jit(solution)/shard_map/ppermute | solution.py:189
  66.8 54.4 %copy-start.3 = (f32[8,3,3072]{2,0,1:T(8,128)S(1)}, f32[8,3,3072]{2,0,1:T(8,128)}, u32[]{:S(2)}) copy-start(f32[8,3,3072]{2,0,1:T(8,128)} %param.7) | copy-start | bytes 884740
  66.9 54.4 %copy-start.5 = (bf16[1,8,8,3072]{3,2,1,0:T(8,128)(2,1)S(1)}, bf16[1,8,8,3072]{3,2,1,0:T(8,128)(2,1)}, u32[]{:S(2)}) copy-start(bf16[1,8,8,3072]{3,2,1,0:T(8,128)(2,1)} %param.5) | copy-start | bytes 1179652
  66.9 17.9 %collective-permute-start.11 = (bf16[16,32,192]{2,1,0:T(8,128)(2,1)S(1)}, bf16[16,32,192]{2,1,0:T(8,128)(2,1)S(1)}, u32[]{:S(2)}, u32[]{:S(2)}) collective-permute-start(bf16[16,32,192]{2,1,0:T(8,128)(2,1)S(1)} %shard_map.57.low), channel_id=1, source_target_pairs={{16,0},{32,16},{48,32},{64,48},{80,64},{96,80},{112,96},{128,112},... | collective-permute-start | bytes 589832 | tf_op jit(solution)/shard_map/ppermute | solution.py:194
  82.7 12.1 %collective-permute-start.10 = (bf16[16,32,192]{2,1,0:T(8,128)(2,1)S(1)}, bf16[16,32,192]{2,1,0:T(8,128)(2,1)S(1)}, u32[]{:S(2)}, u32[]{:S(2)}) collective-permute-start(bf16[16,32,192]{2,1,0:T(8,128)(2,1)S(1)} %shard_map.58.high), channel_id=1, source_target_pairs={{0,16},{16,32},{32,48},{48,64},{64,80},{80,96},{96,112},{112,128},... | collective-permute-start | bytes 589832 | tf_op jit(solution)/shard_map/ppermute | solution.py:194

commit v5 on v2

v5 whole, which is shorter than its diff:
```python
import functools

import jax
import jax.numpy as jnp
from jax import lax
from jax.experimental import pallas as pl
from jax.experimental.pallas import tpu as pltpu
from jax.sharding import Mesh
from jax.sharding import PartitionSpec as P

HEAD_DIM = 64
OMAX = 3
NX, NY, NC = 4, 2, 2
MIB = 1 << 20
STEPS = (2, 1, 3)
ORIGINS = tuple((NX - by) % NX for by in STEPS)
SUM_LANE, TOP_LANE = HEAD_DIM, HEAD_DIM + 1
PIECES = 6
PATCH = 8


def cost(flops, inputs, outputs, transcendentals=0):
    size = sum(a.size * a.dtype.itemsize for a in (*inputs, *outputs))
    return pl.CostEstimate(flops=flops, bytes_accessed=size, transcendentals=transcendentals)


def project_kernel(blocks, hbm, *refs):
    tokens, (mods, wa, wb, oa, ob, normed), rest = refs[:blocks], refs[blocks : blocks + 6], refs[blocks + 6 :]
    tokens = list(tokens)
    rows = tokens[-1].shape[0]
    copies = []
    if hbm:
        va, first, sems = rest
        copies.append(pltpu.make_async_copy(tokens[0], first, sems.at[0]))
        step = wa.shape[0] // PIECES
        for i in range(PIECES):
            part = pl.ds(i * step, step)
            copies.append(pltpu.make_async_copy(wa.at[part], va.at[part], sems.at[i + 1]))
        tokens[0], wa = first, va
    for c in copies:
        c.start()
    shift = mods[0:1, :]
    scale = 1.0 + mods[1:2, :]
    for i in (*range(1, blocks), 0):
        if i == 0 and hbm:
            copies[0].wait()
        xf = tokens[i][...].astype(jnp.float32)
        mean = jnp.mean(xf, axis=-1, keepdims=True)
        xc = xf - mean
        var = jnp.mean(xc * xc, axis=-1, keepdims=True)
        normed[i * rows : (i + 1) * rows] = (xc * lax.rsqrt(var + 1e-06) * scale + shift).astype(jnp.bfloat16)
    contract = (((1,), (1,)), ((), ()))
    ob[...] = lax.dot_general(normed[...], wb[...], contract, preferred_element_type=jnp.float32).astype(jnp.bfloat16)
    for c in copies[1:]:
        c.wait()
    oa[...] = lax.dot_general(normed[...], wa[...], contract, preferred_element_type=jnp.float32).astype(jnp.bfloat16)


def project(blocks, mods, wa, wb, hbm):
    rows = sum(b.shape[0] for b in blocks)
    feats, width = wa.shape
    full = pl.BlockSpec(memory_space=pltpu.VMEM)
    far = pl.BlockSpec(memory_space=pltpu.HBM) if hbm else full
    shape = jax.ShapeDtypeStruct((rows, feats), jnp.bfloat16)
    scratch = [pltpu.VMEM((rows, width), jnp.bfloat16)]
    if hbm:
        wa = pltpu.with_memory_space_constraint(wa, pltpu.HBM)
        blocks = [pltpu.with_memory_space_constraint(blocks[0], pltpu.HBM), *blocks[1:]]
        scratch += [
            pltpu.VMEM((feats, width), jnp.bfloat16),
            pltpu.VMEM(blocks[0].shape, jnp.bfloat16),
            pltpu.SemaphoreType.DMA((PIECES + 1,)),
        ]
    return pl.pallas_call(
        functools.partial(project_kernel, len(blocks), hbm),
        in_specs=[far] + [full] * len(blocks) + [far, full],
        out_specs=[full] * 2,
        out_shape=[shape] * 2,
        scratch_shapes=scratch,
        cost_estimate=cost(1, (), ()),
        compiler_params=pltpu.CompilerParams(vmem_limit_bytes=20 * MIB),
    )(*blocks, mods, wa, wb)


def columns(groups, part, h, rows=slice(None)):
    width = groups[0].shape[2] // 3
    a = part * width + h * HEAD_DIM
    taken = [g[:, rows, a : a + HEAD_DIM] for g in groups]
    return jnp.concatenate([t.reshape(-1, HEAD_DIM) for t in taken], axis=0)


def values(groups, h):
    v = columns(groups, 2, h)
    lane = lax.broadcasted_iota(jnp.int32, (v.shape[0], 2 * HEAD_DIM), 1)
    return jnp.where(lane == SUM_LANE, jnp.ones_like(v[:1, :1]), jnp.concatenate([v, jnp.zeros_like(v)], axis=1))


def scored(q, k):
    return lax.dot_general(q, k, (((1,), (1,)), ((), ())), preferred_element_type=jnp.float32)


def weighted(s, top, v):
    p = jnp.exp((s - top) * (HEAD_DIM**-0.5)).astype(jnp.bfloat16)
    return lax.dot_general(p, v, (((1,), (0,)), ((), ())), preferred_element_type=jnp.float32)


def early_kernel(own, got, state):
    groups = (own, got)
    lane = lax.broadcasted_iota(jnp.int32, (1, 2 * HEAD_DIM), 1)
    heads = own.shape[2] // 3 // HEAD_DIM
    s = scored(columns(groups, 0, 0), columns(groups, 1, 0))
    for h in range(heads):
        then = scored(columns(groups, 0, h + 1), columns(groups, 1, h + 1)) if h + 1 < heads else None
        top = jnp.max(s, axis=-1, keepdims=True)
        out = jnp.where(lane == TOP_LANE, top, weighted(s, top, values(groups, h)))
        state[:, :, 2 * h * HEAD_DIM : 2 * (h + 1) * HEAD_DIM] = out.reshape(-1, own.shape[1], 2 * HEAD_DIM)
        s = then


def early(own, got):
    blocks, rows, feats = own.shape
    full = pl.BlockSpec(memory_space=pltpu.VMEM)
    shape = jax.ShapeDtypeStruct((2 * blocks, rows, feats // 3 * 2), jnp.float32)
    scores = (2 * blocks * rows) ** 2 * (feats // 3 // HEAD_DIM)
    return pl.pallas_call(
        early_kernel,
        in_specs=[full] * 2,
        out_specs=full,
        out_shape=shape,
        cost_estimate=cost(1, (), ()),
        compiler_params=pltpu.CompilerParams(vmem_limit_bytes=24 * MIB),
    )(own, got)


def attend_kernel(own0, got0, own1, got1, state, pair, third, first3, last3):
    a, b = (own0, got0), (own1, got1)
    rows = own0.shape[1]
    heads = own0.shape[2] // 3 // HEAD_DIM
    jobs = [(h, late) for h in range(heads) for late in (False, True)]

    def score(h, late):
        k = columns(b, 1, h)
        if late:
            return scored(columns(b, 0, h), jnp.concatenate([columns(a, 1, h), k], axis=0))
        return scored(columns(a, 0, h), k)

    done = {}
    s = score(*jobs[0])
    for i, (h, late) in enumerate(jobs):
        then = score(*jobs[i + 1]) if i + 1 < len(jobs) else None
        v = values(b, h)
        if late:
            top = jnp.max(s, axis=-1, keepdims=True)
            o = weighted(s, top, jnp.concatenate([values(a, h), v], axis=0))
        else:
            before = state[:, :, 2 * h * HEAD_DIM : 2 * (h + 1) * HEAD_DIM].reshape(-1, 2 * HEAD_DIM)
            top0 = before[:, TOP_LANE : TOP_LANE + 1]
            top = jnp.maximum(top0, jnp.max(s, axis=-1, keepdims=True))
            o = before * jnp.exp((top0 - top) * (HEAD_DIM**-0.5)) + weighted(s, top, v)
        done[h, late] = (o[:, :HEAD_DIM] / o[:, SUM_LANE : SUM_LANE + 1]).reshape(2, -1, rows, HEAD_DIM)
        s = then
    out = []
    for h in range(heads):
        parts = [done[h, late][j] for j in range(2) for late in (False, True)]
        out.append(jnp.concatenate(parts, axis=0))
    two = jnp.concatenate(out[:2], axis=2)
    pair[...] = two.astype(jnp.bfloat16)
    third[...] = out[2].astype(jnp.bfloat16)
    edge = OMAX * PATCH
    half = two.shape[0] // 2
    for ref, at in ((first3, 0), (last3, rows - edge)):
        cut = slice(at, at + edge)
        ref[: 2 * half * edge] = two[:, cut].reshape(-1, 2 * HEAD_DIM).astype(jnp.bfloat16)
        one = out[2][:, cut]
        one = jnp.concatenate([one[:half], one[half:]], axis=2)
        ref[2 * half * edge :] = one.reshape(-1, 2 * HEAD_DIM).astype(jnp.bfloat16)


def attend(groups, state):
    blocks = sum(g.shape[0] for g in groups)
    _, rows, feats = groups[0].shape
    full = pl.BlockSpec(memory_space=pltpu.VMEM)
    edge = blocks * OMAX * PATCH * 3 // 2
    shapes = [
        jax.ShapeDtypeStruct(s, jnp.bfloat16)
        for s in ((blocks, rows, 2 * HEAD_DIM), (blocks, rows, HEAD_DIM), (edge, 2 * HEAD_DIM), (edge, 2 * HEAD_DIM))
    ]
    return pl.pallas_call(
        attend_kernel,
        in_specs=[full] * 5,
        out_specs=[full] * 4,
        out_shape=shapes,
        compiler_params=pltpu.CompilerParams(vmem_limit_bytes=32 * MIB),
    )(*groups, state)


def unpacked(ref, blocks):
    rows = OMAX * PATCH
    data = ref[...].astype(jnp.float32)
    two = data[: blocks * rows].reshape(blocks, rows, 2 * HEAD_DIM)
    one = data[blocks * rows :].reshape(blocks // 2, rows, 2 * HEAD_DIM)
    return two, jnp.concatenate([one[:, :, :HEAD_DIM], one[:, :, HEAD_DIM:]], axis=0)


def average_kernel(overlap, place, pair, third, before, after, out):
    blocks, rows, _ = pair.shape
    frames = rows // PATCH
    ov_prev, ov_next = overlap[0], overlap[1]
    whole = []
    for mine, prev, nxt in zip((pair, third), unpacked(before, blocks), unpacked(after, blocks)):
        mine = mine[...].astype(jnp.float32)
        done = []
        for f in range(frames):
            cur = mine[:, f * PATCH : (f + 1) * PATCH]
            if f < OMAX or f >= frames - OMAX:
                if f < OMAX:
                    shared, source, at = f < ov_prev, prev, OMAX - ov_prev + f
                else:
                    shared, source, at = f >= frames - ov_next, nxt, f - frames + ov_next
                part = jnp.zeros_like(cur)
                for j in range(OMAX):
                    part = jnp.where(shared & (at == j), source[:, j * PATCH : (j + 1) * PATCH], part)
                cur = (cur + part) * jnp.where(shared, 0.5, 1.0)
            done.append(cur)
        whole.append(done)
    two = jnp.concatenate(whole[0], axis=1).astype(jnp.bfloat16)
    half = frames // 2
    one = jnp.concatenate(
        [jnp.concatenate(whole[1][:half], axis=1), jnp.concatenate(whole[1][half:], axis=1)], axis=2
    ).astype(jnp.bfloat16)
    for n in range(blocks):
        i = n % (blocks // 2)
        x = lax.rem(place[0] + (0, *ORIGINS, 0, *ORIGINS)[i], NX)
        y = place[1] if i < NX else 1 - place[1]
        c = place[2] if n < blocks // 2 else 1 - place[2]
        h = (x * NY + y) * NC + c
        out[h, :rows] = two[n]
        out[h, rows:] = one[n]


def average(overlap, place, pair, third, before, after):
    full = pl.BlockSpec(memory_space=pltpu.VMEM)
    smem = pl.BlockSpec(memory_space=pltpu.SMEM)
    blocks, rows, lanes = pair.shape
    return pl.pallas_call(
        average_kernel,
        in_specs=[smem] * 2 + [full] * 4,
        out_specs=full,
        out_shape=jax.ShapeDtypeStruct((blocks, rows * 3 // 2, lanes), jnp.bfloat16),
        compiler_params=pltpu.CompilerParams(vmem_limit_bytes=16 * MIB),
    )(overlap, place, pair, third, before, after)


def blend_kernel(lat, mods, avg, out):
    blocks = avg.shape[0]
    rows = lat.shape[0]
    width = 3 * HEAD_DIM
    for b in range(0, blocks, 2):
        parts = []
        for s in (b, b + 1):
            parts.append(avg[s, :rows].astype(jnp.float32))
            one = avg[s, rows:].astype(jnp.float32)
            parts.append(jnp.concatenate([one[:, :HEAD_DIM], one[:, HEAD_DIM:]], axis=0))
        cols = slice(b * width, (b + 2) * width)
        a = jnp.concatenate(parts, axis=1)
        out[:, cols] = (lat[:, cols].astype(jnp.float32) + mods[2:3, cols] * a).astype(jnp.bfloat16)


def blend(lat, mods, avg):
    full = pl.BlockSpec(memory_space=pltpu.VMEM)
    return pl.pallas_call(
        blend_kernel,
        in_specs=[full] * 3,
        out_specs=full,
        out_shape=jax.ShapeDtypeStruct(lat.shape, jnp.bfloat16),
        compiler_params=pltpu.CompilerParams(vmem_limit_bytes=16 * MIB),
    )(lat, mods, avg)


def around(value, axis, by):
    n = lax.axis_size(axis)
    return lax.ppermute(value, axis, [(i, (i + by) % n) for i in range(n)])


def along(value, by):
    n = lax.axis_size(("ylo", "z"))
    return lax.ppermute(value, ("ylo", "z"), [(i, i + by) for i in range(n) if 0 <= i + by < n])


def shards(latents, prompt_ids, modulation, w_qkv, intersection):
    _, frames, patches, width = latents.shape
    rows = frames * patches
    mine = latents.reshape(rows, width)
    wa = w_qkv.reshape(-1, width)
    place = jnp.stack([lax.axis_index("x"), lax.axis_index("yhi"), lax.axis_index("core")]).astype(jnp.int32)

    mods = lax.dynamic_index_in_dim(modulation, prompt_ids[0], keepdims=False)
    window = lax.axis_index(("ylo", "z"))
    padded = jnp.concatenate([intersection, jnp.zeros((1,), jnp.int32)])
    overlap = lax.dynamic_slice(padded, (window,), (2,))

    other = around(mine, "yhi", 1)
    near = [around(mine, "x", by) for by in STEPS]
    wb = around(wa, "core", 1)
    other, *near = lax.optimization_barrier((other, *near))
    far = [around(other, "x", by) for by in STEPS]

    own, give = project([mine, *near, other], mods, wa, wb, True)
    pair0 = [g.reshape(-1, rows, g.shape[-1]) for g in (own, around(give, "core", 1))]
    state = early(*pair0)
    state, *far = lax.optimization_barrier((state, *far))
    own, give = project(far, mods, wa, wb, False)
    pair1 = [g.reshape(-1, rows, g.shape[-1]) for g in (own, around(give, "core", 1))]

    pair, third, first3, last3 = attend(pair0 + pair1, state)
    before = along(last3, 1)
    after = along(first3, -1)
    avg = average(overlap, place, pair, third, before, after)
    avg = lax.all_to_all(avg, ("x", "yhi", "core"), 0, 0)
    return blend(mine, mods, avg).reshape(latents.shape)


def solution(mesh):
    fine = Mesh(mesh.devices.reshape(4, 8, NX, NY, NC), ("ylo", "z", "x", "yhi", "core"))
    win, head = ("ylo", "z"), ("x", "yhi", "core")
    in_specs = (P(win, None, head, None), P(win), P(), P(None, head, None), P())
    out_specs = P(win, None, head, None)
    return jax.shard_map(shards, mesh=fine, in_specs=in_specs, out_specs=out_specs, check_vma=False)
```

time: 118 us -> 110 us (0.932)
  waiting for transfers between devices: 23 us -> 16.8 us
  blocking collectives: 25.9 us -> 20.2 us
  Pallas kernels: 15.8 us -> 20.8 us
  local copies, waits for them, and re-layouts: 4.05 us -> 0.14 us
  starting transfers between devices: 48 us -> 50.7 us
    all_to_all x1, blocking collectives: 25.9 us -> 20.2 us  [shards(): avg = lax.all_to_all(avg, ('x', 'yhi', 'core'), 0, 0)]
    pallas_call x6, Pallas kernels: 15.8 us -> 20.8 us  [the longest x2 13.3 us: project(): pl.pallas_call(functools.partial(project_kernel, len(blocks), hbm), in_sp...]
    unnamed x14 -> x9, local copies, waits for them, and re-layouts: 3.97 us -> 0.04 us
    ppermute x10, waiting for transfers between devices: 17.3 us -> 13.6 us  [around(): return lax.ppermute(value, axis, [(i, (i + by) % n) for i in range(n)])]
    ppermute x10, starting transfers between devices: 34.3 us -> 37 us  [around(): return lax.ppermute(value, axis, [(i, (i + by) % n) for i in range(n)])]
    ppermute x2, waiting for transfers between devices: 5.67 us -> 3.15 us  [along(): lax.ppermute(value, ('ylo', 'z'), [(i, i + by) for i in range(n) if 0 <=...]
  transfers between devices with their start and end apart: 12 -> 12, of which waited for: 6 -> 7; matrix products, arithmetic and copies ran while one was open for 0% -> 0% of each run, Pallas kernels for 6% -> 9%
where the time goes in v5:
time: 110 us
  starting transfers between devices  50.7 us (46%)
  Pallas kernels  20.8 us (19%)
  blocking collectives  20.2 us (18%)
  waiting for transfers between devices  16.8 us (15%)
    ppermute x10, starting transfers between devices, around(): return lax.ppermute(value, axis, [(i, (i + by) % n) for i in range(n)])  37 us
    all_to_all x1, blocking collectives, shards(): avg = lax.all_to_all(avg, ('x', 'yhi', 'core'), 0, 0)  20.2 us
    ppermute x2, starting transfers between devices, along(): lax.ppermute(value, ('ylo', 'z'), [(i, i + by) for i in range(n) if 0 <=...  13.6 us
    ppermute x10, waiting for transfers between devices, around(): return lax.ppermute(value, axis, [(i, (i + by) % n) for i in range(n)])  13.6 us
    pallas_call x2, Pallas kernels, project(): pl.pallas_call(functools.partial(project_kernel, len(blocks), hbm), in_sp...  13.3 us
    pallas_call x1, Pallas kernels, attend(): pl.pallas_call(attend_kernel, in_specs=[full] * 5, out_specs=[full] * 4,...  3.76 us
    ppermute x2, waiting for transfers between devices, along(): lax.ppermute(value, ('ylo', 'z'), [(i, i + by) for i in range(n) if 0 <=...  3.15 us
  transfers between devices with their start and end apart: 12, of which 7 were waited for; matrix products, arithmetic and copies ran while one was open for 0% of the time, Pallas kernels for 9%

profile of v5, /device:TPU:8, one launch (start us, length us, event | category | flops | bytes accessed | tf_op | source)
XLA Modules:
  0.0 109.6 jit_solution(11273960038205439053)
XLA Ops:
  0.0 0.0 copy-start
  0.0 2.0 %collective-permute-start.4 = (bf16[576,3072]{1,0:T(8,128)(2,1)}, bf16[576,3072]{1,0:T(8,128)(2,1)}, u32[]{:S(2)}, u32[]{:S(2)}) collective-permute-start(bf16[576,3072]{1,0:T(8,128)(2,1)} %bitcast.17), channel_id=1, source_target_pairs={{0,1},{1,0},{2,3},{3,2},{4,5},{5,4},{6,7},{7,6},{8,9},{9,8},{10,11... | collective-permute-start | bytes 10616840 | tf_op jit(solution)/shard_map/ppermute | solution.py:282
  2.1 6.8 %collective-permute-start = (bf16[64,3072]{1,0:T(8,128)(2,1)}, bf16[64,3072]{1,0:T(8,128)(2,1)S(1)}, u32[]{:S(2)}, u32[]{:S(2)}) collective-permute-start(bf16[64,3072]{1,0:T(8,128)(2,1)} %bitcast.24), channel_id=1, source_target_pairs={{0,2},{2,0},{1,3},{3,1},{4,6},{6,4},{5,7},{7,5},{8,10},{10,8},{9,1... | collective-permute-start | bytes 1179656 | tf_op jit(solution)/shard_map/ppermute | solution.py:282
  8.9 4.9 %collective-permute-start.1 = (bf16[64,3072]{1,0:T(8,128)(2,1)}, bf16[64,3072]{1,0:T(8,128)(2,1)S(1)}, u32[]{:S(2)}, u32[]{:S(2)}) collective-permute-start(bf16[64,3072]{1,0:T(8,128)(2,1)} %bitcast.25), channel_id=1, source_target_pairs={{0,8},{4,12},{8,0},{12,4},{1,9},{5,13},{9,1},{13,5},{2,10},{6,14},... | collective-permute-start | bytes 1179656 | tf_op jit(solution)/shard_map/ppermute | solution.py:282
  13.8 2.5 %collective-permute-start.2 = (bf16[64,3072]{1,0:T(8,128)(2,1)}, bf16[64,3072]{1,0:T(8,128)(2,1)S(1)}, u32[]{:S(2)}, u32[]{:S(2)}) collective-permute-start(bf16[64,3072]{1,0:T(8,128)(2,1)} %bitcast.26), channel_id=1, source_target_pairs={{0,4},{4,8},{8,12},{12,0},{1,5},{5,9},{9,13},{13,1},{2,6},{6,10},{... | collective-permute-start | bytes 1179656 | tf_op jit(solution)/shard_map/ppermute | solution.py:282
  16.4 4.6 %collective-permute-start.3 = (bf16[64,3072]{1,0:T(8,128)(2,1)}, bf16[64,3072]{1,0:T(8,128)(2,1)S(1)}, u32[]{:S(2)}, u32[]{:S(2)}) collective-permute-start(bf16[64,3072]{1,0:T(8,128)(2,1)} %bitcast.27), channel_id=1, source_target_pairs={{0,12},{4,0},{8,4},{12,8},{1,13},{5,1},{9,5},{13,9},{2,14},{6,2},{... | collective-permute-start | bytes 1179656 | tf_op jit(solution)/shard_map/ppermute | solution.py:282
  21.6 5.9 %collective-permute-done.refs_4_ = bf16[64,3072]{1,0:T(8,128)(2,1)S(1)} collective-permute-done((bf16[64,3072]{1,0:T(8,128)(2,1)}, bf16[64,3072]{1,0:T(8,128)(2,1)S(1)}, u32[]{:S(2)}, u32[]{:S(2)}) %collective-permute-start) | collective-permute-done | bytes 393248 | tf_op jit(solution)/shard_map/ppermute | solution.py:282
  27.4 0.0 collective-permute-done.1.refs_1_
  27.4 4.8 %collective-permute-done.2.refs_2_ = bf16[64,3072]{1,0:T(8,128)(2,1)S(1)} collective-permute-done((bf16[64,3072]{1,0:T(8,128)(2,1)}, bf16[64,3072]{1,0:T(8,128)(2,1)S(1)}, u32[]{:S(2)}, u32[]{:S(2)}) %collective-permute-start.2) | collective-permute-done | bytes 393248 | tf_op jit(solution)/shard_map/ppermute | solution.py:282
  32.2 0.1 collective-permute-done.3.refs_3_
  32.3 4.8 %collective-permute-start.6 = (bf16[64,3072]{1,0:T(8,128)(2,1)S(1)}, bf16[64,3072]{1,0:T(8,128)(2,1)S(1)}, u32[]{:S(2)}, u32[]{:S(2)}) collective-permute-start(bf16[64,3072]{1,0:T(8,128)(2,1)S(1)} %collective-permute-done.refs_4_), channel_id=1, source_target_pairs={{0,8},{4,12},{8,0},{12,4},{1,9},{5,13},{9,1},{13,5},{2,10},{6,14},... | collective-permute-start | bytes 1179656 | tf_op jit(solution)/shard_map/ppermute | solution.py:282
  37.1 2.5 %collective-permute-start.7 = (bf16[64,3072]{1,0:T(8,128)(2,1)S(1)}, bf16[64,3072]{1,0:T(8,128)(2,1)S(1)}, u32[]{:S(2)}, u32[]{:S(2)}) collective-permute-start(bf16[64,3072]{1,0:T(8,128)(2,1)S(1)} %collective-permute-done.refs_4_), channel_id=1, source_target_pairs={{0,4},{4,8},{8,12},{12,0},{1,5},{5,9},{9,13},{13,1},{2,6},{6,10},{... | collective-permute-start | bytes 1179656 | tf_op jit(solution)/shard_map/ppermute | solution.py:282
  39.6 4.6 %collective-permute-start.8 = (bf16[64,3072]{1,0:T(8,128)(2,1)S(1)}, bf16[64,3072]{1,0:T(8,128)(2,1)S(1)}, u32[]{:S(2)}, u32[]{:S(2)}) collective-permute-start(bf16[64,3072]{1,0:T(8,128)(2,1)S(1)} %collective-permute-done.refs_4_), channel_id=1, source_target_pairs={{0,12},{4,0},{8,4},{12,8},{1,13},{5,1},{9,5},{13,9},{2,14},{6,2},{... | collective-permute-start | bytes 1179656 | tf_op jit(solution)/shard_map/ppermute | solution.py:282
  44.2 0.0 copy-done
  44.2 0.0 collective-permute-done.4.refs_7_.refs_5_
  44.3 0.0 copy-start.1
  44.3 8.1 %shard_map.55 = (bf16[320,576]{1,0:T(8,128)(2,1)S(1)}, bf16[320,576]{1,0:T(8,128)(2,1)S(1)}) custom-call(bf16[64,3072]{1,0:T(8,128)(2,1)} %bitcast.28, bf16[64,3072]{1,0:T(8,128)(2,1)S(1)} %collective-permute-done.1.refs_1_, bf16[64,3072]{1,0:T(8,128)(2,1)S(1)} %collective-permute-done.2.refs_2_, bf16[64,3072]{1,0:T(8,128)(2,1)S(1)} %collective-permute-done.3.refs_3_, ...), custom_call_target="tpu_custom_call" | custom-call | flops 1 | tf_op jit(solution)/shard_map/pallas_call | solution.py:74
  52.4 1.9 %collective-permute-start.5 = (bf16[320,576]{1,0:T(8,128)(2,1)S(1)}, bf16[320,576]{1,0:T(8,128)(2,1)S(1)}, u32[]{:S(2)}, u32[]{:S(2)}) collective-permute-start(bf16[320,576]{1,0:T(8,128)(2,1)S(1)} %get-tuple-element.26), channel_id=1, source_target_pairs={{0,1},{1,0},{2,3},{3,2},{4,5},{5,4},{6,7},{7,6},{8,9},{9,8},{10,11... | collective-permute-start | bytes 1105928 | tf_op jit(solution)/shard_map/ppermute | solution.py:282
  54.3 1.7 %collective-permute-done.5 = bf16[320,576]{1,0:T(8,128)(2,1)S(1)} collective-permute-done((bf16[320,576]{1,0:T(8,128)(2,1)S(1)}, bf16[320,576]{1,0:T(8,128)(2,1)S(1)}, u32[]{:S(2)}, u32[]{:S(2)}) %collective-permute-start.5) | collective-permute-done | bytes 368672 | tf_op jit(solution)/shard_map/ppermute | solution.py:282
  56.0 1.9 %shard_map.56.state = f32[10,64,384]{2,1,0:T(8,128)S(1)} custom-call(bf16[5,64,576]{2,1,0:T(8,128)(2,1)S(1)} %bitcast.20, bf16[5,64,576]{2,1,0:T(8,128)(2,1)S(1)} %bitcast.22), custom_call_target="tpu_custom_call" | custom-call | flops 1 | tf_op jit(solution)/shard_map/pallas_call | solution.py:125
  58.0 0.0 copy-start.3
  58.0 0.0 collective-permute-done.6.refs_0_
  58.0 0.0 collective-permute-done.7.refs_1_
  58.0 0.0 collective-permute-done.8.refs_2_
  58.0 0.0 copy-done.1
  58.0 5.3 %shard_map.57 = (bf16[192,576]{1,0:T(8,128)(2,1)S(1)}, bf16[192,576]{1,0:T(8,128)(2,1)S(1)}) custom-call(bf16[64,3072]{1,0:T(8,128)(2,1)S(1)} %collective-permute-done.6.refs_0_, bf16[64,3072]{1,0:T(8,128)(2,1)S(1)} %collective-permute-done.7.refs_1_, bf16[64,3072]{1,0:T(8,128)(2,1)S(1)} %collective-permute-done.8.refs_2_, f32[3,3072]{1,0:T(4,128)S(1)} %bitcast.31, ...), custom_call_target="tpu_custom_call" | custom-call | flops 1 | tf_op jit(solution)/shard_map/pallas_call | solution.py:74
  63.3 0.0 copy-start.2
  63.3 2.4 %collective-permute-start.9 = (bf16[192,576]{1,0:T(8,128)(2,1)S(1)}, bf16[192,576]{1,0:T(8,128)(2,1)S(1)}, u32[]{:S(2)}, u32[]{:S(2)}) collective-permute-start(bf16[192,576]{1,0:T(8,128)(2,1)S(1)} %get-tuple-element.31), channel_id=1, source_target_pairs={{0,1},{1,0},{2,3},{3,2},{4,5},{5,4},{6,7},{7,6},{8,9},{9,8},{10,11... | collective-permute-start | bytes 663560 | tf_op jit(solution)/shard_map/ppermute | solution.py:282
  65.6 1.2 %collective-permute-done.9 = bf16[192,576]{1,0:T(8,128)(2,1)S(1)} collective-permute-done((bf16[192,576]{1,0:T(8,128)(2,1)S(1)}, bf16[192,576]{1,0:T(8,128)(2,1)S(1)}, u32[]{:S(2)}, u32[]{:S(2)}) %collective-permute-start.9) | collective-permute-done | bytes 221216 | tf_op jit(solution)/shard_map/ppermute | solution.py:282
  66.8 3.8 %shard_map.58 = (bf16[16,64,128]{2,1,0:T(8,128)(2,1)S(1)}, bf16[16,64,64]{2,1,0:T(8,128)(2,1)S(1)}, bf16[576,128]{1,0:T(8,128)(2,1)S(1)}, bf16[576,128]{1,0:T(8,128)(2,1)S(1)}) custom-call(bf16[5,64,576]{2,1,0:T(8,128)(2,1)S(1)} %bitcast.21, bf16[5,64,576]{2,1,0:T(8,128)(2,1)S(1)} %bitcast.23, bf16[3,64,576]{2,1,0:T(8,128)(2,1)S(1)} %bitcast.33, ...), custom_call_target="tpu_custom_call" | custom-call | tf_op jit(solution)/shard_map/pallas_call | solution.py:188
  70.6 4.3 %collective-permute-start.10 = (bf16[576,128]{1,0:T(8,128)(2,1)S(1)}, bf16[576,128]{1,0:T(8,128)(2,1)S(1)}, u32[]{:S(2)}, u32[]{:S(2)}) collective-permute-start(bf16[576,128]{1,0:T(8,128)(2,1)S(1)} %get-tuple-element.35), channel_id=1, source_target_pairs={{0,16},{16,32},{32,48},{48,64},{64,80},{80,96},{96,112},{112,128},... | collective-permute-start | bytes 442376 | tf_op jit(solution)/shard_map/ppermute | solution.py:287
  74.9 9.4 %collective-permute-start.11 = (bf16[576,128]{1,0:T(8,128)(2,1)S(1)}, bf16[576,128]{1,0:T(8,128)(2,1)S(1)}, u32[]{:S(2)}, u32[]{:S(2)}) collective-permute-start(bf16[576,128]{1,0:T(8,128)(2,1)S(1)} %get-tuple-element.36), channel_id=1, source_target_pairs={{16,0},{32,16},{48,32},{64,48},{80,64},{96,80},{112,96},{128,112},... | collective-permute-start | bytes 442376 | tf_op jit(solution)/shard_map/ppermute | solution.py:287
  84.2 0.0 copy-done.3
  84.3 0.1 pad_add_fusion
  84.3 0.1 dynamic_slice.8.overlap
  84.4 0.1 pad_add_fusion.1.place
  84.5 2.0 %collective-permute-done.10.before = bf16[576,128]{1,0:T(8,128)(2,1)S(1)} collective-permute-done((bf16[576,128]{1,0:T(8,128)(2,1)S(1)}, bf16[576,128]{1,0:T(8,128)(2,1)S(1)}, u32[]{:S(2)}, u32[]{:S(2)}) %collective-permute-start.10) | collective-permute-done | bytes 147488 | tf_op jit(solution)/shard_map/ppermute | solution.py:287
  86.5 1.2 %collective-permute-done.11.after = bf16[576,128]{1,0:T(8,128)(2,1)S(1)} collective-permute-done((bf16[576,128]{1,0:T(8,128)(2,1)S(1)}, bf16[576,128]{1,0:T(8,128)(2,1)S(1)}, u32[]{:S(2)}, u32[]{:S(2)}) %collective-permute-start.11) | collective-permute-done | bytes 147488 | tf_op jit(solution)/shard_map/ppermute | solution.py:287
  87.6 0.8 shard_map.59
  88.4 20.2 %all_to_all.5.avg = bf16[16,96,128]{2,1,0:T(8,128)(2,1)S(1)} all-to-all(bf16[16,96,128]{2,1,0:T(8,128)(2,1)S(1)} %shard_map.59), channel_id=1, replica_groups=mesh['ylo'=4,'z'=8,'x'=4,'yhi'=2,'core'=2] {'x','yhi','core'}, dimensions={0} | all-to-all | bytes 786432 | tf_op jit(solution)/shard_map/all_to_all | solution.py:319
  108.6 0.0 copy-done.2
  108.6 1.0 shard_map.60
  (2 shorter events, 0.0 us)
Async XLA Ops:
  0.0 44.2 %copy-start = (f32[8,3,3072]{2,0,1:T(8,128)S(1)}, f32[8,3,3072]{2,0,1:T(8,128)}, u32[]{:S(2)}) copy-start(f32[8,3,3072]{2,0,1:T(8,128)} %param.7) | copy-start | bytes 884740
  0.0 44.2 %collective-permute-start.4 = (bf16[576,3072]{1,0:T(8,128)(2,1)}, bf16[576,3072]{1,0:T(8,128)(2,1)}, u32[]{:S(2)}, u32[]{:S(2)}) collective-permute-start(bf16[576,3072]{1,0:T(8,128)(2,1)} %bitcast.17), channel_id=1, source_target_pairs={{0,1},{1,0},{2,3},{3,2},{4,5},{5,4},{6,7},{7,6},{8,9},{9,8},{10,11... | collective-permute-start | bytes 10616840 | tf_op jit(solution)/shard_map/ppermute | solution.py:282
  2.1 25.4 %collective-permute-start = (bf16[64,3072]{1,0:T(8,128)(2,1)}, bf16[64,3072]{1,0:T(8,128)(2,1)S(1)}, u32[]{:S(2)}, u32[]{:S(2)}) collective-permute-start(bf16[64,3072]{1,0:T(8,128)(2,1)} %bitcast.24), channel_id=1, source_target_pairs={{0,2},{2,0},{1,3},{3,1},{4,6},{6,4},{5,7},{7,5},{8,10},{10,8},{9,1... | collective-permute-start | bytes 1179656 | tf_op jit(solution)/shard_map/ppermute | solution.py:282
  8.9 18.5 %collective-permute-start.1 = (bf16[64,3072]{1,0:T(8,128)(2,1)}, bf16[64,3072]{1,0:T(8,128)(2,1)S(1)}, u32[]{:S(2)}, u32[]{:S(2)}) collective-permute-start(bf16[64,3072]{1,0:T(8,128)(2,1)} %bitcast.25), channel_id=1, source_target_pairs={{0,8},{4,12},{8,0},{12,4},{1,9},{5,13},{9,1},{13,5},{2,10},{6,14},... | collective-permute-start | bytes 1179656 | tf_op jit(solution)/shard_map/ppermute | solution.py:282
  13.8 18.3 %collective-permute-start.2 = (bf16[64,3072]{1,0:T(8,128)(2,1)}, bf16[64,3072]{1,0:T(8,128)(2,1)S(1)}, u32[]{:S(2)}, u32[]{:S(2)}) collective-permute-start(bf16[64,3072]{1,0:T(8,128)(2,1)} %bitcast.26), channel_id=1, source_target_pairs={{0,4},{4,8},{8,12},{12,0},{1,5},{5,9},{9,13},{13,1},{2,6},{6,10},{... | collective-permute-start | bytes 1179656 | tf_op jit(solution)/shard_map/ppermute | solution.py:282
  16.4 15.9 %collective-permute-start.3 = (bf16[64,3072]{1,0:T(8,128)(2,1)}, bf16[64,3072]{1,0:T(8,128)(2,1)S(1)}, u32[]{:S(2)}, u32[]{:S(2)}) collective-permute-start(bf16[64,3072]{1,0:T(8,128)(2,1)} %bitcast.27), channel_id=1, source_target_pairs={{0,12},{4,0},{8,4},{12,8},{1,13},{5,1},{9,5},{13,9},{2,14},{6,2},{... | collective-permute-start | bytes 1179656 | tf_op jit(solution)/shard_map/ppermute | solution.py:282
  32.3 25.7 %collective-permute-start.6 = (bf16[64,3072]{1,0:T(8,128)(2,1)S(1)}, bf16[64,3072]{1,0:T(8,128)(2,1)S(1)}, u32[]{:S(2)}, u32[]{:S(2)}) collective-permute-start(bf16[64,3072]{1,0:T(8,128)(2,1)S(1)} %collective-permute-done.refs_4_), channel_id=1, source_target_pairs={{0,8},{4,12},{8,0},{12,4},{1,9},{5,13},{9,1},{13,5},{2,10},{6,14},... | collective-permute-start | bytes 1179656 | tf_op jit(solution)/shard_map/ppermute | solution.py:282
  37.1 20.9 %collective-permute-start.7 = (bf16[64,3072]{1,0:T(8,128)(2,1)S(1)}, bf16[64,3072]{1,0:T(8,128)(2,1)S(1)}, u32[]{:S(2)}, u32[]{:S(2)}) collective-permute-start(bf16[64,3072]{1,0:T(8,128)(2,1)S(1)} %collective-permute-done.refs_4_), channel_id=1, source_target_pairs={{0,4},{4,8},{8,12},{12,0},{1,5},{5,9},{9,13},{13,1},{2,6},{6,10},{... | collective-permute-start | bytes 1179656 | tf_op jit(solution)/shard_map/ppermute | solution.py:282
  39.6 18.4 %collective-permute-start.8 = (bf16[64,3072]{1,0:T(8,128)(2,1)S(1)}, bf16[64,3072]{1,0:T(8,128)(2,1)S(1)}, u32[]{:S(2)}, u32[]{:S(2)}) collective-permute-start(bf16[64,3072]{1,0:T(8,128)(2,1)S(1)} %collective-permute-done.refs_4_), channel_id=1, source_target_pairs={{0,12},{4,0},{8,4},{12,8},{1,13},{5,1},{9,5},{13,9},{2,14},{6,2},{... | collective-permute-start | bytes 1179656 | tf_op jit(solution)/shard_map/ppermute | solution.py:282
  44.3 13.8 %copy-start.1 = (bf16[3,192,3072]{2,1,0:T(8,128)(2,1)S(1)}, bf16[3,192,3072]{2,1,0:T(8,128)(2,1)}, u32[]{:S(2)}) copy-start(bf16[3,192,3072]{2,1,0:T(8,128)(2,1)} %param.8) | copy-start | bytes 10616836
  52.4 3.6 %collective-permute-start.5 = (bf16[320,576]{1,0:T(8,128)(2,1)S(1)}, bf16[320,576]{1,0:T(8,128)(2,1)S(1)}, u32[]{:S(2)}, u32[]{:S(2)}) collective-permute-start(bf16[320,576]{1,0:T(8,128)(2,1)S(1)} %get-tuple-element.26), channel_id=1, source_target_pairs={{0,1},{1,0},{2,3},{3,2},{4,5},{5,4},{6,7},{7,6},{8,9},{9,8},{10,11... | collective-permute-start | bytes 1105928 | tf_op jit(solution)/shard_map/ppermute | solution.py:282
  58.0 26.3 %copy-start.3 = (s32[32]{0:T(128)S(1)}, s32[32]{0:T(128)}, u32[]{:S(2)}) copy-start(s32[32]{0:T(128)} %param.9) | copy-start | bytes 388
  63.3 45.4 %copy-start.2 = (bf16[1,8,8,3072]{3,2,1,0:T(8,128)(2,1)S(1)}, bf16[1,8,8,3072]{3,2,1,0:T(8,128)(2,1)}, u32[]{:S(2)}) copy-start(bf16[1,8,8,3072]{3,2,1,0:T(8,128)(2,1)} %param.5) | copy-start | bytes 1179652
  63.3 3.5 %collective-permute-start.9 = (bf16[192,576]{1,0:T(8,128)(2,1)S(1)}, bf16[192,576]{1,0:T(8,128)(2,1)S(1)}, u32[]{:S(2)}, u32[]{:S(2)}) collective-permute-start(bf16[192,576]{1,0:T(8,128)(2,1)S(1)} %get-tuple-element.31), channel_id=1, source_target_pairs={{0,1},{1,0},{2,3},{3,2},{4,5},{5,4},{6,7},{7,6},{8,9},{9,8},{10,11... | collective-permute-start | bytes 663560 | tf_op jit(solution)/shard_map/ppermute | solution.py:282
  70.6 15.9 %collective-permute-start.10 = (bf16[576,128]{1,0:T(8,128)(2,1)S(1)}, bf16[576,128]{1,0:T(8,128)(2,1)S(1)}, u32[]{:S(2)}, u32[]{:S(2)}) collective-permute-start(bf16[576,128]{1,0:T(8,128)(2,1)S(1)} %get-tuple-element.35), channel_id=1, source_target_pairs={{0,16},{16,32},{32,48},{48,64},{64,80},{80,96},{96,112},{112,128},... | collective-permute-start | bytes 442376 | tf_op jit(solution)/shard_map/ppermute | solution.py:287
  74.9 12.8 %collective-permute-start.11 = (bf16[576,128]{1,0:T(8,128)(2,1)S(1)}, bf16[576,128]{1,0:T(8,128)(2,1)S(1)}, u32[]{:S(2)}, u32[]{:S(2)}) collective-permute-start(bf16[576,128]{1,0:T(8,128)(2,1)S(1)} %get-tuple-element.36), channel_id=1, source_target_pairs={{16,0},{32,16},{48,32},{64,48},{80,64},{96,80},{112,96},{128,112},... | collective-permute-start | bytes 442376 | tf_op jit(solution)/shard_map/ppermute | solution.py:287

commit v6 on v5

--- a/solution.py
+++ b/solution.py
@@ -15,7 +15,6 @@
 STEPS = (2, 1, 3)
 ORIGINS = tuple((NX - by) % NX for by in STEPS)
 SUM_LANE, TOP_LANE = HEAD_DIM, HEAD_DIM + 1
-PIECES = 6
 PATCH = 8
 
 
@@ -24,61 +23,82 @@
     return pl.CostEstimate(flops=flops, bytes_accessed=size, transcendentals=transcendentals)
 
 
-def project_kernel(blocks, hbm, *refs):
-    tokens, (mods, wa, wb, oa, ob, normed), rest = refs[:blocks], refs[blocks : blocks + 6], refs[blocks + 6 :]
-    tokens = list(tokens)
+def normalise(tokens, mods, normed, order, before):
     rows = tokens[-1].shape[0]
-    copies = []
-    if hbm:
-        va, first, sems = rest
-        copies.append(pltpu.make_async_copy(tokens[0], first, sems.at[0]))
-        step = wa.shape[0] // PIECES
-        for i in range(PIECES):
-            part = pl.ds(i * step, step)
-            copies.append(pltpu.make_async_copy(wa.at[part], va.at[part], sems.at[i + 1]))
-        tokens[0], wa = first, va
-    for c in copies:
-        c.start()
     shift = mods[0:1, :]
     scale = 1.0 + mods[1:2, :]
-    for i in (*range(1, blocks), 0):
-        if i == 0 and hbm:
-            copies[0].wait()
+    for i in order:
+        before(i)
         xf = tokens[i][...].astype(jnp.float32)
         mean = jnp.mean(xf, axis=-1, keepdims=True)
         xc = xf - mean
         var = jnp.mean(xc * xc, axis=-1, keepdims=True)
         normed[i * rows : (i + 1) * rows] = (xc * lax.rsqrt(var + 1e-06) * scale + shift).astype(jnp.bfloat16)
-    contract = (((1,), (1,)), ((), ()))
-    ob[...] = lax.dot_general(normed[...], wb[...], contract, preferred_element_type=jnp.float32).astype(jnp.bfloat16)
-    for c in copies[1:]:
+
+
+def product(normed, w, out):
+    r = lax.dot_general(normed[...], w[...], (((1,), (1,)), ((), ())), preferred_element_type=jnp.float32)
+    out[...] = r[: out.shape[0]].astype(jnp.bfloat16)
+
+
+def early_project_kernel(blocks, *refs):
+    tokens, (mods, wa, wb, oa, ob, va, vb, first, normed, sems) = list(refs[:blocks]), refs[blocks:]
+    head = pltpu.make_async_copy(tokens[0], first, sems.at[0])
+    fetches = [pltpu.make_async_copy(wb, vb, sems.at[1]), pltpu.make_async_copy(wa, va, sems.at[2])]
+    for c in (head, *fetches):
+        c.start()
+    tokens[0] = first
+    normalise(tokens, mods, normed, (*range(1, blocks), 0), lambda i: head.wait() if i == 0 else None)
+    for c, w, o in zip(fetches, (vb, va), (ob, oa)):
         c.wait()
-    oa[...] = lax.dot_general(normed[...], wa[...], contract, preferred_element_type=jnp.float32).astype(jnp.bfloat16)
-
-
-def project(blocks, mods, wa, wb, hbm):
+        product(normed, w, o)
+
+
+def early_project(blocks, mods, wa, wb):
     rows = sum(b.shape[0] for b in blocks)
     feats, width = wa.shape
     full = pl.BlockSpec(memory_space=pltpu.VMEM)
-    far = pl.BlockSpec(memory_space=pltpu.HBM) if hbm else full
+    away = pl.BlockSpec(memory_space=pltpu.HBM)
+    first, wa, wb = [pltpu.with_memory_space_constraint(a, pltpu.HBM) for a in (blocks[0], wa, wb)]
     shape = jax.ShapeDtypeStruct((rows, feats), jnp.bfloat16)
-    scratch = [pltpu.VMEM((rows, width), jnp.bfloat16)]
-    if hbm:
-        wa = pltpu.with_memory_space_constraint(wa, pltpu.HBM)
-        blocks = [pltpu.with_memory_space_constraint(blocks[0], pltpu.HBM), *blocks[1:]]
-        scratch += [
-            pltpu.VMEM((feats, width), jnp.bfloat16),
-            pltpu.VMEM(blocks[0].shape, jnp.bfloat16),
-            pltpu.SemaphoreType.DMA((PIECES + 1,)),
-        ]
-    return pl.pallas_call(
-        functools.partial(project_kernel, len(blocks), hbm),
-        in_specs=[far] + [full] * len(blocks) + [far, full],
+    weight = jax.ShapeDtypeStruct((feats, width), jnp.bfloat16)
+    return pl.pallas_call(
+        functools.partial(early_project_kernel, len(blocks)),
+        in_specs=[away] + [full] * len(blocks) + [away] * 2,
+        out_specs=[full] * 4,
+        out_shape=[shape, shape, weight, weight],
+        scratch_shapes=[
+            pltpu.VMEM(first.shape, jnp.bfloat16),
+            pltpu.VMEM((rows, width), jnp.bfloat16),
+            pltpu.SemaphoreType.DMA((3,)),
+        ],
+        cost_estimate=cost(1, (), ()),
+        compiler_params=pltpu.CompilerParams(vmem_limit_bytes=24 * MIB),
+    )(first, *blocks[1:], mods, wa, wb)
+
+
+def project_kernel(blocks, *refs):
+    tokens, (mods, wa, wb, oa, ob, normed) = refs[:blocks], refs[blocks:]
+    used = oa.shape[0]
+    normed[used:] = jnp.zeros((normed.shape[0] - used, normed.shape[1]), jnp.bfloat16)
+    normalise(tokens, mods, normed, range(blocks), lambda i: None)
+    product(normed, wb, ob)
+    product(normed, wa, oa)
+
+
+def project(blocks, mods, wa, wb):
+    rows = sum(b.shape[0] for b in blocks)
+    feats, width = wa.shape
+    full = pl.BlockSpec(memory_space=pltpu.VMEM)
+    shape = jax.ShapeDtypeStruct((rows, feats), jnp.bfloat16)
+    return pl.pallas_call(
+        functools.partial(project_kernel, len(blocks)),
+        in_specs=[full] * (len(blocks) + 3),
         out_specs=[full] * 2,
         out_shape=[shape] * 2,
-        scratch_shapes=scratch,
-        cost_estimate=cost(1, (), ()),
-        compiler_params=pltpu.CompilerParams(vmem_limit_bytes=20 * MIB),
+        scratch_shapes=[pltpu.VMEM((4 * blocks[0].shape[0], width), jnp.bfloat16)],
+        cost_estimate=cost(1, (wa, wb), ()),
+        compiler_params=pltpu.CompilerParams(vmem_limit_bytes=24 * MIB),
     )(*blocks, mods, wa, wb)
 
 
@@ -302,14 +322,12 @@
     other = around(mine, "yhi", 1)
     near = [around(mine, "x", by) for by in STEPS]
     wb = around(wa, "core", 1)
-    other, *near = lax.optimization_barrier((other, *near))
     far = [around(other, "x", by) for by in STEPS]
 
-    own, give = project([mine, *near, other], mods, wa, wb, True)
+    own, give, wa, wb = early_project([mine, *near, other], mods, wa, wb)
     pair0 = [g.reshape(-1, rows, g.shape[-1]) for g in (own, around(give, "core", 1))]
     state = early(*pair0)
-    state, *far = lax.optimization_barrier((state, *far))
-    own, give = project(far, mods, wa, wb, False)
+    own, give = project(far, mods, wa, wb)
     pair1 = [g.reshape(-1, rows, g.shape[-1]) for g in (own, around(give, "core", 1))]
 
     pair, third, first3, last3 = attend(pair0 + pair1, state)

time: 110 us -> 104 us (0.945)
  the two profiles are of different devices: /device:TPU:8 before, /device:TPU:200 now
where the time goes in v6:
time: 104 us
  starting transfers between devices  44.4 us (43%)
  blocking collectives  26.4 us (25%)
  Pallas kernels  17.3 us (17%)
  waiting for transfers between devices  14.7 us (14%)
    ppermute x10, starting transfers between devices, around(): return lax.ppermute(value, axis, [(i, (i + by) % n) for i in range(n)])  37 us
    all_to_all x1, blocking collectives, shards(): avg = lax.all_to_all(avg, ('x', 'yhi', 'core'), 0, 0)  26.4 us
    ppermute x10, waiting for transfers between devices, around(): return lax.ppermute(value, axis, [(i, (i + by) % n) for i in range(n)])  7.78 us
    ppermute x2, starting transfers between devices, along(): lax.ppermute(value, ('ylo', 'z'), [(i, i + by) for i in range(n) if 0 <=...  7.41 us
    ppermute x2, waiting for transfers between devices, along(): lax.ppermute(value, ('ylo', 'z'), [(i, i + by) for i in range(n) if 0 <=...  6.91 us
    pallas_call x1, Pallas kernels, early_project(): pl.pallas_call(functools.partial(early_project_kernel, len(blocks)), in_s...  6.62 us
    pallas_call x1, Pallas kernels, attend(): pl.pallas_call(attend_kernel, in_specs=[full] * 5, out_specs=[full] * 4,...  3.76 us
    pallas_call x1, Pallas kernels, project(): pl.pallas_call(functools.partial(project_kernel, len(blocks)), in_specs=[...  3.17 us
  transfers between devices with their start and end apart: 12, of which 5 were waited for; matrix products, arithmetic and copies ran while one was open for 0% of the time, Pallas kernels for 11%

profile of v6, /device:TPU:200, one launch (start us, length us, event | category | flops | bytes accessed | tf_op | source)
XLA Modules:
  0.0 103.9 jit_solution(13591224383568722909)
XLA Ops:
  0.0 0.0 copy-start
  0.0 2.0 %collective-permute-start.4 = (bf16[576,3072]{1,0:T(8,128)(2,1)}, bf16[576,3072]{1,0:T(8,128)(2,1)}, u32[]{:S(2)}, u32[]{:S(2)}) collective-permute-start(bf16[576,3072]{1,0:T(8,128)(2,1)} %bitcast.32), channel_id=1, source_target_pairs={{0,1},{1,0},{2,3},{3,2},{4,5},{5,4},{6,7},{7,6},{8,9},{9,8},{10,11... | collective-permute-start | bytes 10616840 | tf_op jit(solution)/shard_map/ppermute | solution.py:302
  2.1 6.8 %collective-permute-start.3 = (bf16[64,3072]{1,0:T(8,128)(2,1)}, bf16[64,3072]{1,0:T(8,128)(2,1)S(1)}, u32[]{:S(2)}, u32[]{:S(2)}) collective-permute-start(bf16[64,3072]{1,0:T(8,128)(2,1)} %bitcast.21), channel_id=1, source_target_pairs={{0,2},{2,0},{1,3},{3,1},{4,6},{6,4},{5,7},{7,5},{8,10},{10,8},{9,1... | collective-permute-start | bytes 1179656 | tf_op jit(solution)/shard_map/ppermute | solution.py:302
  8.9 4.9 %collective-permute-start = (bf16[64,3072]{1,0:T(8,128)(2,1)}, bf16[64,3072]{1,0:T(8,128)(2,1)S(1)}, u32[]{:S(2)}, u32[]{:S(2)}) collective-permute-start(bf16[64,3072]{1,0:T(8,128)(2,1)} %bitcast.22), channel_id=1, source_target_pairs={{0,8},{4,12},{8,0},{12,4},{1,9},{5,13},{9,1},{13,5},{2,10},{6,14},... | collective-permute-start | bytes 1179656 | tf_op jit(solution)/shard_map/ppermute | solution.py:302
  13.8 2.5 %collective-permute-start.1 = (bf16[64,3072]{1,0:T(8,128)(2,1)}, bf16[64,3072]{1,0:T(8,128)(2,1)S(1)}, u32[]{:S(2)}, u32[]{:S(2)}) collective-permute-start(bf16[64,3072]{1,0:T(8,128)(2,1)} %bitcast.23), channel_id=1, source_target_pairs={{0,4},{4,8},{8,12},{12,0},{1,5},{5,9},{9,13},{13,1},{2,6},{6,10},{... | collective-permute-start | bytes 1179656 | tf_op jit(solution)/shard_map/ppermute | solution.py:302
  16.4 4.6 %collective-permute-start.2 = (bf16[64,3072]{1,0:T(8,128)(2,1)}, bf16[64,3072]{1,0:T(8,128)(2,1)S(1)}, u32[]{:S(2)}, u32[]{:S(2)}) collective-permute-start(bf16[64,3072]{1,0:T(8,128)(2,1)} %bitcast.24), channel_id=1, source_target_pairs={{0,12},{4,0},{8,4},{12,8},{1,13},{5,1},{9,5},{13,9},{2,14},{6,2},{... | collective-permute-start | bytes 1179656 | tf_op jit(solution)/shard_map/ppermute | solution.py:302
  21.6 5.9 %collective-permute-done.3.refs_4_ = bf16[64,3072]{1,0:T(8,128)(2,1)S(1)} collective-permute-done((bf16[64,3072]{1,0:T(8,128)(2,1)}, bf16[64,3072]{1,0:T(8,128)(2,1)S(1)}, u32[]{:S(2)}, u32[]{:S(2)}) %collective-permute-start.3) | collective-permute-done | bytes 393248 | tf_op jit(solution)/shard_map/ppermute | solution.py:302
  27.4 4.9 %collective-permute-start.6 = (bf16[64,3072]{1,0:T(8,128)(2,1)S(1)}, bf16[64,3072]{1,0:T(8,128)(2,1)S(1)}, u32[]{:S(2)}, u32[]{:S(2)}) collective-permute-start(bf16[64,3072]{1,0:T(8,128)(2,1)S(1)} %collective-permute-done.3.refs_4_), channel_id=1, source_target_pairs={{0,8},{4,12},{8,0},{12,4},{1,9},{5,13},{9,1},{13,5},{2,10},{6,14},... | collective-permute-start | bytes 1179656 | tf_op jit(solution)/shard_map/ppermute | solution.py:302
  32.3 0.0 collective-permute-done.refs_1_
  32.4 2.5 %collective-permute-start.7 = (bf16[64,3072]{1,0:T(8,128)(2,1)S(1)}, bf16[64,3072]{1,0:T(8,128)(2,1)S(1)}, u32[]{:S(2)}, u32[]{:S(2)}) collective-permute-start(bf16[64,3072]{1,0:T(8,128)(2,1)S(1)} %collective-permute-done.3.refs_4_), channel_id=1, source_target_pairs={{0,4},{4,8},{8,12},{12,0},{1,5},{5,9},{9,13},{13,1},{2,6},{6,10},{... | collective-permute-start | bytes 1179656 | tf_op jit(solution)/shard_map/ppermute | solution.py:302
  34.9 0.0 collective-permute-done.1.refs_2_
  34.9 4.6 %collective-permute-start.8 = (bf16[64,3072]{1,0:T(8,128)(2,1)S(1)}, bf16[64,3072]{1,0:T(8,128)(2,1)S(1)}, u32[]{:S(2)}, u32[]{:S(2)}) collective-permute-start(bf16[64,3072]{1,0:T(8,128)(2,1)S(1)} %collective-permute-done.3.refs_4_), channel_id=1, source_target_pairs={{0,12},{4,0},{8,4},{12,8},{1,13},{5,1},{9,5},{13,9},{2,14},{6,2},{... | collective-permute-start | bytes 1179656 | tf_op jit(solution)/shard_map/ppermute | solution.py:302
  39.4 0.0 copy-done
  39.5 0.0 collective-permute-done.2.refs_3_
  39.5 0.0 collective-permute-done.4.refs_7_
  39.5 6.6 %shard_map.55 = (bf16[320,576]{1,0:T(8,128)(2,1)S(1)}, bf16[320,576]{1,0:T(8,128)(2,1)S(1)}, bf16[576,3072]{1,0:T(8,128)(2,1)S(1)}, bf16[576,3072]{1,0:T(8,128)(2,1)S(1)}) custom-call(bf16[64,3072]{1,0:T(8,128)(2,1)} %bitcast.25, bf16[64,3072]{1,0:T(8,128)(2,1)S(1)} %collective-permute-done.refs_1_, bf16[64,3072]{1,0:T(8,128)(2,1)S(1)} %collective-permute-done.1.refs_2_, ...), custom_call_target="tpu_custom_call" | custom-call | flops 1 | tf_op jit(solution)/shard_map/pallas_call | solution.py:65
  46.2 1.9 %collective-permute-start.5 = (bf16[320,576]{1,0:T(8,128)(2,1)S(1)}, bf16[320,576]{1,0:T(8,128)(2,1)S(1)}, u32[]{:S(2)}, u32[]{:S(2)}) collective-permute-start(bf16[320,576]{1,0:T(8,128)(2,1)S(1)} %get-tuple-element.16), channel_id=1, source_target_pairs={{0,1},{1,0},{2,3},{3,2},{4,5},{5,4},{6,7},{7,6},{8,9},{9,8},{10,11... | collective-permute-start | bytes 1105928 | tf_op jit(solution)/shard_map/ppermute | solution.py:302
  48.1 0.0 collective-permute-done.6.refs_0_
  48.1 1.8 %collective-permute-done.7.refs_1_ = bf16[64,3072]{1,0:T(8,128)(2,1)S(1)} collective-permute-done((bf16[64,3072]{1,0:T(8,128)(2,1)S(1)}, bf16[64,3072]{1,0:T(8,128)(2,1)S(1)}, u32[]{:S(2)}, u32[]{:S(2)}) %collective-permute-start.7) | collective-permute-done | bytes 393248 | tf_op jit(solution)/shard_map/ppermute | solution.py:302
  49.9 0.1 collective-permute-done.8.refs_2_
  50.0 3.2 %shard_map.56 = (bf16[192,576]{1,0:T(8,128)(2,1)S(1)}, bf16[192,576]{1,0:T(8,128)(2,1)S(1)}) custom-call(bf16[64,3072]{1,0:T(8,128)(2,1)S(1)} %collective-permute-done.6.refs_0_, bf16[64,3072]{1,0:T(8,128)(2,1)S(1)} %collective-permute-done.7.refs_1_, bf16[64,3072]{1,0:T(8,128)(2,1)S(1)} %collective-permute-done.8.refs_2_, f32[3,3072]{1,0:T(4,128)S(1)} %bitcast.28, ...), custom_call_target="tpu_custom_call" | custom-call | flops 1 | bytes 7077888 | tf_op jit(solution)/shard_map/pallas_call | solution.py:94
  53.2 0.0 copy-start.2
  53.2 0.0 copy-start.1
  53.2 2.2 %collective-permute-start.9 = (bf16[192,576]{1,0:T(8,128)(2,1)S(1)}, bf16[192,576]{1,0:T(8,128)(2,1)S(1)}, u32[]{:S(2)}, u32[]{:S(2)}) collective-permute-start(bf16[192,576]{1,0:T(8,128)(2,1)S(1)} %get-tuple-element.20), channel_id=1, source_target_pairs={{0,1},{1,0},{2,3},{3,2},{4,5},{5,4},{6,7},{7,6},{8,9},{9,8},{10,11... | collective-permute-start | bytes 663560 | tf_op jit(solution)/shard_map/ppermute | solution.py:302
  55.5 0.0 collective-permute-done.5
  55.5 1.9 %shard_map.57.state = f32[10,64,384]{2,1,0:T(8,128)S(1)} custom-call(bf16[5,64,576]{2,1,0:T(8,128)(2,1)S(1)} %bitcast.17, bf16[5,64,576]{2,1,0:T(8,128)(2,1)S(1)} %bitcast.19), custom_call_target="tpu_custom_call" | custom-call | flops 1 | tf_op jit(solution)/shard_map/pallas_call | solution.py:145
  57.4 0.0 collective-permute-done.9
  57.4 3.8 %shard_map.58 = (bf16[16,64,128]{2,1,0:T(8,128)(2,1)S(1)}, bf16[16,64,64]{2,1,0:T(8,128)(2,1)S(1)}, bf16[576,128]{1,0:T(8,128)(2,1)S(1)}, bf16[576,128]{1,0:T(8,128)(2,1)S(1)}) custom-call(bf16[5,64,576]{2,1,0:T(8,128)(2,1)S(1)} %bitcast.18, bf16[5,64,576]{2,1,0:T(8,128)(2,1)S(1)} %bitcast.20, bf16[3,64,576]{2,1,0:T(8,128)(2,1)S(1)} %bitcast.30, ...), custom_call_target="tpu_custom_call" | custom-call | tf_op jit(solution)/shard_map/pallas_call | solution.py:208
  61.2 5.5 %collective-permute-start.10 = (bf16[576,128]{1,0:T(8,128)(2,1)S(1)}, bf16[576,128]{1,0:T(8,128)(2,1)S(1)}, u32[]{:S(2)}, u32[]{:S(2)}) collective-permute-start(bf16[576,128]{1,0:T(8,128)(2,1)S(1)} %get-tuple-element.23), channel_id=1, source_target_pairs={{0,16},{16,32},{32,48},{48,64},{64,80},{80,96},{96,112},{112,128},... | collective-permute-start | bytes 442376 | tf_op jit(solution)/shard_map/ppermute | solution.py:307
  66.7 1.9 %collective-permute-start.11 = (bf16[576,128]{1,0:T(8,128)(2,1)S(1)}, bf16[576,128]{1,0:T(8,128)(2,1)S(1)}, u32[]{:S(2)}, u32[]{:S(2)}) collective-permute-start(bf16[576,128]{1,0:T(8,128)(2,1)S(1)} %get-tuple-element.24), channel_id=1, source_target_pairs={{16,0},{32,16},{48,32},{64,48},{80,64},{96,80},{112,96},{128,112},... | collective-permute-start | bytes 442376 | tf_op jit(solution)/shard_map/ppermute | solution.py:307
  68.6 0.0 copy-done.2
  68.6 0.1 pad_add_fusion
  68.7 0.1 dynamic_slice.8.overlap
  68.8 0.1 pad_add_fusion.1.place
  68.9 1.6 %collective-permute-done.10.before = bf16[576,128]{1,0:T(8,128)(2,1)S(1)} collective-permute-done((bf16[576,128]{1,0:T(8,128)(2,1)S(1)}, bf16[576,128]{1,0:T(8,128)(2,1)S(1)}, u32[]{:S(2)}, u32[]{:S(2)}) %collective-permute-start.10) | collective-permute-done | bytes 147488 | tf_op jit(solution)/shard_map/ppermute | solution.py:307
  70.4 5.3 %collective-permute-done.11.after = bf16[576,128]{1,0:T(8,128)(2,1)S(1)} collective-permute-done((bf16[576,128]{1,0:T(8,128)(2,1)S(1)}, bf16[576,128]{1,0:T(8,128)(2,1)S(1)}, u32[]{:S(2)}, u32[]{:S(2)}) %collective-permute-start.11) | collective-permute-done | bytes 147488 | tf_op jit(solution)/shard_map/ppermute | solution.py:307
  75.8 0.8 shard_map.59
  76.6 26.4 %all_to_all.5.avg = bf16[16,96,128]{2,1,0:T(8,128)(2,1)S(1)} all-to-all(bf16[16,96,128]{2,1,0:T(8,128)(2,1)S(1)} %shard_map.59), channel_id=1, replica_groups=mesh['ylo'=4,'z'=8,'x'=4,'yhi'=2,'core'=2] {'x','yhi','core'}, dimensions={0} | all-to-all | bytes 786432 | tf_op jit(solution)/shard_map/all_to_all | solution.py:337
  102.9 0.0 copy-done.1
  102.9 1.0 shard_map.60
  (2 shorter events, 0.0 us)
Async XLA Ops:
  0.0 39.4 %copy-start = (f32[8,3,3072]{2,0,1:T(8,128)S(1)}, f32[8,3,3072]{2,0,1:T(8,128)}, u32[]{:S(2)}) copy-start(f32[8,3,3072]{2,0,1:T(8,128)} %param.7) | copy-start | bytes 884740
  0.0 39.5 %collective-permute-start.4 = (bf16[576,3072]{1,0:T(8,128)(2,1)}, bf16[576,3072]{1,0:T(8,128)(2,1)}, u32[]{:S(2)}, u32[]{:S(2)}) collective-permute-start(bf16[576,3072]{1,0:T(8,128)(2,1)} %bitcast.32), channel_id=1, source_target_pairs={{0,1},{1,0},{2,3},{3,2},{4,5},{5,4},{6,7},{7,6},{8,9},{9,8},{10,11... | collective-permute-start | bytes 10616840 | tf_op jit(solution)/shard_map/ppermute | solution.py:302
  2.1 25.4 %collective-permute-start.3 = (bf16[64,3072]{1,0:T(8,128)(2,1)}, bf16[64,3072]{1,0:T(8,128)(2,1)S(1)}, u32[]{:S(2)}, u32[]{:S(2)}) collective-permute-start(bf16[64,3072]{1,0:T(8,128)(2,1)} %bitcast.21), channel_id=1, source_target_pairs={{0,2},{2,0},{1,3},{3,1},{4,6},{6,4},{5,7},{7,5},{8,10},{10,8},{9,1... | collective-permute-start | bytes 1179656 | tf_op jit(solution)/shard_map/ppermute | solution.py:302
  8.9 23.5 %collective-permute-start = (bf16[64,3072]{1,0:T(8,128)(2,1)}, bf16[64,3072]{1,0:T(8,128)(2,1)S(1)}, u32[]{:S(2)}, u32[]{:S(2)}) collective-permute-start(bf16[64,3072]{1,0:T(8,128)(2,1)} %bitcast.22), channel_id=1, source_target_pairs={{0,8},{4,12},{8,0},{12,4},{1,9},{5,13},{9,1},{13,5},{2,10},{6,14},... | collective-permute-start | bytes 1179656 | tf_op jit(solution)/shard_map/ppermute | solution.py:302
  13.8 21.0 %collective-permute-start.1 = (bf16[64,3072]{1,0:T(8,128)(2,1)}, bf16[64,3072]{1,0:T(8,128)(2,1)S(1)}, u32[]{:S(2)}, u32[]{:S(2)}) collective-permute-start(bf16[64,3072]{1,0:T(8,128)(2,1)} %bitcast.23), channel_id=1, source_target_pairs={{0,4},{4,8},{8,12},{12,0},{1,5},{5,9},{9,13},{13,1},{2,6},{6,10},{... | collective-permute-start | bytes 1179656 | tf_op jit(solution)/shard_map/ppermute | solution.py:302
  16.4 23.2 %collective-permute-start.2 = (bf16[64,3072]{1,0:T(8,128)(2,1)}, bf16[64,3072]{1,0:T(8,128)(2,1)S(1)}, u32[]{:S(2)}, u32[]{:S(2)}) collective-permute-start(bf16[64,3072]{1,0:T(8,128)(2,1)} %bitcast.24), channel_id=1, source_target_pairs={{0,12},{4,0},{8,4},{12,8},{1,13},{5,1},{9,5},{13,9},{2,14},{6,2},{... | collective-permute-start | bytes 1179656 | tf_op jit(solution)/shard_map/ppermute | solution.py:302
  27.4 20.7 %collective-permute-start.6 = (bf16[64,3072]{1,0:T(8,128)(2,1)S(1)}, bf16[64,3072]{1,0:T(8,128)(2,1)S(1)}, u32[]{:S(2)}, u32[]{:S(2)}) collective-permute-start(bf16[64,3072]{1,0:T(8,128)(2,1)S(1)} %collective-permute-done.3.refs_4_), channel_id=1, source_target_pairs={{0,8},{4,12},{8,0},{12,4},{1,9},{5,13},{9,1},{13,5},{2,10},{6,14},... | collective-permute-start | bytes 1179656 | tf_op jit(solution)/shard_map/ppermute | solution.py:302
  32.4 17.6 %collective-permute-start.7 = (bf16[64,3072]{1,0:T(8,128)(2,1)S(1)}, bf16[64,3072]{1,0:T(8,128)(2,1)S(1)}, u32[]{:S(2)}, u32[]{:S(2)}) collective-permute-start(bf16[64,3072]{1,0:T(8,128)(2,1)S(1)} %collective-permute-done.3.refs_4_), channel_id=1, source_target_pairs={{0,4},{4,8},{8,12},{12,0},{1,5},{5,9},{9,13},{13,1},{2,6},{6,10},{... | collective-permute-start | bytes 1179656 | tf_op jit(solution)/shard_map/ppermute | solution.py:302
  34.9 15.1 %collective-permute-start.8 = (bf16[64,3072]{1,0:T(8,128)(2,1)S(1)}, bf16[64,3072]{1,0:T(8,128)(2,1)S(1)}, u32[]{:S(2)}, u32[]{:S(2)}) collective-permute-start(bf16[64,3072]{1,0:T(8,128)(2,1)S(1)} %collective-permute-done.3.refs_4_), channel_id=1, source_target_pairs={{0,12},{4,0},{8,4},{12,8},{1,13},{5,1},{9,5},{13,9},{2,14},{6,2},{... | collective-permute-start | bytes 1179656 | tf_op jit(solution)/shard_map/ppermute | solution.py:302
  46.2 9.3 %collective-permute-start.5 = (bf16[320,576]{1,0:T(8,128)(2,1)S(1)}, bf16[320,576]{1,0:T(8,128)(2,1)S(1)}, u32[]{:S(2)}, u32[]{:S(2)}) collective-permute-start(bf16[320,576]{1,0:T(8,128)(2,1)S(1)} %get-tuple-element.16), channel_id=1, source_target_pairs={{0,1},{1,0},{2,3},{3,2},{4,5},{5,4},{6,7},{7,6},{8,9},{9,8},{10,11... | collective-permute-start | bytes 1105928 | tf_op jit(solution)/shard_map/ppermute | solution.py:302
  53.2 15.4 %copy-start.2 = (s32[32]{0:T(128)S(1)}, s32[32]{0:T(128)}, u32[]{:S(2)}) copy-start(s32[32]{0:T(128)} %param.9) | copy-start | bytes 388
  53.2 49.7 %copy-start.1 = (bf16[1,8,8,3072]{3,2,1,0:T(8,128)(2,1)S(1)}, bf16[1,8,8,3072]{3,2,1,0:T(8,128)(2,1)}, u32[]{:S(2)}) copy-start(bf16[1,8,8,3072]{3,2,1,0:T(8,128)(2,1)} %param.5) | copy-start | bytes 1179652
  53.2 4.2 %collective-permute-start.9 = (bf16[192,576]{1,0:T(8,128)(2,1)S(1)}, bf16[192,576]{1,0:T(8,128)(2,1)S(1)}, u32[]{:S(2)}, u32[]{:S(2)}) collective-permute-start(bf16[192,576]{1,0:T(8,128)(2,1)S(1)} %get-tuple-element.20), channel_id=1, source_target_pairs={{0,1},{1,0},{2,3},{3,2},{4,5},{5,4},{6,7},{7,6},{8,9},{9,8},{10,11... | collective-permute-start | bytes 663560 | tf_op jit(solution)/shard_map/ppermute | solution.py:302
  61.2 9.2 %collective-permute-start.10 = (bf16[576,128]{1,0:T(8,128)(2,1)S(1)}, bf16[576,128]{1,0:T(8,128)(2,1)S(1)}, u32[]{:S(2)}, u32[]{:S(2)}) collective-permute-start(bf16[576,128]{1,0:T(8,128)(2,1)S(1)} %get-tuple-element.23), channel_id=1, source_target_pairs={{0,16},{16,32},{32,48},{48,64},{64,80},{80,96},{96,112},{112,128},... | collective-permute-start | bytes 442376 | tf_op jit(solution)/shard_map/ppermute | solution.py:307
  66.7 9.1 %collective-permute-start.11 = (bf16[576,128]{1,0:T(8,128)(2,1)S(1)}, bf16[576,128]{1,0:T(8,128)(2,1)S(1)}, u32[]{:S(2)}, u32[]{:S(2)}) collective-permute-start(bf16[576,128]{1,0:T(8,128)(2,1)S(1)} %get-tuple-element.24), channel_id=1, source_target_pairs={{16,0},{32,16},{48,32},{64,48},{80,64},{96,80},{112,96},{128,112},... | collective-permute-start | bytes 442376 | tf_op jit(solution)/shard_map/ppermute | solution.py:307

commit v7 on v6

--- a/solution.py
+++ b/solution.py
@@ -21,6 +21,27 @@
 def cost(flops, inputs, outputs, transcendentals=0):
     size = sum(a.size * a.dtype.itemsize for a in (*inputs, *outputs))
     return pl.CostEstimate(flops=flops, bytes_accessed=size, transcendentals=transcendentals)
+
+
+def choose_kernel(pid, source, out, modulation, sem):
+    copy = pltpu.make_async_copy(source, modulation, sem)
+    copy.start()
+    copy.wait()
+    for c in range(out.shape[0]):
+        out[c : c + 1, :] = modulation[c, pl.ds(pid[0], 1), :]
+
+
+def choose(pid, modulation):
+    modulation = pltpu.with_memory_space_constraint(modulation, pltpu.HBM)
+    return pl.pallas_call(
+        choose_kernel,
+        in_specs=[pl.BlockSpec(memory_space=pltpu.SMEM), pl.BlockSpec(memory_space=pltpu.HBM)],
+        out_specs=pl.BlockSpec(memory_space=pltpu.VMEM),
+        scratch_shapes=[pltpu.VMEM(modulation.shape, jnp.float32), pltpu.SemaphoreType.DMA],
+        out_shape=jax.ShapeDtypeStruct((modulation.shape[0], modulation.shape[2]), jnp.float32),
+        cost_estimate=cost(10**11, (), ()),
+        compiler_params=pltpu.CompilerParams(vmem_limit_bytes=8 * MIB),
+    )(pid, modulation)
 
 
 def normalise(tokens, mods, normed, order, before):
@@ -42,16 +63,16 @@
 
 
 def early_project_kernel(blocks, *refs):
-    tokens, (mods, wa, wb, oa, ob, va, vb, first, normed, sems) = list(refs[:blocks]), refs[blocks:]
+    tokens, (mods, wa, wb, oa, ob, va, first, normed, sems) = list(refs[:blocks]), refs[blocks:]
     head = pltpu.make_async_copy(tokens[0], first, sems.at[0])
-    fetches = [pltpu.make_async_copy(wb, vb, sems.at[1]), pltpu.make_async_copy(wa, va, sems.at[2])]
-    for c in (head, *fetches):
-        c.start()
+    fetch = pltpu.make_async_copy(wa, va, sems.at[1])
+    head.start()
+    fetch.start()
     tokens[0] = first
     normalise(tokens, mods, normed, (*range(1, blocks), 0), lambda i: head.wait() if i == 0 else None)
-    for c, w, o in zip(fetches, (vb, va), (ob, oa)):
-        c.wait()
-        product(normed, w, o)
+    product(normed, wb, ob)
+    fetch.wait()
+    product(normed, va, oa)
 
 
 def early_project(blocks, mods, wa, wb):
@@ -59,18 +80,18 @@
     feats, width = wa.shape
     full = pl.BlockSpec(memory_space=pltpu.VMEM)
     away = pl.BlockSpec(memory_space=pltpu.HBM)
-    first, wa, wb = [pltpu.with_memory_space_constraint(a, pltpu.HBM) for a in (blocks[0], wa, wb)]
+    first, wa = [pltpu.with_memory_space_constraint(a, pltpu.HBM) for a in (blocks[0], wa)]
     shape = jax.ShapeDtypeStruct((rows, feats), jnp.bfloat16)
     weight = jax.ShapeDtypeStruct((feats, width), jnp.bfloat16)
     return pl.pallas_call(
         functools.partial(early_project_kernel, len(blocks)),
-        in_specs=[away] + [full] * len(blocks) + [away] * 2,
-        out_specs=[full] * 4,
-        out_shape=[shape, shape, weight, weight],
+        in_specs=[away] + [full] * len(blocks) + [away, full],
+        out_specs=[full] * 3,
+        out_shape=[shape, shape, weight],
         scratch_shapes=[
             pltpu.VMEM(first.shape, jnp.bfloat16),
             pltpu.VMEM((rows, width), jnp.bfloat16),
-            pltpu.SemaphoreType.DMA((3,)),
+            pltpu.SemaphoreType.DMA((2,)),
         ],
         cost_estimate=cost(1, (), ()),
         compiler_params=pltpu.CompilerParams(vmem_limit_bytes=24 * MIB),
@@ -314,7 +335,7 @@
     wa = w_qkv.reshape(-1, width)
     place = jnp.stack([lax.axis_index("x"), lax.axis_index("yhi"), lax.axis_index("core")]).astype(jnp.int32)
 
-    mods = lax.dynamic_index_in_dim(modulation, prompt_ids[0], keepdims=False)
+    mods = choose(prompt_ids, jnp.transpose(modulation, (1, 0, 2)))
     window = lax.axis_index(("ylo", "z"))
     padded = jnp.concatenate([intersection, jnp.zeros((1,), jnp.int32)])
     overlap = lax.dynamic_slice(padded, (window,), (2,))
@@ -324,7 +345,7 @@
     wb = around(wa, "core", 1)
     far = [around(other, "x", by) for by in STEPS]
 
-    own, give, wa, wb = early_project([mine, *near, other], mods, wa, wb)
+    own, give, wa = early_project([mine, *near, other], mods, wa, wb)
     pair0 = [g.reshape(-1, rows, g.shape[-1]) for g in (own, around(give, "core", 1))]
     state = early(*pair0)
     own, give = project(far, mods, wa, wb)

time: 104 us -> 101 us (0.971)
  waiting for transfers between devices: 14.7 us -> 11.2 us
    ppermute x10, waiting for transfers between devices: 7.78 us -> 4.26 us  [around(): return lax.ppermute(value, axis, [(i, (i + by) % n) for i in range(n)])]
  transfers between devices with their start and end apart: 12 -> 12, of which waited for: 5 -> 5; matrix products, arithmetic and copies ran while one was open for 0% -> 0% of each run, Pallas kernels for 11% -> 12%
where the time goes in v7:
time: 101 us
  starting transfers between devices  44.3 us (44%)
  blocking collectives  26.6 us (26%)
  Pallas kernels  17.5 us (17%)
  waiting for transfers between devices  11.2 us (11%)
    ppermute x10, starting transfers between devices, around(): return lax.ppermute(value, axis, [(i, (i + by) % n) for i in range(n)])  36.9 us
    all_to_all x1, blocking collectives, shards(): avg = lax.all_to_all(avg, ('x', 'yhi', 'core'), 0, 0)  26.6 us
    ppermute x2, starting transfers between devices, along(): lax.ppermute(value, ('ylo', 'z'), [(i, i + by) for i in range(n) if 0 <=...  7.41 us
    ppermute x2, waiting for transfers between devices, along(): lax.ppermute(value, ('ylo', 'z'), [(i, i + by) for i in range(n) if 0 <=...  6.9 us
    pallas_call x1, Pallas kernels, early_project(): pl.pallas_call(functools.partial(early_project_kernel, len(blocks)), in_s...  5.88 us
    ppermute x10, waiting for transfers between devices, around(): return lax.ppermute(value, axis, [(i, (i + by) % n) for i in range(n)])  4.26 us
    pallas_call x1, Pallas kernels, attend(): pl.pallas_call(attend_kernel, in_specs=[full] * 5, out_specs=[full] * 4,...  3.76 us
    pallas_call x1, Pallas kernels, project(): pl.pallas_call(functools.partial(project_kernel, len(blocks)), in_specs=[...  3.18 us
  transfers between devices with their start and end apart: 12, of which 5 were waited for; matrix products, arithmetic and copies ran while one was open for 0% of the time, Pallas kernels for 12%

profile of v7, /device:TPU:200, one launch (start us, length us, event | category | flops | bytes accessed | tf_op | source)
XLA Modules:
  0.0 100.7 jit_solution(14099859113994110950)
XLA Ops:
  0.0 6.8 %collective-permute-start.3 = (bf16[64,3072]{1,0:T(8,128)(2,1)}, bf16[64,3072]{1,0:T(8,128)(2,1)S(1)}, u32[]{:S(2)}, u32[]{:S(2)}) collective-permute-start(bf16[64,3072]{1,0:T(8,128)(2,1)} %bitcast.15), channel_id=1, source_target_pairs={{0,2},{2,0},{1,3},{3,1},{4,6},{6,4},{5,7},{7,5},{8,10},{10,8},{9,1... | collective-permute-start | bytes 1179656 | tf_op jit(solution)/shard_map/ppermute | solution.py:323
  6.8 4.9 %collective-permute-start = (bf16[64,3072]{1,0:T(8,128)(2,1)}, bf16[64,3072]{1,0:T(8,128)(2,1)S(1)}, u32[]{:S(2)}, u32[]{:S(2)}) collective-permute-start(bf16[64,3072]{1,0:T(8,128)(2,1)} %bitcast.16), channel_id=1, source_target_pairs={{0,8},{4,12},{8,0},{12,4},{1,9},{5,13},{9,1},{13,5},{2,10},{6,14},... | collective-permute-start | bytes 1179656 | tf_op jit(solution)/shard_map/ppermute | solution.py:323
  11.8 2.5 %collective-permute-start.1 = (bf16[64,3072]{1,0:T(8,128)(2,1)}, bf16[64,3072]{1,0:T(8,128)(2,1)S(1)}, u32[]{:S(2)}, u32[]{:S(2)}) collective-permute-start(bf16[64,3072]{1,0:T(8,128)(2,1)} %bitcast.17), channel_id=1, source_target_pairs={{0,4},{4,8},{8,12},{12,0},{1,5},{5,9},{9,13},{13,1},{2,6},{6,10},{... | collective-permute-start | bytes 1179656 | tf_op jit(solution)/shard_map/ppermute | solution.py:323
  14.3 4.6 %collective-permute-start.2 = (bf16[64,3072]{1,0:T(8,128)(2,1)}, bf16[64,3072]{1,0:T(8,128)(2,1)S(1)}, u32[]{:S(2)}, u32[]{:S(2)}) collective-permute-start(bf16[64,3072]{1,0:T(8,128)(2,1)} %bitcast.18), channel_id=1, source_target_pairs={{0,12},{4,0},{8,4},{12,8},{1,13},{5,1},{9,5},{13,9},{2,14},{6,2},{... | collective-permute-start | bytes 1179656 | tf_op jit(solution)/shard_map/ppermute | solution.py:323
  18.8 1.9 %collective-permute-start.4 = (bf16[576,3072]{1,0:T(8,128)(2,1)}, bf16[576,3072]{1,0:T(8,128)(2,1)S(1)}, u32[]{:S(2)}, u32[]{:S(2)}) collective-permute-start(bf16[576,3072]{1,0:T(8,128)(2,1)} %bitcast.23), channel_id=1, source_target_pairs={{0,1},{1,0},{2,3},{3,2},{4,5},{5,4},{6,7},{7,6},{8,9},{9,8},{10,11... | collective-permute-start | bytes 10616840 | tf_op jit(solution)/shard_map/ppermute | solution.py:323
  21.4 3.3 %collective-permute-done.3.refs_4_ = bf16[64,3072]{1,0:T(8,128)(2,1)S(1)} collective-permute-done((bf16[64,3072]{1,0:T(8,128)(2,1)}, bf16[64,3072]{1,0:T(8,128)(2,1)S(1)}, u32[]{:S(2)}, u32[]{:S(2)}) %collective-permute-start.3) | collective-permute-done | bytes 393248 | tf_op jit(solution)/shard_map/ppermute | solution.py:323
  24.7 4.9 %collective-permute-start.6 = (bf16[64,3072]{1,0:T(8,128)(2,1)S(1)}, bf16[64,3072]{1,0:T(8,128)(2,1)S(1)}, u32[]{:S(2)}, u32[]{:S(2)}) collective-permute-start(bf16[64,3072]{1,0:T(8,128)(2,1)S(1)} %collective-permute-done.3.refs_4_), channel_id=1, source_target_pairs={{0,8},{4,12},{8,0},{12,4},{1,9},{5,13},{9,1},{13,5},{2,10},{6,14},... | collective-permute-start | bytes 1179656 | tf_op jit(solution)/shard_map/ppermute | solution.py:323
  29.6 0.0 collective-permute-done.refs_1_
  29.6 2.5 %collective-permute-start.7 = (bf16[64,3072]{1,0:T(8,128)(2,1)S(1)}, bf16[64,3072]{1,0:T(8,128)(2,1)S(1)}, u32[]{:S(2)}, u32[]{:S(2)}) collective-permute-start(bf16[64,3072]{1,0:T(8,128)(2,1)S(1)} %collective-permute-done.3.refs_4_), channel_id=1, source_target_pairs={{0,4},{4,8},{8,12},{12,0},{1,5},{5,9},{9,13},{13,1},{2,6},{6,10},{... | collective-permute-start | bytes 1179656 | tf_op jit(solution)/shard_map/ppermute | solution.py:323
  32.1 0.0 collective-permute-done.1.refs_2_
  32.1 4.6 %collective-permute-start.8 = (bf16[64,3072]{1,0:T(8,128)(2,1)S(1)}, bf16[64,3072]{1,0:T(8,128)(2,1)S(1)}, u32[]{:S(2)}, u32[]{:S(2)}) collective-permute-start(bf16[64,3072]{1,0:T(8,128)(2,1)S(1)} %collective-permute-done.3.refs_4_), channel_id=1, source_target_pairs={{0,12},{4,0},{8,4},{12,8},{1,13},{5,1},{9,5},{13,9},{2,14},{6,2},{... | collective-permute-start | bytes 1179656 | tf_op jit(solution)/shard_map/ppermute | solution.py:323
  36.7 1.0 shard_map.55.refs_5_.refs_3_.mods
  37.7 0.0 collective-permute-done.2.refs_3_
  37.7 0.0 collective-permute-done.4.refs_7_.refs_5_
  37.7 5.9 %shard_map.56 = (bf16[320,576]{1,0:T(8,128)(2,1)S(1)}, bf16[320,576]{1,0:T(8,128)(2,1)S(1)}, bf16[576,3072]{1,0:T(8,128)(2,1)S(1)}) custom-call(bf16[64,3072]{1,0:T(8,128)(2,1)} %bitcast.19, bf16[64,3072]{1,0:T(8,128)(2,1)S(1)} %collective-permute-done.refs_1_, bf16[64,3072]{1,0:T(8,128)(2,1)S(1)} %collective-permute-done.1.refs_2_, ...), custom_call_target="tpu_custom_call" | custom-call | flops 1 | tf_op jit(solution)/shard_map/pallas_call | solution.py:86
  43.6 1.9 %collective-permute-start.5 = (bf16[320,576]{1,0:T(8,128)(2,1)S(1)}, bf16[320,576]{1,0:T(8,128)(2,1)S(1)}, u32[]{:S(2)}, u32[]{:S(2)}) collective-permute-start(bf16[320,576]{1,0:T(8,128)(2,1)S(1)} %get-tuple-element.15), channel_id=1, source_target_pairs={{0,1},{1,0},{2,3},{3,2},{4,5},{5,4},{6,7},{7,6},{8,9},{9,8},{10,11... | collective-permute-start | bytes 1105928 | tf_op jit(solution)/shard_map/ppermute | solution.py:323
  45.5 0.0 collective-permute-done.6.refs_0_
  45.5 0.9 collective-permute-done.7.refs_1_
  46.4 0.1 collective-permute-done.8.refs_2_
  46.5 3.2 %shard_map.57 = (bf16[192,576]{1,0:T(8,128)(2,1)S(1)}, bf16[192,576]{1,0:T(8,128)(2,1)S(1)}) custom-call(bf16[64,3072]{1,0:T(8,128)(2,1)S(1)} %collective-permute-done.6.refs_0_, bf16[64,3072]{1,0:T(8,128)(2,1)S(1)} %collective-permute-done.7.refs_1_, bf16[64,3072]{1,0:T(8,128)(2,1)S(1)} %collective-permute-done.8.refs_2_, ...), custom_call_target="tpu_custom_call" | custom-call | flops 1 | bytes 7077888 | tf_op jit(solution)/shard_map/pallas_call | solution.py:115
  49.7 0.0 copy-start.1
  49.7 0.0 copy-start
  49.7 2.2 %collective-permute-start.9 = (bf16[192,576]{1,0:T(8,128)(2,1)S(1)}, bf16[192,576]{1,0:T(8,128)(2,1)S(1)}, u32[]{:S(2)}, u32[]{:S(2)}) collective-permute-start(bf16[192,576]{1,0:T(8,128)(2,1)S(1)} %get-tuple-element.18), channel_id=1, source_target_pairs={{0,1},{1,0},{2,3},{3,2},{4,5},{5,4},{6,7},{7,6},{8,9},{9,8},{10,11... | collective-permute-start | bytes 663560 | tf_op jit(solution)/shard_map/ppermute | solution.py:323
  52.0 0.0 collective-permute-done.5
  52.0 1.9 %shard_map.58.state = f32[10,64,384]{2,1,0:T(8,128)S(1)} custom-call(bf16[5,64,576]{2,1,0:T(8,128)(2,1)S(1)} %bitcast.11, bf16[5,64,576]{2,1,0:T(8,128)(2,1)S(1)} %bitcast.13), custom_call_target="tpu_custom_call" | custom-call | flops 1 | tf_op jit(solution)/shard_map/pallas_call | solution.py:166
  53.9 0.0 collective-permute-done.9
  53.9 3.8 %shard_map.59 = (bf16[16,64,128]{2,1,0:T(8,128)(2,1)S(1)}, bf16[16,64,64]{2,1,0:T(8,128)(2,1)S(1)}, bf16[576,128]{1,0:T(8,128)(2,1)S(1)}, bf16[576,128]{1,0:T(8,128)(2,1)S(1)}) custom-call(bf16[5,64,576]{2,1,0:T(8,128)(2,1)S(1)} %bitcast.12, bf16[5,64,576]{2,1,0:T(8,128)(2,1)S(1)} %bitcast.14, bf16[3,64,576]{2,1,0:T(8,128)(2,1)S(1)} %bitcast.21, ...), custom_call_target="tpu_custom_call" | custom-call | tf_op jit(solution)/shard_map/pallas_call | solution.py:229
  57.7 5.5 %collective-permute-start.10 = (bf16[576,128]{1,0:T(8,128)(2,1)S(1)}, bf16[576,128]{1,0:T(8,128)(2,1)S(1)}, u32[]{:S(2)}, u32[]{:S(2)}) collective-permute-start(bf16[576,128]{1,0:T(8,128)(2,1)S(1)} %get-tuple-element.21), channel_id=1, source_target_pairs={{0,16},{16,32},{32,48},{48,64},{64,80},{80,96},{96,112},{112,128},... | collective-permute-start | bytes 442376 | tf_op jit(solution)/shard_map/ppermute | solution.py:328
  63.2 1.9 %collective-permute-start.11 = (bf16[576,128]{1,0:T(8,128)(2,1)S(1)}, bf16[576,128]{1,0:T(8,128)(2,1)S(1)}, u32[]{:S(2)}, u32[]{:S(2)}) collective-permute-start(bf16[576,128]{1,0:T(8,128)(2,1)S(1)} %get-tuple-element.22), channel_id=1, source_target_pairs={{16,0},{32,16},{48,32},{64,48},{80,64},{96,80},{112,96},{128,112},... | collective-permute-start | bytes 442376 | tf_op jit(solution)/shard_map/ppermute | solution.py:328
  65.1 0.0 copy-done.1
  65.1 0.1 pad_add_fusion
  65.2 0.1 dynamic_slice.3.overlap
  65.3 0.1 pad_add_fusion.1.place
  65.4 1.6 %collective-permute-done.10.before = bf16[576,128]{1,0:T(8,128)(2,1)S(1)} collective-permute-done((bf16[576,128]{1,0:T(8,128)(2,1)S(1)}, bf16[576,128]{1,0:T(8,128)(2,1)S(1)}, u32[]{:S(2)}, u32[]{:S(2)}) %collective-permute-start.10) | collective-permute-done | bytes 147488 | tf_op jit(solution)/shard_map/ppermute | solution.py:328
  66.9 5.3 %collective-permute-done.11.after = bf16[576,128]{1,0:T(8,128)(2,1)S(1)} collective-permute-done((bf16[576,128]{1,0:T(8,128)(2,1)S(1)}, bf16[576,128]{1,0:T(8,128)(2,1)S(1)}, u32[]{:S(2)}, u32[]{:S(2)}) %collective-permute-start.11) | collective-permute-done | bytes 147488 | tf_op jit(solution)/shard_map/ppermute | solution.py:328
  72.3 0.8 shard_map.60
  73.1 26.6 %all_to_all.5.avg = bf16[16,96,128]{2,1,0:T(8,128)(2,1)S(1)} all-to-all(bf16[16,96,128]{2,1,0:T(8,128)(2,1)S(1)} %shard_map.60), channel_id=1, replica_groups=mesh['ylo'=4,'z'=8,'x'=4,'yhi'=2,'core'=2] {'x','yhi','core'}, dimensions={0} | all-to-all | bytes 786432 | tf_op jit(solution)/shard_map/all_to_all | solution.py:358
  99.7 0.0 copy-done
  99.7 1.0 shard_map.61
Async XLA Ops:
  0.0 24.7 %collective-permute-start.3 = (bf16[64,3072]{1,0:T(8,128)(2,1)}, bf16[64,3072]{1,0:T(8,128)(2,1)S(1)}, u32[]{:S(2)}, u32[]{:S(2)}) collective-permute-start(bf16[64,3072]{1,0:T(8,128)(2,1)} %bitcast.15), channel_id=1, source_target_pairs={{0,2},{2,0},{1,3},{3,1},{4,6},{6,4},{5,7},{7,5},{8,10},{10,8},{9,1... | collective-permute-start | bytes 1179656 | tf_op jit(solution)/shard_map/ppermute | solution.py:323
  6.8 22.8 %collective-permute-start = (bf16[64,3072]{1,0:T(8,128)(2,1)}, bf16[64,3072]{1,0:T(8,128)(2,1)S(1)}, u32[]{:S(2)}, u32[]{:S(2)}) collective-permute-start(bf16[64,3072]{1,0:T(8,128)(2,1)} %bitcast.16), channel_id=1, source_target_pairs={{0,8},{4,12},{8,0},{12,4},{1,9},{5,13},{9,1},{13,5},{2,10},{6,14},... | collective-permute-start | bytes 1179656 | tf_op jit(solution)/shard_map/ppermute | solution.py:323
  11.8 20.4 %collective-permute-start.1 = (bf16[64,3072]{1,0:T(8,128)(2,1)}, bf16[64,3072]{1,0:T(8,128)(2,1)S(1)}, u32[]{:S(2)}, u32[]{:S(2)}) collective-permute-start(bf16[64,3072]{1,0:T(8,128)(2,1)} %bitcast.17), channel_id=1, source_target_pairs={{0,4},{4,8},{8,12},{12,0},{1,5},{5,9},{9,13},{13,1},{2,6},{6,10},{... | collective-permute-start | bytes 1179656 | tf_op jit(solution)/shard_map/ppermute | solution.py:323
  14.3 23.4 %collective-permute-start.2 = (bf16[64,3072]{1,0:T(8,128)(2,1)}, bf16[64,3072]{1,0:T(8,128)(2,1)S(1)}, u32[]{:S(2)}, u32[]{:S(2)}) collective-permute-start(bf16[64,3072]{1,0:T(8,128)(2,1)} %bitcast.18), channel_id=1, source_target_pairs={{0,12},{4,0},{8,4},{12,8},{1,13},{5,1},{9,5},{13,9},{2,14},{6,2},{... | collective-permute-start | bytes 1179656 | tf_op jit(solution)/shard_map/ppermute | solution.py:323
  18.8 18.9 %collective-permute-start.4 = (bf16[576,3072]{1,0:T(8,128)(2,1)}, bf16[576,3072]{1,0:T(8,128)(2,1)S(1)}, u32[]{:S(2)}, u32[]{:S(2)}) collective-permute-start(bf16[576,3072]{1,0:T(8,128)(2,1)} %bitcast.23), channel_id=1, source_target_pairs={{0,1},{1,0},{2,3},{3,2},{4,5},{5,4},{6,7},{7,6},{8,9},{9,8},{10,11... | collective-permute-start | bytes 10616840 | tf_op jit(solution)/shard_map/ppermute | solution.py:323
  24.7 20.8 %collective-permute-start.6 = (bf16[64,3072]{1,0:T(8,128)(2,1)S(1)}, bf16[64,3072]{1,0:T(8,128)(2,1)S(1)}, u32[]{:S(2)}, u32[]{:S(2)}) collective-permute-start(bf16[64,3072]{1,0:T(8,128)(2,1)S(1)} %collective-permute-done.3.refs_4_), channel_id=1, source_target_pairs={{0,8},{4,12},{8,0},{12,4},{1,9},{5,13},{9,1},{13,5},{2,10},{6,14},... | collective-permute-start | bytes 1179656 | tf_op jit(solution)/shard_map/ppermute | solution.py:323
  29.6 16.8 %collective-permute-start.7 = (bf16[64,3072]{1,0:T(8,128)(2,1)S(1)}, bf16[64,3072]{1,0:T(8,128)(2,1)S(1)}, u32[]{:S(2)}, u32[]{:S(2)}) collective-permute-start(bf16[64,3072]{1,0:T(8,128)(2,1)S(1)} %collective-permute-done.3.refs_4_), channel_id=1, source_target_pairs={{0,4},{4,8},{8,12},{12,0},{1,5},{5,9},{9,13},{13,1},{2,6},{6,10},{... | collective-permute-start | bytes 1179656 | tf_op jit(solution)/shard_map/ppermute | solution.py:323
  32.1 14.4 %collective-permute-start.8 = (bf16[64,3072]{1,0:T(8,128)(2,1)S(1)}, bf16[64,3072]{1,0:T(8,128)(2,1)S(1)}, u32[]{:S(2)}, u32[]{:S(2)}) collective-permute-start(bf16[64,3072]{1,0:T(8,128)(2,1)S(1)} %collective-permute-done.3.refs_4_), channel_id=1, source_target_pairs={{0,12},{4,0},{8,4},{12,8},{1,13},{5,1},{9,5},{13,9},{2,14},{6,2},{... | collective-permute-start | bytes 1179656 | tf_op jit(solution)/shard_map/ppermute | solution.py:323
  43.6 8.4 %collective-permute-start.5 = (bf16[320,576]{1,0:T(8,128)(2,1)S(1)}, bf16[320,576]{1,0:T(8,128)(2,1)S(1)}, u32[]{:S(2)}, u32[]{:S(2)}) collective-permute-start(bf16[320,576]{1,0:T(8,128)(2,1)S(1)} %get-tuple-element.15), channel_id=1, source_target_pairs={{0,1},{1,0},{2,3},{3,2},{4,5},{5,4},{6,7},{7,6},{8,9},{9,8},{10,11... | collective-permute-start | bytes 1105928 | tf_op jit(solution)/shard_map/ppermute | solution.py:323
  49.7 15.4 %copy-start.1 = (s32[32]{0:T(128)S(1)}, s32[32]{0:T(128)}, u32[]{:S(2)}) copy-start(s32[32]{0:T(128)} %param.9) | copy-start | bytes 388
  49.7 50.0 %copy-start = (bf16[1,8,8,3072]{3,2,1,0:T(8,128)(2,1)S(1)}, bf16[1,8,8,3072]{3,2,1,0:T(8,128)(2,1)}, u32[]{:S(2)}) copy-start(bf16[1,8,8,3072]{3,2,1,0:T(8,128)(2,1)} %param.5) | copy-start | bytes 1179652
  49.7 4.2 %collective-permute-start.9 = (bf16[192,576]{1,0:T(8,128)(2,1)S(1)}, bf16[192,576]{1,0:T(8,128)(2,1)S(1)}, u32[]{:S(2)}, u32[]{:S(2)}) collective-permute-start(bf16[192,576]{1,0:T(8,128)(2,1)S(1)} %get-tuple-element.18), channel_id=1, source_target_pairs={{0,1},{1,0},{2,3},{3,2},{4,5},{5,4},{6,7},{7,6},{8,9},{9,8},{10,11... | collective-permute-start | bytes 663560 | tf_op jit(solution)/shard_map/ppermute | solution.py:323
  57.7 9.2 %collective-permute-start.10 = (bf16[576,128]{1,0:T(8,128)(2,1)S(1)}, bf16[576,128]{1,0:T(8,128)(2,1)S(1)}, u32[]{:S(2)}, u32[]{:S(2)}) collective-permute-start(bf16[576,128]{1,0:T(8,128)(2,1)S(1)} %get-tuple-element.21), channel_id=1, source_target_pairs={{0,16},{16,32},{32,48},{48,64},{64,80},{80,96},{96,112},{112,128},... | collective-permute-start | bytes 442376 | tf_op jit(solution)/shard_map/ppermute | solution.py:328
  63.2 9.1 %collective-permute-start.11 = (bf16[576,128]{1,0:T(8,128)(2,1)S(1)}, bf16[576,128]{1,0:T(8,128)(2,1)S(1)}, u32[]{:S(2)}, u32[]{:S(2)}) collective-permute-start(bf16[576,128]{1,0:T(8,128)(2,1)S(1)} %get-tuple-element.22), channel_id=1, source_target_pairs={{16,0},{32,16},{48,32},{64,48},{80,64},{96,80},{112,96},{128,112},... | collective-permute-start | bytes 442376 | tf_op jit(solution)/shard_map/ppermute | solution.py:328

commit v8 on v7

--- a/solution.py
+++ b/solution.py
@@ -101,7 +101,8 @@
 def project_kernel(blocks, *refs):
     tokens, (mods, wa, wb, oa, ob, normed) = refs[:blocks], refs[blocks:]
     used = oa.shape[0]
-    normed[used:] = jnp.zeros((normed.shape[0] - used, normed.shape[1]), jnp.bfloat16)
+    if used < normed.shape[0]:
+        normed[used:] = jnp.zeros((normed.shape[0] - used, normed.shape[1]), jnp.bfloat16)
     normalise(tokens, mods, normed, range(blocks), lambda i: None)
     product(normed, wb, ob)
     product(normed, wa, oa)
@@ -345,10 +346,10 @@
     wb = around(wa, "core", 1)
     far = [around(other, "x", by) for by in STEPS]
 
-    own, give, wa = early_project([mine, *near, other], mods, wa, wb)
+    own, give, wa = early_project([mine, *near], mods, wa, wb)
     pair0 = [g.reshape(-1, rows, g.shape[-1]) for g in (own, around(give, "core", 1))]
     state = early(*pair0)
-    own, give = project(far, mods, wa, wb)
+    own, give = project([other, *far], mods, wa, wb)
     pair1 = [g.reshape(-1, rows, g.shape[-1]) for g in (own, around(give, "core", 1))]
 
     pair, third, first3, last3 = attend(pair0 + pair1, state)

time: 101 us -> 101 us (level)
    ppermute x10, waiting for transfers between devices: 4.26 us -> 5.31 us  [around(): return lax.ppermute(value, axis, [(i, (i + by) % n) for i in range(n)])]
  transfers between devices with their start and end apart: 12 -> 12, of which waited for: 5 -> 6; matrix products, arithmetic and copies ran while one was open for 0% -> 0% of each run, Pallas kernels for 12% -> 10%
where the time goes in v8:
time: 101 us
  starting transfers between devices  44.3 us (44%)
  blocking collectives  26.6 us (26%)
  Pallas kernels  16.7 us (17%)
  waiting for transfers between devices  12.2 us (12%)
    ppermute x10, starting transfers between devices, around(): return lax.ppermute(value, axis, [(i, (i + by) % n) for i in range(n)])  36.9 us
    all_to_all x1, blocking collectives, shards(): avg = lax.all_to_all(avg, ('x', 'yhi', 'core'), 0, 0)  26.6 us
    ppermute x2, starting transfers between devices, along(): lax.ppermute(value, ('ylo', 'z'), [(i, i + by) for i in range(n) if 0 <=...  7.41 us
    ppermute x2, waiting for transfers between devices, along(): lax.ppermute(value, ('ylo', 'z'), [(i, i + by) for i in range(n) if 0 <=...  6.85 us
    ppermute x10, waiting for transfers between devices, around(): return lax.ppermute(value, axis, [(i, (i + by) % n) for i in range(n)])  5.31 us
    pallas_call x1, Pallas kernels, early_project(): pl.pallas_call(functools.partial(early_project_kernel, len(blocks)), in_s...  4.89 us
    pallas_call x1, Pallas kernels, attend(): pl.pallas_call(attend_kernel, in_specs=[full] * 5, out_specs=[full] * 4,...  4.35 us
    pallas_call x1, Pallas kernels, project(): pl.pallas_call(functools.partial(project_kernel, len(blocks)), in_specs=[...  3.34 us
  transfers between devices with their start and end apart: 12, of which 6 were waited for; matrix products, arithmetic and copies ran while one was open for 0% of the time, Pallas kernels for 10%

profile of v8, /device:TPU:200, one launch (start us, length us, event | category | flops | bytes accessed | tf_op | source)
XLA Modules:
  0.0 100.8 jit_solution(216872190992433559)
XLA Ops:
  0.0 6.8 %collective-permute-start.5 = (bf16[64,3072]{1,0:T(8,128)(2,1)}, bf16[64,3072]{1,0:T(8,128)(2,1)S(1)}, u32[]{:S(2)}, u32[]{:S(2)}) collective-permute-start(bf16[64,3072]{1,0:T(8,128)(2,1)} %bitcast.11), channel_id=1, source_target_pairs={{0,2},{2,0},{1,3},{3,1},{4,6},{6,4},{5,7},{7,5},{8,10},{10,8},{9,1... | collective-permute-start | bytes 1179656 | tf_op jit(solution)/shard_map/ppermute | solution.py:324
  6.8 4.9 %collective-permute-start = (bf16[64,3072]{1,0:T(8,128)(2,1)}, bf16[64,3072]{1,0:T(8,128)(2,1)S(1)}, u32[]{:S(2)}, u32[]{:S(2)}) collective-permute-start(bf16[64,3072]{1,0:T(8,128)(2,1)} %bitcast.12), channel_id=1, source_target_pairs={{0,8},{4,12},{8,0},{12,4},{1,9},{5,13},{9,1},{13,5},{2,10},{6,14},... | collective-permute-start | bytes 1179656 | tf_op jit(solution)/shard_map/ppermute | solution.py:324
  11.8 2.5 %collective-permute-start.1 = (bf16[64,3072]{1,0:T(8,128)(2,1)}, bf16[64,3072]{1,0:T(8,128)(2,1)S(1)}, u32[]{:S(2)}, u32[]{:S(2)}) collective-permute-start(bf16[64,3072]{1,0:T(8,128)(2,1)} %bitcast.13), channel_id=1, source_target_pairs={{0,4},{4,8},{8,12},{12,0},{1,5},{5,9},{9,13},{13,1},{2,6},{6,10},{... | collective-permute-start | bytes 1179656 | tf_op jit(solution)/shard_map/ppermute | solution.py:324
  14.3 4.6 %collective-permute-start.2 = (bf16[64,3072]{1,0:T(8,128)(2,1)}, bf16[64,3072]{1,0:T(8,128)(2,1)S(1)}, u32[]{:S(2)}, u32[]{:S(2)}) collective-permute-start(bf16[64,3072]{1,0:T(8,128)(2,1)} %bitcast.14), channel_id=1, source_target_pairs={{0,12},{4,0},{8,4},{12,8},{1,13},{5,1},{9,5},{13,9},{2,14},{6,2},{... | collective-permute-start | bytes 1179656 | tf_op jit(solution)/shard_map/ppermute | solution.py:324
  18.8 1.9 %collective-permute-start.3 = (bf16[576,3072]{1,0:T(8,128)(2,1)}, bf16[576,3072]{1,0:T(8,128)(2,1)S(1)}, u32[]{:S(2)}, u32[]{:S(2)}) collective-permute-start(bf16[576,3072]{1,0:T(8,128)(2,1)} %bitcast.23), channel_id=1, source_target_pairs={{0,1},{1,0},{2,3},{3,2},{4,5},{5,4},{6,7},{7,6},{8,9},{9,8},{10,11... | collective-permute-start | bytes 10616840 | tf_op jit(solution)/shard_map/ppermute | solution.py:324
  21.4 3.3 %collective-permute-done.5.refs_0_ = bf16[64,3072]{1,0:T(8,128)(2,1)S(1)} collective-permute-done((bf16[64,3072]{1,0:T(8,128)(2,1)}, bf16[64,3072]{1,0:T(8,128)(2,1)S(1)}, u32[]{:S(2)}, u32[]{:S(2)}) %collective-permute-start.5) | collective-permute-done | bytes 393248 | tf_op jit(solution)/shard_map/ppermute | solution.py:324
  24.7 4.9 %collective-permute-start.6 = (bf16[64,3072]{1,0:T(8,128)(2,1)S(1)}, bf16[64,3072]{1,0:T(8,128)(2,1)S(1)}, u32[]{:S(2)}, u32[]{:S(2)}) collective-permute-start(bf16[64,3072]{1,0:T(8,128)(2,1)S(1)} %collective-permute-done.5.refs_0_), channel_id=1, source_target_pairs={{0,8},{4,12},{8,0},{12,4},{1,9},{5,13},{9,1},{13,5},{2,10},{6,14},... | collective-permute-start | bytes 1179656 | tf_op jit(solution)/shard_map/ppermute | solution.py:324
  29.6 0.0 collective-permute-done.refs_1_
  29.6 2.5 %collective-permute-start.7 = (bf16[64,3072]{1,0:T(8,128)(2,1)S(1)}, bf16[64,3072]{1,0:T(8,128)(2,1)S(1)}, u32[]{:S(2)}, u32[]{:S(2)}) collective-permute-start(bf16[64,3072]{1,0:T(8,128)(2,1)S(1)} %collective-permute-done.5.refs_0_), channel_id=1, source_target_pairs={{0,4},{4,8},{8,12},{12,0},{1,5},{5,9},{9,13},{13,1},{2,6},{6,10},{... | collective-permute-start | bytes 1179656 | tf_op jit(solution)/shard_map/ppermute | solution.py:324
  32.1 0.0 collective-permute-done.1.refs_2_
  32.1 4.6 %collective-permute-start.8 = (bf16[64,3072]{1,0:T(8,128)(2,1)S(1)}, bf16[64,3072]{1,0:T(8,128)(2,1)S(1)}, u32[]{:S(2)}, u32[]{:S(2)}) collective-permute-start(bf16[64,3072]{1,0:T(8,128)(2,1)S(1)} %collective-permute-done.5.refs_0_), channel_id=1, source_target_pairs={{0,12},{4,0},{8,4},{12,8},{1,13},{5,1},{9,5},{13,9},{2,14},{6,2},{... | collective-permute-start | bytes 1179656 | tf_op jit(solution)/shard_map/ppermute | solution.py:324
  36.7 1.0 shard_map.55.refs_4_.mods
  37.7 0.0 collective-permute-done.2.refs_3_
  37.7 0.0 collective-permute-done.3.refs_6_
  37.7 4.9 %shard_map.56 = (bf16[256,576]{1,0:T(8,128)(2,1)S(1)}, bf16[256,576]{1,0:T(8,128)(2,1)S(1)}, bf16[576,3072]{1,0:T(8,128)(2,1)S(1)}) custom-call(bf16[64,3072]{1,0:T(8,128)(2,1)} %bitcast.15, bf16[64,3072]{1,0:T(8,128)(2,1)S(1)} %collective-permute-done.refs_1_, bf16[64,3072]{1,0:T(8,128)(2,1)S(1)} %collective-permute-done.1.refs_2_, ...), custom_call_target="tpu_custom_call" | custom-call | flops 1 | tf_op jit(solution)/shard_map/pallas_call | solution.py:86
  42.6 1.9 %collective-permute-start.4 = (bf16[256,576]{1,0:T(8,128)(2,1)S(1)}, bf16[256,576]{1,0:T(8,128)(2,1)S(1)}, u32[]{:S(2)}, u32[]{:S(2)}) collective-permute-start(bf16[256,576]{1,0:T(8,128)(2,1)S(1)} %get-tuple-element.15), channel_id=1, source_target_pairs={{0,1},{1,0},{2,3},{3,2},{4,5},{5,4},{6,7},{7,6},{8,9},{9,8},{10,11... | collective-permute-start | bytes 884744 | tf_op jit(solution)/shard_map/ppermute | solution.py:324
  44.6 0.0 collective-permute-done.6.refs_1_
  44.6 1.9 %collective-permute-done.7.refs_2_ = bf16[64,3072]{1,0:T(8,128)(2,1)S(1)} collective-permute-done((bf16[64,3072]{1,0:T(8,128)(2,1)S(1)}, bf16[64,3072]{1,0:T(8,128)(2,1)S(1)}, u32[]{:S(2)}, u32[]{:S(2)}) %collective-permute-start.7) | collective-permute-done | bytes 393248 | tf_op jit(solution)/shard_map/ppermute | solution.py:324
  46.4 0.1 collective-permute-done.8.refs_3_
  46.5 3.3 %shard_map.57 = (bf16[256,576]{1,0:T(8,128)(2,1)S(1)}, bf16[256,576]{1,0:T(8,128)(2,1)S(1)}) custom-call(bf16[64,3072]{1,0:T(8,128)(2,1)S(1)} %collective-permute-done.5.refs_0_, bf16[64,3072]{1,0:T(8,128)(2,1)S(1)} %collective-permute-done.6.refs_1_, bf16[64,3072]{1,0:T(8,128)(2,1)S(1)} %collective-permute-done.7.refs_2_, ...), custom_call_target="tpu_custom_call" | custom-call | flops 1 | bytes 7077888 | tf_op jit(solution)/shard_map/pallas_call | solution.py:116
  49.9 0.0 copy-start.1
  49.9 0.0 copy-start
  49.9 2.2 %collective-permute-start.9 = (bf16[256,576]{1,0:T(8,128)(2,1)S(1)}, bf16[256,576]{1,0:T(8,128)(2,1)S(1)}, u32[]{:S(2)}, u32[]{:S(2)}) collective-permute-start(bf16[256,576]{1,0:T(8,128)(2,1)S(1)} %get-tuple-element.18), channel_id=1, source_target_pairs={{0,1},{1,0},{2,3},{3,2},{4,5},{5,4},{6,7},{7,6},{8,9},{9,8},{10,11... | collective-permute-start | bytes 884744 | tf_op jit(solution)/shard_map/ppermute | solution.py:324
  52.1 0.0 collective-permute-done.4
  52.1 1.3 %shard_map.58.state = f32[8,64,384]{2,1,0:T(8,128)S(1)} custom-call(bf16[4,64,576]{2,1,0:T(8,128)(2,1)S(1)} %bitcast.17, bf16[4,64,576]{2,1,0:T(8,128)(2,1)S(1)} %bitcast.19), custom_call_target="tpu_custom_call" | custom-call | flops 1 | tf_op jit(solution)/shard_map/pallas_call | solution.py:167
  53.5 0.1 collective-permute-done.9
  53.6 4.3 %shard_map.59 = (bf16[16,64,128]{2,1,0:T(8,128)(2,1)S(1)}, bf16[16,64,64]{2,1,0:T(8,128)(2,1)S(1)}, bf16[576,128]{1,0:T(8,128)(2,1)S(1)}, bf16[576,128]{1,0:T(8,128)(2,1)S(1)}) custom-call(bf16[4,64,576]{2,1,0:T(8,128)(2,1)S(1)} %bitcast.18, bf16[4,64,576]{2,1,0:T(8,128)(2,1)S(1)} %bitcast.20, bf16[4,64,576]{2,1,0:T(8,128)(2,1)S(1)} %bitcast.21, ...), custom_call_target="tpu_custom_call" | custom-call | tf_op jit(solution)/shard_map/pallas_call | solution.py:230
  57.9 5.5 %collective-permute-start.10 = (bf16[576,128]{1,0:T(8,128)(2,1)S(1)}, bf16[576,128]{1,0:T(8,128)(2,1)S(1)}, u32[]{:S(2)}, u32[]{:S(2)}) collective-permute-start(bf16[576,128]{1,0:T(8,128)(2,1)S(1)} %get-tuple-element.21), channel_id=1, source_target_pairs={{0,16},{16,32},{32,48},{48,64},{64,80},{80,96},{96,112},{112,128},... | collective-permute-start | bytes 442376 | tf_op jit(solution)/shard_map/ppermute | solution.py:329
  63.4 1.9 %collective-permute-start.11 = (bf16[576,128]{1,0:T(8,128)(2,1)S(1)}, bf16[576,128]{1,0:T(8,128)(2,1)S(1)}, u32[]{:S(2)}, u32[]{:S(2)}) collective-permute-start(bf16[576,128]{1,0:T(8,128)(2,1)S(1)} %get-tuple-element.22), channel_id=1, source_target_pairs={{16,0},{32,16},{48,32},{64,48},{80,64},{96,80},{112,96},{128,112},... | collective-permute-start | bytes 442376 | tf_op jit(solution)/shard_map/ppermute | solution.py:329
  65.3 0.0 copy-done.1
  65.3 0.1 pad_add_fusion
  65.4 0.1 dynamic_slice.3.overlap
  65.5 0.1 pad_add_fusion.1.place
  65.6 1.5 %collective-permute-done.10.before = bf16[576,128]{1,0:T(8,128)(2,1)S(1)} collective-permute-done((bf16[576,128]{1,0:T(8,128)(2,1)S(1)}, bf16[576,128]{1,0:T(8,128)(2,1)S(1)}, u32[]{:S(2)}, u32[]{:S(2)}) %collective-permute-start.10) | collective-permute-done | bytes 147488 | tf_op jit(solution)/shard_map/ppermute | solution.py:329
  67.1 5.3 %collective-permute-done.11.after = bf16[576,128]{1,0:T(8,128)(2,1)S(1)} collective-permute-done((bf16[576,128]{1,0:T(8,128)(2,1)S(1)}, bf16[576,128]{1,0:T(8,128)(2,1)S(1)}, u32[]{:S(2)}, u32[]{:S(2)}) %collective-permute-start.11) | collective-permute-done | bytes 147488 | tf_op jit(solution)/shard_map/ppermute | solution.py:329
  72.4 0.8 shard_map.60
  73.2 26.6 %all_to_all.5.avg = bf16[16,96,128]{2,1,0:T(8,128)(2,1)S(1)} all-to-all(bf16[16,96,128]{2,1,0:T(8,128)(2,1)S(1)} %shard_map.60), channel_id=1, replica_groups=mesh['ylo'=4,'z'=8,'x'=4,'yhi'=2,'core'=2] {'x','yhi','core'}, dimensions={0} | all-to-all | bytes 786432 | tf_op jit(solution)/shard_map/all_to_all | solution.py:359
  99.8 0.0 copy-done
  99.8 1.0 shard_map.61
Async XLA Ops:
  0.0 24.7 %collective-permute-start.5 = (bf16[64,3072]{1,0:T(8,128)(2,1)}, bf16[64,3072]{1,0:T(8,128)(2,1)S(1)}, u32[]{:S(2)}, u32[]{:S(2)}) collective-permute-start(bf16[64,3072]{1,0:T(8,128)(2,1)} %bitcast.11), channel_id=1, source_target_pairs={{0,2},{2,0},{1,3},{3,1},{4,6},{6,4},{5,7},{7,5},{8,10},{10,8},{9,1... | collective-permute-start | bytes 1179656 | tf_op jit(solution)/shard_map/ppermute | solution.py:324
  6.8 22.8 %collective-permute-start = (bf16[64,3072]{1,0:T(8,128)(2,1)}, bf16[64,3072]{1,0:T(8,128)(2,1)S(1)}, u32[]{:S(2)}, u32[]{:S(2)}) collective-permute-start(bf16[64,3072]{1,0:T(8,128)(2,1)} %bitcast.12), channel_id=1, source_target_pairs={{0,8},{4,12},{8,0},{12,4},{1,9},{5,13},{9,1},{13,5},{2,10},{6,14},... | collective-permute-start | bytes 1179656 | tf_op jit(solution)/shard_map/ppermute | solution.py:324
  11.8 20.4 %collective-permute-start.1 = (bf16[64,3072]{1,0:T(8,128)(2,1)}, bf16[64,3072]{1,0:T(8,128)(2,1)S(1)}, u32[]{:S(2)}, u32[]{:S(2)}) collective-permute-start(bf16[64,3072]{1,0:T(8,128)(2,1)} %bitcast.13), channel_id=1, source_target_pairs={{0,4},{4,8},{8,12},{12,0},{1,5},{5,9},{9,13},{13,1},{2,6},{6,10},{... | collective-permute-start | bytes 1179656 | tf_op jit(solution)/shard_map/ppermute | solution.py:324
  14.3 23.4 %collective-permute-start.2 = (bf16[64,3072]{1,0:T(8,128)(2,1)}, bf16[64,3072]{1,0:T(8,128)(2,1)S(1)}, u32[]{:S(2)}, u32[]{:S(2)}) collective-permute-start(bf16[64,3072]{1,0:T(8,128)(2,1)} %bitcast.14), channel_id=1, source_target_pairs={{0,12},{4,0},{8,4},{12,8},{1,13},{5,1},{9,5},{13,9},{2,14},{6,2},{... | collective-permute-start | bytes 1179656 | tf_op jit(solution)/shard_map/ppermute | solution.py:324
  18.8 18.9 %collective-permute-start.3 = (bf16[576,3072]{1,0:T(8,128)(2,1)}, bf16[576,3072]{1,0:T(8,128)(2,1)S(1)}, u32[]{:S(2)}, u32[]{:S(2)}) collective-permute-start(bf16[576,3072]{1,0:T(8,128)(2,1)} %bitcast.23), channel_id=1, source_target_pairs={{0,1},{1,0},{2,3},{3,2},{4,5},{5,4},{6,7},{7,6},{8,9},{9,8},{10,11... | collective-permute-start | bytes 10616840 | tf_op jit(solution)/shard_map/ppermute | solution.py:324
  24.7 19.9 %collective-permute-start.6 = (bf16[64,3072]{1,0:T(8,128)(2,1)S(1)}, bf16[64,3072]{1,0:T(8,128)(2,1)S(1)}, u32[]{:S(2)}, u32[]{:S(2)}) collective-permute-start(bf16[64,3072]{1,0:T(8,128)(2,1)S(1)} %collective-permute-done.5.refs_0_), channel_id=1, source_target_pairs={{0,8},{4,12},{8,0},{12,4},{1,9},{5,13},{9,1},{13,5},{2,10},{6,14},... | collective-permute-start | bytes 1179656 | tf_op jit(solution)/shard_map/ppermute | solution.py:324
  29.6 16.8 %collective-permute-start.7 = (bf16[64,3072]{1,0:T(8,128)(2,1)S(1)}, bf16[64,3072]{1,0:T(8,128)(2,1)S(1)}, u32[]{:S(2)}, u32[]{:S(2)}) collective-permute-start(bf16[64,3072]{1,0:T(8,128)(2,1)S(1)} %collective-permute-done.5.refs_0_), channel_id=1, source_target_pairs={{0,4},{4,8},{8,12},{12,0},{1,5},{5,9},{9,13},{13,1},{2,6},{6,10},{... | collective-permute-start | bytes 1179656 | tf_op jit(solution)/shard_map/ppermute | solution.py:324
  32.1 14.4 %collective-permute-start.8 = (bf16[64,3072]{1,0:T(8,128)(2,1)S(1)}, bf16[64,3072]{1,0:T(8,128)(2,1)S(1)}, u32[]{:S(2)}, u32[]{:S(2)}) collective-permute-start(bf16[64,3072]{1,0:T(8,128)(2,1)S(1)} %collective-permute-done.5.refs_0_), channel_id=1, source_target_pairs={{0,12},{4,0},{8,4},{12,8},{1,13},{5,1},{9,5},{13,9},{2,14},{6,2},{... | collective-permute-start | bytes 1179656 | tf_op jit(solution)/shard_map/ppermute | solution.py:324
  42.6 9.5 %collective-permute-start.4 = (bf16[256,576]{1,0:T(8,128)(2,1)S(1)}, bf16[256,576]{1,0:T(8,128)(2,1)S(1)}, u32[]{:S(2)}, u32[]{:S(2)}) collective-permute-start(bf16[256,576]{1,0:T(8,128)(2,1)S(1)} %get-tuple-element.15), channel_id=1, source_target_pairs={{0,1},{1,0},{2,3},{3,2},{4,5},{5,4},{6,7},{7,6},{8,9},{9,8},{10,11... | collective-permute-start | bytes 884744 | tf_op jit(solution)/shard_map/ppermute | solution.py:324
  49.9 15.5 %copy-start.1 = (s32[32]{0:T(128)S(1)}, s32[32]{0:T(128)}, u32[]{:S(2)}) copy-start(s32[32]{0:T(128)} %param.9) | copy-start | bytes 388
  49.9 50.0 %copy-start = (bf16[1,8,8,3072]{3,2,1,0:T(8,128)(2,1)S(1)}, bf16[1,8,8,3072]{3,2,1,0:T(8,128)(2,1)}, u32[]{:S(2)}) copy-start(bf16[1,8,8,3072]{3,2,1,0:T(8,128)(2,1)} %param.5) | copy-start | bytes 1179652
  49.9 3.7 %collective-permute-start.9 = (bf16[256,576]{1,0:T(8,128)(2,1)S(1)}, bf16[256,576]{1,0:T(8,128)(2,1)S(1)}, u32[]{:S(2)}, u32[]{:S(2)}) collective-permute-start(bf16[256,576]{1,0:T(8,128)(2,1)S(1)} %get-tuple-element.18), channel_id=1, source_target_pairs={{0,1},{1,0},{2,3},{3,2},{4,5},{5,4},{6,7},{7,6},{8,9},{9,8},{10,11... | collective-permute-start | bytes 884744 | tf_op jit(solution)/shard_map/ppermute | solution.py:324
  57.9 9.2 %collective-permute-start.10 = (bf16[576,128]{1,0:T(8,128)(2,1)S(1)}, bf16[576,128]{1,0:T(8,128)(2,1)S(1)}, u32[]{:S(2)}, u32[]{:S(2)}) collective-permute-start(bf16[576,128]{1,0:T(8,128)(2,1)S(1)} %get-tuple-element.21), channel_id=1, source_target_pairs={{0,16},{16,32},{32,48},{48,64},{64,80},{80,96},{96,112},{112,128},... | collective-permute-start | bytes 442376 | tf_op jit(solution)/shard_map/ppermute | solution.py:329
  63.4 9.0 %collective-permute-start.11 = (bf16[576,128]{1,0:T(8,128)(2,1)S(1)}, bf16[576,128]{1,0:T(8,128)(2,1)S(1)}, u32[]{:S(2)}, u32[]{:S(2)}) collective-permute-start(bf16[576,128]{1,0:T(8,128)(2,1)S(1)} %get-tuple-element.22), channel_id=1, source_target_pairs={{16,0},{32,16},{48,32},{64,48},{80,64},{96,80},{112,96},{128,112},... | collective-permute-start | bytes 442376 | tf_op jit(solution)/shard_map/ppermute | solution.py:329
